TPU v7x, 512 devices: a whole 4x4x16 slice. The times are simulated.
512 devices in a mesh: chol: 16 (over x, z_hi), pair: 32 (over z_lo, y, core).
Axes of the slice: x: 4, y: 4, z: 16 (z_hi: 4, z_lo: 4; z = z_hi * 4 + z_lo), core: 2. Of those that a mesh axis runs over, the one named last changes fastest.
Arguments:
- chol_vectors: bfloat16 [16, 4096, 1024], P(None, ('chol', 'pair')), may hold values from -0.75 to 0.75
- amplitudes: bfloat16 [1024, 64, 1024], P('chol', 'pair'), may hold values from -6 to 6
- fock: bfloat16 [1024, 1024], replicated
- orbital_energy: float32 [16], replicated, may hold values from -1.5 to -0.3
- pair_orbitals: int32 [32, 2], replicated, may hold values from 0 to 15, as said below
- pair_case: int32 [32], replicated, may hold values from 0 to 1
- owner_offsets: int32 [33], replicated, may hold values from 0 to 32, as said below
Outputs:
- residual: float32 [1024, 64, 1024], P('chol', 'pair')
Inputs may be any that keep to these rules, and one draw needn't show every extreme that they name: `pair_orbitals`: each row holds two different orbitals, the smaller first. `owner_offsets`: starts at 0, never falls, ends at 32; each owner holds 0 to 2 pairs and some owner holds exactly 2 in every draw.
All inputs are finite; a program needn't handle non-finite values.
Results may differ from a plain program's by a relative error of at most 0.005.
Values may be sent and summed in bfloat16 or wider, within the bound.
No kernel may reach another device: no remote copies, remote signals or barrier semaphores. Data moves between devices by JAX's collectives and lax.ppermute only.
A program may use at most 64 MiB of HBM per device.

v0:
```python
import jax
import jax.numpy as jnp
from jax import lax
from jax.sharding import PartitionSpec as P


def body(chol_vectors, amplitudes, fock, orbital_energy, pair_orbitals, pair_case, owner_offsets):
    owner_index = lax.axis_index("pair")
    actives, per_device, virtuals = chol_vectors.shape
    row_count, capacity, _ = amplitudes.shape
    first_pair = owner_offsets[:-1]
    owned = owner_offsets[1:] - first_pair
    slot_range = jnp.arange(capacity, dtype=jnp.int32)
    live_all = slot_range[None, :] < owned[:, None]
    pair_all = jnp.where(live_all, first_pair[:, None] + slot_range[None, :], 0)
    orbit_all = pair_orbitals[pair_all]
    live_mine = live_all[owner_index]
    pair_mine = pair_all[owner_index]
    orbit_mine = orbit_all[owner_index]
    gathered = lax.all_gather(chol_vectors, "pair", axis=1, tiled=True)
    needed = gathered[orbit_mine.reshape(-1)]
    coupling = jnp.where(pair_case[pair_mine] == 0, 1.0, -1.0).astype(jnp.float32)
    contract = (((0,), (0,)), ((), ()))
    row_start = lax.axis_index("chol") * row_count
    fock_band = lax.dynamic_slice_in_dim(fock, row_start, row_count, 1)
    amp_flat = amplitudes.reshape(row_count, capacity * virtuals)
    pieces = []
    for slot in range(capacity):
        left_vec = needed[2 * slot]
        right_vec = needed[2 * slot + 1]
        direct = lax.dot_general(left_vec, right_vec, contract, preferred_element_type=jnp.float32)
        swapped = lax.dot_general(right_vec, left_vec, contract, preferred_element_type=jnp.float32)
        pieces.append(0.5 * (direct + coupling[slot] * swapped))
    left_part = jnp.dot(fock_band, amp_flat, preferred_element_type=jnp.float32)
    coupled = lax.psum_scatter(
        (jnp.concatenate(pieces, axis=1) + left_part).astype(jnp.bfloat16),
        "chol",
        scatter_dimension=0,
        tiled=True,
    ).astype(jnp.float32)
    coupled = coupled.reshape(row_count, capacity, virtuals)
    right_term = jnp.dot(
        amplitudes.reshape(row_count * capacity, virtuals), fock, preferred_element_type=jnp.float32
    )
    right_term = right_term.reshape(row_count, capacity, virtuals)
    shift = orbital_energy[orbit_mine[:, 0]] + orbital_energy[orbit_mine[:, 1]]
    result = coupled + right_term - shift[None, :, None] * amplitudes.astype(jnp.float32)
    return jnp.where(live_mine[None, :, None], result, 0.0)


def solution(mesh):
    in_specs = (P(None, ("chol", "pair"), None), P("chol", "pair", None), P(), P(), P(), P(), P())
    out_specs = P("chol", "pair", None)
    return jax.shard_map(body, mesh=mesh, in_specs=in_specs, out_specs=out_specs, check_vma=False)
```

profile of v0, /device:TPU:1, one launch (start us, length us, event | category | flops | bytes accessed | tf_op | source)
XLA Modules:
  0.0 276.1 jit_solution(4443227299332587162)
XLA Ops:
  6.5 0.0 copy-start
  6.5 0.7 all-gather.2.cloned.1.call-update
  7.3 0.0 reduce-scatter.4.cloned.1.call-start
  7.3 0.8 slice_subtract_fusion
  8.1 0.6 dynamic-slice
  8.7 0.1 compare_select_fusion
  8.8 0.1 reshape.155
  8.9 0.8 copy.52
  9.7 0.6 gather_fusion
  10.3 0.1 reshape_squeeze.3
  10.3 0.1 copy.70
  10.4 1.0 copy.72
  11.4 0.1 iota_compare_fusion.1
  11.5 0.7 fusion.20
  12.2 1.3 gather_fusion.2
  13.5 0.6 fusion.24
  14.1 75.6 %all-gather.2.cloned.1.call-done = bf16[16,256,1024]{2,1,0:T(8,128)(2,1)} async-done(((bf16[16,8,1024]{2,1,0:T(8,128)(2,1)}), bf16[16,256,1024]{2,1,0:T(8,128)(2,1)}) %all-gather.2.cloned.1.call-update) | async-done | bytes 8388624 | tf_op jit(solution)/shard_map/all_gather | solution.py:20
  89.8 5.4 %gather_fusion.1 = bf16[4,256,1024]{2,1,0:T(8,128)(2,1)} fusion(bf16[16,256,1024]{2,1,0:T(8,128)(2,1)} %all-gather.2.cloned.1.call-done, s32[1024]{0:T(1024)S(1)} %pad_clamp_fusion.3), kind=kCustom, calls=%fused_computation.1 | custom fusion | bytes 4194320 | tf_op jit(solution)/shard_map/gather | solution.py:21
  95.2 2.1 fusion.13
  97.3 0.8 fusion.12
  98.0 1.4 add_multiply_fusion
  99.4 1.4 add_multiply_fusion.1
  100.9 3.1 %fusion = bf16[1024,2048]{0,1:T(8,128)(2,1)} fusion(f32[1024,1024]{0,1:T(8,128)S(1)} %add_multiply_fusion, f32[1024,1024]{0,1:T(8,128)S(1)} %add_multiply_fusion.1, bf16[64,2048]{1,0:T(8,128)(2,1)S(1)} %bitcast.58, bf16[1024,1024]{1,0:T(8,128)(2,1)S(1)} %copy-done, s32[]{:T(128)S(6)} %select_n.74), kind=kOutput, calls=%fused_computation.6 | convolution fusion | flops 274726912 | bytes 13107204 | tf_op jit(solution)/shard_map/dot_general | solution.py:34
  104.0 6.5 %copy.68 = bf16[1024,2048]{1,0:T(8,128)(2,1)} copy(bf16[1024,2048]{0,1:T(8,128)(2,1)} %fusion) | data formatting | bytes 8388608
  110.5 0.0 reduce-scatter.4.cloned.1.call-update
  110.5 0.6 copy-done.1
  111.1 0.6 gather_fusion.4
  111.8 0.6 gather_fusion.3
  112.4 154.1 %reduce-scatter.4.cloned.1.call-done = bf16[64,2048]{1,0:T(8,128)(2,1)} async-done(((bf16[1024,2048]{1,0:T(8,128)(2,1)}), bf16[64,2048]{1,0:T(8,128)(2,1)}) %reduce-scatter.4.cloned.1.call-update) | async-done | bytes 262160 | tf_op jit(solution)/shard_map/reduce_scatter | solution.py:35
  266.6 1.0 reshape.151
  267.6 0.5 fusion.9
  268.1 1.2 copy.63
  (17 shorter events, 0.1 us)
Async XLA Ops:
  6.5 94.3 %copy-start = (bf16[1024,1024]{1,0:T(8,128)(2,1)S(1)}, bf16[1024,1024]{1,0:T(8,128)(2,1)}, u32[]{:S(2)}) copy-start(bf16[1024,1024]{1,0:T(8,128)(2,1)} %param.9) | copy-start | bytes 6291460
  6.5 83.2 %all-gather.2.cloned.1.call-start = ((), (), s32[]{:S(2)}) async-start(), calls=%async_computation.1 | async-start | bytes 8650752 | tf_op jit(solution)/shard_map/all_gather | solution.py:20
  7.3 259.3 %reduce-scatter.4.cloned.1.call-start = ((), (), s32[]{:S(2)}) async-start(), calls=%async_computation.2 | async-start | bytes 4456448 | tf_op jit(solution)/shard_map/reduce_scatter | solution.py:35
  95.2 2.1 copy-start.2
  110.5 0.7 copy-start.1
  110.5 157.1 %copy-start.3 = (bf16[64,2,1024]{2,1,0:T(2,128)(2,1)S(1)}, bf16[64,2,1024]{2,1,0:T(2,128)(2,1)}, u32[]{:S(2)}) copy-start(bf16[64,2,1024]{2,1,0:T(2,128)(2,1)} %param.8) | copy-start | bytes 786436
Sparse Core Ops, SparseCore 0:
  9.5 80.1 all-gather.1
  110.6 155.8 reduce-scatter.3
where the time goes:
time: 276 us
  waiting for transfers between devices  230 us (83%)
  local copies, waits for them, and re-layouts  20.2 us (7%)
  between operations  13.5 us (5%)
  matrix products  9.23 us (3%)
    reduce_scatter x1, waiting for transfers between devices, body(): lax.psum_scatter((jnp.concatenate(pieces, axis=1) + left_part).astype(jnp...  154 us
    all_gather x1, waiting for transfers between devices, body(): gathered = lax.all_gather(chol_vectors, 'pair', axis=1, tiled=True)  75.6 us
    unnamed x12, local copies, waits for them, and re-layouts  9.02 us
  transfers between devices with their start and end apart: 2, of which 2 were waited for; matrix products, arithmetic and copies ran while one was open for 3% of the time, Pallas kernels for 0%

commit v1 on v0

v1 whole, which is shorter than its diff:
```python
import jax
import jax.numpy as jnp
from jax import lax
from jax.experimental import pallas as pl
from jax.experimental.pallas import tpu as pltpu
from jax.sharding import Mesh, PartitionSpec as P

CHOL = ("x", "zh")
PAIR = ("zl", "y", "core")
VMEM = pl.BlockSpec(memory_space=pltpu.VMEM)
SMEM = pl.BlockSpec(memory_space=pltpu.SMEM)
LIMIT = pltpu.CompilerParams(vmem_limit_bytes=32 * 1024 * 1024)


def pair_at(zl, y, core):
    return y * 8 + zl * 2 + core


def select_kernel(orbitals, vectors, out):
    for dest in range(32):
        pair = pair_at(dest // 8, dest // 2 % 4, dest % 2)
        out[dest, 0] = vectors[orbitals[0, pair]]
        out[dest, 1] = vectors[orbitals[1, pair]]


def couple_kernel(case, vectors, out):
    pair = pair_at(lax.axis_index("zl"), lax.axis_index("y"), lax.axis_index("core"))
    swap = jnp.where(case[pair] == 0, 0.5, -0.5).astype(jnp.float32)
    left = vectors[:, 0].astype(jnp.float32)
    right = vectors[:, 1].astype(jnp.float32)
    rows = jnp.stack([left, right], axis=1).reshape(512, 1024)
    cols = jnp.stack([0.5 * right, swap * left], axis=1).reshape(512, 1024).astype(jnp.bfloat16)
    for i in range(4):
        block = rows[:, i * 256 : (i + 1) * 256].T.astype(jnp.bfloat16)
        for j in range(4):
            product = jnp.dot(block, cols[:, j * 256 : (j + 1) * 256], preferred_element_type=jnp.float32)
            out[i * 4 + j] = product.astype(jnp.bfloat16)


def route_kernel(offsets, parts, out, total):
    total[...] = jnp.sum(parts[...].astype(jnp.float32), axis=0).astype(jnp.bfloat16)
    member = lax.axis_index("zl") * 2 + lax.axis_index("core")
    for chip in range(16):
        end = offsets[chip * 2 + 2]
        which = jnp.maximum(((end + 7 - member) >> 3) - 1, 0)
        out[chip] = total[which]


def body(chol_vectors, amplitudes, fock, orbital_energy, pair_orbitals, pair_case, owner_offsets):
    zl, y, core = (lax.axis_index(name) for name in PAIR)
    owner = zl * 8 + y * 2 + core
    band = lax.axis_index("x") * 4 + lax.axis_index("zh")
    flat = amplitudes.reshape(64, 2048)
    all_amps = lax.all_gather(flat, CHOL, axis=0, tiled=True)

    chosen = pl.pallas_call(
        select_kernel,
        out_shape=jax.ShapeDtypeStruct((32, 2, 8, 1024), jnp.bfloat16),
        in_specs=[SMEM, VMEM],
        out_specs=VMEM,
        compiler_params=LIMIT,
    )(pair_orbitals.T, chol_vectors)
    vectors = lax.all_to_all(chosen, PAIR, 0, 0, tiled=True)
    partial = pl.pallas_call(
        couple_kernel,
        out_shape=jax.ShapeDtypeStruct((16, 256, 256), jnp.bfloat16),
        in_specs=[SMEM, VMEM],
        out_specs=VMEM,
        compiler_params=LIMIT,
    )(pair_case, vectors)
    parts = lax.all_to_all(partial, ("x", "y"), 0, 0, tiled=True)
    parts = jnp.sum(parts.reshape(4, 4, 4, 64, 256).astype(jnp.float32), axis=0).astype(jnp.bfloat16)
    parts = lax.all_to_all(jnp.swapaxes(parts, 0, 1), "zh", 0, 0, tiled=True)
    routed = pl.pallas_call(
        route_kernel,
        out_shape=jax.ShapeDtypeStruct((16, 64, 256), jnp.bfloat16),
        in_specs=[SMEM, VMEM],
        out_specs=VMEM,
        scratch_shapes=[pltpu.VMEM((4, 64, 256), jnp.bfloat16)],
        compiler_params=LIMIT,
    )(owner_offsets, parts)
    arrived = lax.all_to_all(routed, ("zl", "y"), 0, 0, tiled=True).reshape(4, 4, 64, 256)

    def held(first):
        pair = first + ((first ^ core) & 1)
        return lax.dynamic_index_in_dim(arrived, (pair & 7) >> 1, 0, keepdims=False)

    first = owner_offsets[owner]
    count = owner_offsets[owner + 1] - first
    other = lax.ppermute(held(owner_offsets[owner ^ 1]), "core", [(0, 1), (1, 0)])
    mine = held(first)
    own_first = (first & 1) == core
    slots = [jnp.where(own_first, mine, other), jnp.where(own_first, other, mine)]

    rows = lax.dynamic_slice_in_dim(fock, band * 64, 64, 0)
    left = jnp.dot(rows, all_amps, preferred_element_type=jnp.float32)
    pieces = []
    for slot in range(2):
        pair = jnp.minimum(first + slot, 31)
        shift = orbital_energy[pair_orbitals[pair, 0]] + orbital_energy[pair_orbitals[pair, 1]]
        amp = flat[:, slot * 1024 : (slot + 1) * 1024]
        term = jnp.dot(amp, fock, preferred_element_type=jnp.float32)
        coupled = jnp.swapaxes(slots[slot], 0, 1).reshape(64, 1024).astype(jnp.float32)
        result = coupled + left[:, slot * 1024 : (slot + 1) * 1024] + term - shift * amp.astype(jnp.float32)
        pieces.append(jnp.where(slot < count, result, 0.0))
    return jnp.stack(pieces, axis=1)


def solution(mesh):
    fine = Mesh(mesh.devices.reshape(4, 4, 4, 4, 2), ("x", "zh", "zl", "y", "core"))
    in_specs = (P(None, CHOL + PAIR, None), P(CHOL, PAIR, None), P(), P(), P(), P(), P())
    return jax.shard_map(body, mesh=fine, in_specs=in_specs, out_specs=P(CHOL, PAIR, None), check_vma=False)
```

time: 276 us -> 219 us (0.79)
  waiting for transfers between devices: 230 us -> 25.9 us
  blocking collectives: 0 us -> 126 us
  starting transfers between devices: 0.04 us -> 18.8 us
  between operations: 13.5 us -> 29.9 us
  local copies, waits for them, and re-layouts: 20.2 us -> 6.85 us
  matrix products: 9.23 us -> 4.03 us
  Pallas kernels: 0 us -> 3.94 us
    reduce_scatter x1 -> x0, waiting for transfers between devices: 154 us -> none  [body(): lax.psum_scatter((jnp.concatenate(pieces, axis=1) + left_part).astype(jnp...]
    all_to_all x0 -> x2, blocking collectives: none -> 126 us  [the longest x1 92.5 us: body(): parts = lax.all_to_all(jnp.swapaxes(parts, 0, 1), 'zh', 0, 0, tiled=True)]
    all_gather x1, waiting for transfers between devices: 75.6 us -> 0.02 us  [body(): all_amps = lax.all_gather(flat, CHOL, axis=0, tiled=True)]
    all_to_all x0 -> x2, waiting for transfers between devices: none -> 25.9 us  [the longest x1 25.9 us: body(): vectors = lax.all_to_all(chosen, PAIR, 0, 0, tiled=True)]
    all_to_all x0 -> x2, starting transfers between devices: none -> 14 us  [the longest x1 10.5 us: body(): vectors = lax.all_to_all(chosen, PAIR, 0, 0, tiled=True)]
    gather x5 -> x0, local copies, waits for them, and re-layouts: 8.58 us -> none  [the longest x1 5.42 us: body(): needed = gathered[orbit_mine.reshape(-1)]]
    unnamed x12 -> x21, local copies, waits for them, and re-layouts: 9.02 us -> 3.53 us
    dot_general x6 -> x3, matrix products: 9.23 us -> 4.03 us  [the longest x1 3.03 us: body(): left = jnp.dot(rows, all_amps, preferred_element_type=jnp.float32)]
  transfers between devices with their start and end apart: 2 -> 4, of which waited for: 2 -> 1; matrix products, arithmetic and copies ran while one was open for 3% -> 4% of each run, Pallas kernels for 0% -> 2%
where the time goes in v1:
time: 219 us; the launch traced here: 218 us
  blocking collectives  126 us (58%)
  between operations  29.9 us (14%)
  waiting for transfers between devices  25.9 us (12%)
  starting transfers between devices  18.8 us (9%)
  local copies, waits for them, and re-layouts  6.85 us (3%)
  matrix products  4.03 us (2%)
  Pallas kernels  3.94 us (2%)
    all_to_all x1, blocking collectives, body(): parts = lax.all_to_all(jnp.swapaxes(parts, 0, 1), 'zh', 0, 0, tiled=True)  92.5 us
    all_to_all x1, blocking collectives, body(): parts = lax.all_to_all(partial, ('x', 'y'), 0, 0, tiled=True)  33.8 us
    all_to_all x1, waiting for transfers between devices, body(): vectors = lax.all_to_all(chosen, PAIR, 0, 0, tiled=True)  25.9 us
    all_to_all x1, starting transfers between devices, body(): vectors = lax.all_to_all(chosen, PAIR, 0, 0, tiled=True)  10.5 us
    ppermute x1, starting transfers between devices, body(): lax.ppermute(held(owner_offsets[owner ^ 1]), 'core', [(0, 1), (1, 0)])  4.72 us
  transfers between devices with their start and end apart: 4, of which 1 were waited for; matrix products, arithmetic and copies ran while one was open for 4% of the time, Pallas kernels for 2%

profile of v1, /device:TPU:1, one launch (start us, length us, event | category | flops | bytes accessed | tf_op | source)
XLA Modules:
  0.0 217.8 jit_solution(1206207892128480330)
XLA Ops:
  6.5 0.0 copy-start
  6.5 1.1 copy-done.2
  7.6 0.7 copy-done.3
  8.3 0.6 shard_map.73
  8.9 0.0 copy-start.1
  9.0 1.0 copy-done.1
  9.9 10.5 %all-to-all-start = ((bf16[32,2,8,1024]{3,2,1,0:T(8,128)(2,1)}), bf16[32,2,8,1024]{3,2,1,0:T(8,128)(2,1)S(1)}, u32[]{:S(2)}, u32[]{:S(2)}) async-start(bf16[32,2,8,1024]{3,2,1,0:T(8,128)(2,1)} %copy-done.1), calls=%async_computation | async-start | bytes 2097152 | tf_op jit(solution)/shard_map/all_to_all | solution.py:63
  20.4 0.0 all-gather.2.cloned.1.call-start
  20.4 0.0 copy-done.8
  20.4 0.8 copy.18
  21.2 0.0 all-gather.2.cloned.1.call-update
  21.2 25.9 %all-to-all-done.vectors = bf16[32,2,8,1024]{3,2,1,0:T(8,128)(2,1)S(1)} async-done(((bf16[32,2,8,1024]{3,2,1,0:T(8,128)(2,1)}), bf16[32,2,8,1024]{3,2,1,0:T(8,128)(2,1)S(1)}, u32[]{:S(2)}, u32[]{:S(2)}) %all-to-all-start) | async-done | bytes 1048608 | tf_op jit(solution)/shard_map/all_to_all | solution.py:63
  47.1 1.9 shard_map.74
  48.9 33.8 %all_to_all.20 = bf16[16,256,256]{2,1,0:T(8,128)(2,1)} all-to-all(bf16[16,256,256]{2,1,0:T(8,128)(2,1)S(1)} %shard_map.74), channel_id=1, replica_groups=mesh['x'=4,'zh'=4,'zl'=4,'y'=4,'core'=2] {'x','y'}, dimensions={0} | all-to-all | bytes 4194304 | tf_op jit(solution)/shard_map/all_to_all | solution.py:71
  82.7 2.0 reduce_sum.12
  84.8 0.0 copy-start.4
  84.8 0.0 copy-start.9
  84.8 92.5 %all_to_all.21.parts = bf16[4,4,64,256]{3,2,1,0:T(8,128)(2,1)S(1)} all-to-all(bf16[4,4,64,256]{3,2,1,0:T(8,128)(2,1)S(1)} %bitcast.46), channel_id=1, replica_groups=mesh['x'=4,'zh'=4,'zl'=4,'y'=4,'core'=2] {'zh'}, dimensions={0} | all-to-all | bytes 1048576 | tf_op jit(solution)/shard_map/all_to_all | solution.py:73
  177.3 1.5 shard_map.75
  178.8 3.6 %all-to-all-start.3 = ((bf16[16,64,256]{2,1,0:T(8,128)(2,1)}), bf16[16,64,256]{2,1,0:T(8,128)(2,1)S(1)}, u32[]{:S(2)}, u32[]{:S(2)}) async-start(bf16[16,64,256]{2,1,0:T(8,128)(2,1)} %shard_map.75), calls=%async_computation.3 | async-start | bytes 1048576 | tf_op jit(solution)/shard_map/all_to_all | solution.py:82
  182.4 0.7 fusion.12
  188.9 0.0 copy-done.4
  188.9 0.7 constant_dynamic-slice_fusion.3
  197.5 0.7 fusion.11
  200.7 0.0 all-to-all-done.3
  200.8 4.7 %collective-permute-start = (bf16[4,64,256]{2,1,0:T(8,128)(2,1)S(1)}, bf16[4,64,256]{2,1,0:T(8,128)(2,1)S(1)}, u32[]{:S(2)}, u32[]{:S(2)}) collective-permute-start(bf16[4,64,256]{2,1,0:T(8,128)(2,1)S(1)} %dynamic-slice_bitcast_fusion), channel_id=1, source_target_pairs={{0,1},{1,0},{2,3},{3,2},{4,5},{5,4},{6,7},{7,6},{8,9},{9,8},{10,11... | collective-permute-start | bytes 393224 | tf_op jit(solution)/shard_map/ppermute | solution.py:90
  205.5 0.0 all-gather.2.cloned.1.call-done
  205.5 3.0 %fusion.8 = f32[64,2048]{1,0:T(8,128)S(1)} fusion(bf16[1024,2048]{1,0:T(8,128)(2,1)} %all-gather.2.cloned.1.call-done, bf16[1024,1024]{1,0:T(8,128)(2,1)S(1)} %copy-done, s32[]{:T(128)S(6)} %select_n.73), kind=kOutput, calls=%fused_computation.18 | convolution fusion | flops 268435456 | bytes 4849668 | tf_op jit(solution)/shard_map/dot_general | solution.py:96
  208.6 0.0 collective-permute-done
  208.7 0.5 fusion.5
  209.2 0.5 fusion.2
  209.8 1.2 copy.15
  (17 shorter events, 0.2 us)
Async XLA Ops:
  6.5 199.0 %copy-start = (bf16[1024,1024]{1,0:T(8,128)(2,1)S(1)}, bf16[1024,1024]{1,0:T(8,128)(2,1)}, u32[]{:S(2)}) copy-start(bf16[1024,1024]{1,0:T(8,128)(2,1)} %param.9) | copy-start | bytes 6291460
  6.5 1.1 copy-start.2
  7.6 0.7 copy-start.3
  8.3 12.1 %copy-start.8 = (bf16[64,2,1024]{2,1,0:T(2,128)(2,1)S(1)}, bf16[64,2,1024]{2,1,0:T(2,128)(2,1)}, u32[]{:S(2)}) copy-start(bf16[64,2,1024]{2,1,0:T(2,128)(2,1)} %param.8) | copy-start | bytes 786436
  8.3 38.8 %copy-start.6 = (s32[32]{0:T(128)S(1)}, s32[32]{0:T(128)}, u32[]{:S(2)}) copy-start(s32[32]{0:T(128)} %case.1) | copy-start | bytes 388
  8.9 1.0 copy-start.1
  9.9 37.2 %all-to-all-start = ((bf16[32,2,8,1024]{3,2,1,0:T(8,128)(2,1)}), bf16[32,2,8,1024]{3,2,1,0:T(8,128)(2,1)S(1)}, u32[]{:S(2)}, u32[]{:S(2)}) async-start(bf16[32,2,8,1024]{3,2,1,0:T(8,128)(2,1)} %copy-done.1), calls=%async_computation | async-start | bytes 2097152 | tf_op jit(solution)/shard_map/all_to_all | solution.py:63
  20.4 185.1 %all-gather.2.cloned.1.call-start = ((), (), s32[]{:S(2)}) async-start(), calls=%async_computation.4 | async-start | bytes 4456448 | tf_op jit(solution)/shard_map/all_gather | solution.py:54
  82.7 94.6 %copy-start.5 = (s32[33]{0:T(128)S(1)}, s32[33]{0:T(128)}, u32[]{:S(2)}) copy-start(s32[33]{0:T(128)} %offsets.1) | copy-start | bytes 400
  84.8 104.1 %copy-start.4 = (s32[32,2]{0,1:T(2,128)S(1)}, s32[32,2]{0,1:T(2,128)}, u32[]{:S(2)}) copy-start(s32[32,2]{0,1:T(2,128)} %param.11) | copy-start | bytes 772
  84.8 112.7 %copy-start.9 = (f32[16]{0:T(128)S(1)}, f32[16]{0:T(128)}, u32[]{:S(2)}) copy-start(f32[16]{0:T(128)} %param.10) | copy-start | bytes 196
  178.8 21.9 %all-to-all-start.3 = ((bf16[16,64,256]{2,1,0:T(8,128)(2,1)}), bf16[16,64,256]{2,1,0:T(8,128)(2,1)S(1)}, u32[]{:S(2)}, u32[]{:S(2)}) async-start(bf16[16,64,256]{2,1,0:T(8,128)(2,1)} %shard_map.75), calls=%async_computation.3 | async-start | bytes 1048576 | tf_op jit(solution)/shard_map/all_to_all | solution.py:82
  200.8 7.9 %copy-start.7 = (bf16[8,8,2,1024]{3,1,2,0:T(8,128)(2,1)S(1)}, bf16[8,8,2,1024]{3,1,2,0:T(8,128)(2,1)}, u32[]{:S(2)}) copy-start(bf16[8,8,2,1024]{3,1,2,0:T(8,128)(2,1)} %copy.18) | copy-start | bytes 786436
  200.8 7.8 %collective-permute-start = (bf16[4,64,256]{2,1,0:T(8,128)(2,1)S(1)}, bf16[4,64,256]{2,1,0:T(8,128)(2,1)S(1)}, u32[]{:S(2)}, u32[]{:S(2)}) collective-permute-start(bf16[4,64,256]{2,1,0:T(8,128)(2,1)S(1)} %dynamic-slice_bitcast_fusion), channel_id=1, source_target_pairs={{0,1},{1,0},{2,3},{3,2},{4,5},{5,4},{6,7},{7,6},{8,9},{9,8},{10,11... | collective-permute-start | bytes 393224 | tf_op jit(solution)/shard_map/ppermute | solution.py:90
Sparse Core Ops, SparseCore 0:
  24.2 153.4 all-gather.1

commit v2 on v1

v2 whole, which is shorter than its diff:
```python
import jax
import jax.numpy as jnp
from jax import lax
from jax.experimental import pallas as pl
from jax.experimental.pallas import tpu as pltpu
from jax.sharding import Mesh, PartitionSpec as P

CHOL = ("x", "zh")
PAIR = ("zl", "y", "core")
VMEM = pl.BlockSpec(memory_space=pltpu.VMEM)
ANY = pl.BlockSpec(memory_space=pl.ANY)
SMEM = pl.BlockSpec(memory_space=pltpu.SMEM)
LIMIT = pltpu.CompilerParams(vmem_limit_bytes=32 * 1024 * 1024)


def pair_at(zl, y, core):
    return y * 8 + zl * 2 + core


def chol_at(dx, dz):
    return (lax.axis_index("x") ^ dx) * 4 + (lax.axis_index("zh") ^ dz)


def select_kernel(orbitals, vectors, out):
    for dest in range(32):
        pair = pair_at(dest // 8, dest // 2 % 4, dest % 2)
        out[dest, 0] = vectors[orbitals[0, pair]]
        out[dest, 1] = vectors[orbitals[1, pair]]


def split_kernel(amps, out):
    for dx in range(4):
        for dz in range(4):
            start = pl.multiple_of(chol_at(dx, dz) * 128, 128)
            out[dx, dz] = amps[:, pl.ds(start, 128)]


def fock_kernel(fock, *refs):
    blocks, out, columns, product = refs[:4], refs[4], refs[5], refs[6]
    for dz in range(4):
        for dx in range(4):
            start = pl.multiple_of(chol_at(dx, dz) * 64, 64)
            columns[pl.ds(start, 64)] = blocks[dz][dx]
    product[...] = jnp.dot(fock[...], columns[...], preferred_element_type=jnp.float32).astype(jnp.bfloat16)
    for dz in range(4):
        for dx in range(4):
            start = pl.multiple_of(chol_at(dx, dz) * 64, 64)
            out[dz, dx] = product[pl.ds(start, 64)]


def local_kernel(offsets, orbitals, energy, amps, fock, *refs):
    blocks, out = refs[:4], refs[4]
    owner = lax.axis_index("zl") * 8 + lax.axis_index("y") * 2 + lax.axis_index("core")
    for dx in range(4):
        for dz in range(4):
            start = pl.multiple_of(chol_at(dx, dz) * 128, 128)
            out[:, pl.ds(start, 128)] = blocks[dx][dz].astype(jnp.float32)
    for slot in range(2):
        pair = jnp.minimum(offsets[owner] + slot, 31)
        shift = energy[orbitals[0, pair]] + energy[orbitals[1, pair]]
        here = slice(slot * 1024, (slot + 1) * 1024)
        amp = amps[:, here]
        term = jnp.dot(amp, fock[...], preferred_element_type=jnp.float32)
        out[:, here] += term - shift * amp.astype(jnp.float32)


def couple_kernel(case, vectors, *refs):
    out = refs[-1]
    pair = pair_at(lax.axis_index("zl"), lax.axis_index("y"), lax.axis_index("core"))
    swap = jnp.where(case[pair] == 0, 0.5, -0.5).astype(jnp.float32)
    left = vectors[:, 0].astype(jnp.float32)
    right = vectors[:, 1].astype(jnp.float32)
    rows = jnp.stack([left, right], axis=1).reshape(512, 1024)
    cols = jnp.stack([0.5 * right, swap * left], axis=1).reshape(512, 1024).astype(jnp.bfloat16)
    for i in range(4):
        block = rows[:, i * 256 : (i + 1) * 256].T.astype(jnp.bfloat16)
        for j in range(4):
            product = jnp.dot(block, cols[:, j * 256 : (j + 1) * 256], preferred_element_type=jnp.float32)
            out[i * 4 + j] = product.astype(jnp.bfloat16)


def add_kernel(parts, *refs):
    out = refs[-1]
    for y in range(4):
        total = jnp.zeros((256, 256), jnp.float32)
        for x in range(4):
            total += parts[x * 4 + y].astype(jnp.float32)
        for zh in range(4):
            out[zh, y] = total[zh * 64 : (zh + 1) * 64].astype(jnp.bfloat16)


def route_kernel(offsets, parts, *refs):
    out, total = refs[-2:]
    total[...] = jnp.sum(parts[...].astype(jnp.float32), axis=0).astype(jnp.bfloat16)
    member = lax.axis_index("zl") * 2 + lax.axis_index("core")
    for chip in range(16):
        end = offsets[chip * 2 + 2]
        which = jnp.maximum(((end + 7 - member) >> 3) - 1, 0)
        out[chip] = total[which]


def call(kernel, out, in_specs, *args, scratch=()):
    return pl.pallas_call(
        kernel, out_shape=out, in_specs=in_specs, out_specs=VMEM, scratch_shapes=list(scratch), compiler_params=LIMIT
    )(*args)


def half(*shape):
    return jax.ShapeDtypeStruct(shape, jnp.bfloat16)


def exchange(blocks, axis):
    moved = [lax.ppermute(blocks[k], axis, [(i, i ^ k) for i in range(4)]) for k in range(1, 4)]
    return [blocks[0], *moved]


def regroup(blocks):
    return [jnp.stack([block[k] for block in blocks]) for k in range(4)]


def body(chol_vectors, amplitudes, fock, orbital_energy, pair_orbitals, pair_case, owner_offsets):
    zl, y, core = (lax.axis_index(name) for name in PAIR)
    owner = zl * 8 + y * 2 + core
    flat = amplitudes.reshape(64, 2048)
    orbitals = pair_orbitals.T

    chosen = call(select_kernel, half(32, 2, 8, 1024), [SMEM, VMEM], orbitals, chol_vectors)
    vectors = lax.all_to_all(chosen, PAIR, 0, 0, tiled=True)
    columns = exchange(call(split_kernel, half(4, 4, 64, 128), [VMEM], flat), "x")

    partial = call(couple_kernel, half(16, 256, 256), [SMEM, VMEM] + [ANY] * 3, pair_case, vectors, *columns[1:])
    parts = lax.all_to_all(partial, ("x", "y"), 0, 0, tiled=True)
    columns = exchange(regroup(columns), "zh")
    left = call(
        fock_kernel, half(4, 4, 64, 128), [VMEM] * 5, fock, *columns,
        scratch=[pltpu.VMEM((1024, 128), jnp.bfloat16), pltpu.VMEM((1024, 128), jnp.bfloat16)],
    )

    parts = call(add_kernel, half(4, 4, 64, 256), [VMEM, ANY], parts, left)
    parts = lax.all_to_all(parts, "zh", 0, 0, tiled=True)
    left = exchange(left, "zh")

    routed = call(
        route_kernel, half(16, 64, 256), [SMEM, VMEM] + [ANY] * 3, owner_offsets, parts, *left[1:],
        scratch=[pltpu.VMEM((4, 64, 256), jnp.bfloat16)],
    )
    arrived = lax.all_to_all(routed, ("zl", "y"), 0, 0, tiled=True).reshape(4, 4, 64, 256)
    left = exchange(regroup(left), "x")
    local = call(
        local_kernel, jax.ShapeDtypeStruct((64, 2048), jnp.float32), [SMEM] * 3 + [VMEM] * 6,
        owner_offsets, orbitals, orbital_energy, flat, fock, *left,
    )

    def held(first):
        pair = first + ((first ^ core) & 1)
        return lax.dynamic_index_in_dim(arrived, (pair & 7) >> 1, 0, keepdims=False)

    first = owner_offsets[owner]
    count = owner_offsets[owner + 1] - first
    other = lax.ppermute(held(owner_offsets[owner ^ 1]), "core", [(0, 1), (1, 0)])
    mine = held(first)
    own_first = (first & 1) == core
    slots = [jnp.where(own_first, mine, other), jnp.where(own_first, other, mine)]
    pieces = []
    for slot in range(2):
        coupled = jnp.swapaxes(slots[slot], 0, 1).reshape(64, 1024).astype(jnp.float32)
        result = coupled + local[:, slot * 1024 : (slot + 1) * 1024]
        pieces.append(jnp.where(slot < count, result, 0.0))
    return jnp.stack(pieces, axis=1)


def solution(mesh):
    fine = Mesh(mesh.devices.reshape(4, 4, 4, 4, 2), ("x", "zh", "zl", "y", "core"))
    in_specs = (P(None, CHOL + PAIR, None), P(CHOL, PAIR, None), P(), P(), P(), P(), P())
    return jax.shard_map(body, mesh=fine, in_specs=in_specs, out_specs=P(CHOL, PAIR, None), check_vma=False)
```

time: 219 us -> 168 us (0.77)
  blocking collectives: 126 us -> 0 us
  starting transfers between devices: 18.8 us -> 94.4 us
  waiting for transfers between devices: 25.9 us -> 52.2 us
  between operations: 29.9 us -> 4.91 us
  Pallas kernels: 3.94 us -> 9.04 us
  matrix products: 4.03 us -> 0 us
    all_to_all x2 -> x0, blocking collectives: 126 us -> none  [the longest x1 92.5 us: body(): parts = lax.all_to_all(jnp.swapaxes(parts, 0, 1), 'zh', 0, 0, tiled=True)]
    ppermute x0 -> x12, starting transfers between devices: none -> 57.5 us  [exchange(): lax.ppermute(blocks[k], axis, [(i, i ^ k) for i in range(4)])]
    ppermute x0 -> x12, waiting for transfers between devices: none -> 39.4 us  [exchange(): lax.ppermute(blocks[k], axis, [(i, i ^ k) for i in range(4)])]
    all_to_all x0 -> x2, starting transfers between devices: none -> 17.7 us  [the longest x1 11.9 us: body(): parts = lax.all_to_all(parts, 'zh', 0, 0, tiled=True)]
    all_to_all x1, waiting for transfers between devices: 25.9 us -> 12.8 us  [body(): vectors = lax.all_to_all(chosen, PAIR, 0, 0, tiled=True)]
    pallas_call x3 -> x7, Pallas kernels: 3.94 us -> 9.04 us  [call(): pl.pallas_call(kernel, out_shape=out, in_specs=in_specs, out_specs=VMEM,...]
    dot_general x3 -> x0, matrix products: 4.03 us -> none  [the longest x1 3.03 us: body(): left = jnp.dot(rows, all_amps, preferred_element_type=jnp.float32)]
  transfers between devices with their start and end apart: 4 -> 17, of which waited for: 1 -> 6; matrix products, arithmetic and copies ran while one was open for 4% -> 1% of each run, Pallas kernels for 2% -> 1%
where the time goes in v2:
time: 168 us; the launch traced here: 167 us
  starting transfers between devices  94.4 us (56%)
  waiting for transfers between devices  52.2 us (31%)
  Pallas kernels  9.04 us (5%)
  local copies, waits for them, and re-layouts  5.98 us (4%)
  between operations  4.91 us (3%)
    ppermute x12, starting transfers between devices, exchange(): lax.ppermute(blocks[k], axis, [(i, i ^ k) for i in range(4)])  57.5 us
    ppermute x12, waiting for transfers between devices, exchange(): lax.ppermute(blocks[k], axis, [(i, i ^ k) for i in range(4)])  39.4 us
    all_to_all x1, waiting for transfers between devices, body(): vectors = lax.all_to_all(chosen, PAIR, 0, 0, tiled=True)  12.8 us
    all_to_all x1, starting transfers between devices, body(): parts = lax.all_to_all(parts, 'zh', 0, 0, tiled=True)  11.9 us
    all_to_all x1, starting transfers between devices, body(): vectors = lax.all_to_all(chosen, PAIR, 0, 0, tiled=True)  10.6 us
    pallas_call x7, Pallas kernels, call(): pl.pallas_call(kernel, out_shape=out, in_specs=in_specs, out_specs=VMEM,...  9.04 us
    all_to_all x1, starting transfers between devices, body(): parts = lax.all_to_all(partial, ('x', 'y'), 0, 0, tiled=True)  5.8 us
    ppermute x1, starting transfers between devices, body(): lax.ppermute(held(owner_offsets[owner ^ 1]), 'core', [(0, 1), (1, 0)])  5.01 us
  transfers between devices with their start and end apart: 17, of which 6 were waited for; matrix products, arithmetic and copies ran while one was open for 1% of the time, Pallas kernels for 1%

profile of v2, /device:TPU:1, one launch (start us, length us, event | category | flops | bytes accessed | tf_op | source)
XLA Modules:
  0.0 166.9 jit_solution(4364092670287538634)
XLA Ops:
  0.0 0.9 copy-done.3
  1.6 1.6 shard_map.73
  3.2 10.6 %all-to-all-start = ((bf16[32,2,8,1024]{3,2,1,0:T(8,128)(2,1)}), bf16[32,2,8,1024]{3,2,1,0:T(8,128)(2,1)S(1)}, u32[]{:S(2)}, u32[]{:S(2)}) async-start(bf16[32,2,8,1024]{3,2,1,0:T(8,128)(2,1)} %shard_map.73), calls=%async_computation | async-start | bytes 2097152 | tf_op jit(solution)/shard_map/all_to_all | solution.py:128
  14.0 2.9 %collective-permute-start = (bf16[4,64,128]{2,1,0:T(8,128)(2,1)S(1)}, bf16[4,64,128]{2,1,0:T(8,128)(2,1)S(1)}, u32[]{:S(2)}, u32[]{:S(2)}) collective-permute-start(bf16[4,64,128]{2,1,0:T(8,128)(2,1)S(1)} %get-tuple-element.24), channel_id=1, source_target_pairs={{0,128},{128,0},{256,384},{384,256},{1,129},{129,1},{257,385},{385... | collective-permute-start | bytes 196616 | tf_op jit(solution)/shard_map/ppermute | solution.py:113
  16.9 4.4 %collective-permute-start.1 = (bf16[4,64,128]{2,1,0:T(8,128)(2,1)S(1)}, bf16[4,64,128]{2,1,0:T(8,128)(2,1)S(1)}, u32[]{:S(2)}, u32[]{:S(2)}) collective-permute-start(bf16[4,64,128]{2,1,0:T(8,128)(2,1)S(1)} %get-tuple-element.23), channel_id=1, source_target_pairs={{0,256},{128,384},{256,0},{384,128},{1,257},{129,385},{257,1},{385... | collective-permute-start | bytes 196616 | tf_op jit(solution)/shard_map/ppermute | solution.py:113
  21.2 2.4 %collective-permute-start.2 = (bf16[4,64,128]{2,1,0:T(8,128)(2,1)S(1)}, bf16[4,64,128]{2,1,0:T(8,128)(2,1)S(1)}, u32[]{:S(2)}, u32[]{:S(2)}) collective-permute-start(bf16[4,64,128]{2,1,0:T(8,128)(2,1)S(1)} %get-tuple-element.22), channel_id=1, source_target_pairs={{0,384},{128,256},{256,128},{384,0},{1,385},{129,257},{257,129},{3... | collective-permute-start | bytes 196616 | tf_op jit(solution)/shard_map/ppermute | solution.py:113
  23.7 4.1 %collective-permute-done.2.refs_2_ = bf16[4,64,128]{2,1,0:T(8,128)(2,1)S(1)} collective-permute-done((bf16[4,64,128]{2,1,0:T(8,128)(2,1)S(1)}, bf16[4,64,128]{2,1,0:T(8,128)(2,1)S(1)}, u32[]{:S(2)}, u32[]{:S(2)}) %collective-permute-start.2) | collective-permute-done | bytes 65568 | tf_op jit(solution)/shard_map/ppermute | solution.py:113
  27.8 12.8 %all-to-all-done.vectors = bf16[32,2,8,1024]{3,2,1,0:T(8,128)(2,1)S(1)} async-done(((bf16[32,2,8,1024]{3,2,1,0:T(8,128)(2,1)}), bf16[32,2,8,1024]{3,2,1,0:T(8,128)(2,1)S(1)}, u32[]{:S(2)}, u32[]{:S(2)}) %all-to-all-start) | async-done | bytes 1048608 | tf_op jit(solution)/shard_map/all_to_all | solution.py:128
  40.5 1.9 %shard_map.75 = bf16[16,256,256]{2,1,0:T(8,128)(2,1)S(1)} custom-call(s32[32]{0:T(128)S(1)} %copy-done.7, bf16[32,2,8,1024]{3,2,1,0:T(8,128)(2,1)S(1)} %all-to-all-done.vectors, bf16[4,64,128]{2,1,0:T(8,128)(2,1)S(1)} %collective-permute-done.refs_0_, bf16[4,64,128]{2,1,0:T(8,128)(2,1)S(1)} %collective-permute-done.1.refs_1_, ...), custom_call_target="tpu_custom_call" | custom-call | tf_op jit(solution)/shard_map/pallas_call | solution.py:103
  42.4 1.3 copy-done.1
  43.7 5.8 %all-to-all-start.1 = ((bf16[16,256,256]{2,1,0:T(8,128)(2,1)}), bf16[16,256,256]{2,1,0:T(8,128)(2,1)}, u32[]{:S(2)}, u32[]{:S(2)}) async-start(bf16[16,256,256]{2,1,0:T(8,128)(2,1)} %copy-done.1), calls=%async_computation.1 | async-start | bytes 4194304 | tf_op jit(solution)/shard_map/all_to_all | solution.py:132
  49.6 8.8 %collective-permute-start.3 = (bf16[4,64,128]{2,1,0:T(8,128)(2,1)S(1)}, bf16[4,64,128]{2,1,0:T(8,128)(2,1)S(1)}, u32[]{:S(2)}, u32[]{:S(2)}) collective-permute-start(bf16[4,64,128]{2,1,0:T(8,128)(2,1)S(1)} %pad_maximum_fusion.2), channel_id=1, source_target_pairs={{0,32},{32,0},{64,96},{96,64},{1,33},{33,1},{65,97},{97,65},{2,34}... | collective-permute-start | bytes 196616 | tf_op jit(solution)/shard_map/ppermute | solution.py:113
  58.5 7.9 %collective-permute-start.4 = (bf16[4,64,128]{2,1,0:T(8,128)(2,1)S(1)}, bf16[4,64,128]{2,1,0:T(8,128)(2,1)S(1)}, u32[]{:S(2)}, u32[]{:S(2)}) collective-permute-start(bf16[4,64,128]{2,1,0:T(8,128)(2,1)S(1)} %pad_maximum_fusion.3), channel_id=1, source_target_pairs={{0,64},{32,96},{64,0},{96,32},{1,65},{33,97},{65,1},{97,33},{2,66}... | collective-permute-start | bytes 196616 | tf_op jit(solution)/shard_map/ppermute | solution.py:113
  66.4 1.9 %collective-permute-start.5 = (bf16[4,64,128]{2,1,0:T(8,128)(2,1)S(1)}, bf16[4,64,128]{2,1,0:T(8,128)(2,1)S(1)}, u32[]{:S(2)}, u32[]{:S(2)}) collective-permute-start(bf16[4,64,128]{2,1,0:T(8,128)(2,1)S(1)} %pad_maximum_fusion.4), channel_id=1, source_target_pairs={{0,96},{32,64},{64,32},{96,0},{1,97},{33,65},{65,33},{97,1},{2,98}... | collective-permute-start | bytes 196616 | tf_op jit(solution)/shard_map/ppermute | solution.py:113
  68.4 3.8 %collective-permute-done.4.refs_2_ = bf16[4,64,128]{2,1,0:T(8,128)(2,1)S(1)} collective-permute-done((bf16[4,64,128]{2,1,0:T(8,128)(2,1)S(1)}, bf16[4,64,128]{2,1,0:T(8,128)(2,1)S(1)}, u32[]{:S(2)}, u32[]{:S(2)}) %collective-permute-start.4) | collective-permute-done | bytes 65568 | tf_op jit(solution)/shard_map/ppermute | solution.py:113
  72.2 5.9 %collective-permute-done.5.refs_3_ = bf16[4,64,128]{2,1,0:T(8,128)(2,1)S(1)} collective-permute-done((bf16[4,64,128]{2,1,0:T(8,128)(2,1)S(1)}, bf16[4,64,128]{2,1,0:T(8,128)(2,1)S(1)}, u32[]{:S(2)}, u32[]{:S(2)}) %collective-permute-start.5) | collective-permute-done | bytes 65568 | tf_op jit(solution)/shard_map/ppermute | solution.py:113
  78.9 1.8 %shard_map.77 = bf16[4,4,64,256]{3,2,1,0:T(8,128)(2,1)S(1)} custom-call(bf16[16,256,256]{2,1,0:T(8,128)(2,1)} %all-to-all-done.1.parts, bf16[4,4,64,128]{3,2,1,0:T(8,128)(2,1)S(1)} %shard_map.76.refs_0_), custom_call_target="tpu_custom_call" | custom-call | tf_op jit(solution)/shard_map/pallas_call | solution.py:103
  80.7 0.8 copy-done.2
  81.5 11.9 %all-to-all-start.2 = ((bf16[4,4,64,256]{3,2,1,0:T(8,128)(2,1)}), bf16[4,4,64,256]{3,2,1,0:T(8,128)(2,1)S(1)}, u32[]{:S(2)}, u32[]{:S(2)}) async-start(bf16[4,4,64,256]{3,2,1,0:T(8,128)(2,1)} %copy-done.2), calls=%async_computation.2 | async-start | bytes 1048576 | tf_op jit(solution)/shard_map/all_to_all | solution.py:140
  93.4 7.3 %collective-permute-start.6 = (bf16[4,64,128]{2,1,0:T(8,128)(2,1)S(1)}, bf16[4,64,128]{2,1,0:T(8,128)(2,1)S(1)}, u32[]{:S(2)}, u32[]{:S(2)}) collective-permute-start(bf16[4,64,128]{2,1,0:T(8,128)(2,1)S(1)} %get-tuple-element.17), channel_id=1, source_target_pairs={{0,32},{32,0},{64,96},{96,64},{1,33},{33,1},{65,97},{97,65},{2,34}... | collective-permute-start | bytes 196616 | tf_op jit(solution)/shard_map/ppermute | solution.py:113
  100.7 7.0 %collective-permute-start.7 = (bf16[4,64,128]{2,1,0:T(8,128)(2,1)S(1)}, bf16[4,64,128]{2,1,0:T(8,128)(2,1)S(1)}, u32[]{:S(2)}, u32[]{:S(2)}) collective-permute-start(bf16[4,64,128]{2,1,0:T(8,128)(2,1)S(1)} %get-tuple-element.16), channel_id=1, source_target_pairs={{0,64},{32,96},{64,0},{96,32},{1,65},{33,97},{65,1},{97,33},{2,66}... | collective-permute-start | bytes 196616 | tf_op jit(solution)/shard_map/ppermute | solution.py:113
  107.8 1.9 %collective-permute-start.8 = (bf16[4,64,128]{2,1,0:T(8,128)(2,1)S(1)}, bf16[4,64,128]{2,1,0:T(8,128)(2,1)S(1)}, u32[]{:S(2)}, u32[]{:S(2)}) collective-permute-start(bf16[4,64,128]{2,1,0:T(8,128)(2,1)S(1)} %get-tuple-element.15), channel_id=1, source_target_pairs={{0,96},{32,64},{64,32},{96,0},{1,97},{33,65},{65,33},{97,1},{2,98}... | collective-permute-start | bytes 196616 | tf_op jit(solution)/shard_map/ppermute | solution.py:113
  109.7 23.2 %collective-permute-done.6.refs_0_ = bf16[4,64,128]{2,1,0:T(8,128)(2,1)S(1)} collective-permute-done((bf16[4,64,128]{2,1,0:T(8,128)(2,1)S(1)}, bf16[4,64,128]{2,1,0:T(8,128)(2,1)S(1)}, u32[]{:S(2)}, u32[]{:S(2)}) %collective-permute-start.6) | collective-permute-done | bytes 65568 | tf_op jit(solution)/shard_map/ppermute | solution.py:113
  132.9 1.5 shard_map.78
  134.4 3.6 %all-to-all-start.3 = ((bf16[16,64,256]{2,1,0:T(8,128)(2,1)}), bf16[16,64,256]{2,1,0:T(8,128)(2,1)S(1)}, u32[]{:S(2)}, u32[]{:S(2)}) async-start(bf16[16,64,256]{2,1,0:T(8,128)(2,1)} %shard_map.78), calls=%async_computation.3 | async-start | bytes 1048576 | tf_op jit(solution)/shard_map/all_to_all | solution.py:147
  143.1 1.9 %collective-permute-start.10 = (bf16[4,64,128]{2,1,0:T(8,128)(2,1)S(1)}, bf16[4,64,128]{2,1,0:T(8,128)(2,1)S(1)}, u32[]{:S(2)}, u32[]{:S(2)}) collective-permute-start(bf16[4,64,128]{2,1,0:T(8,128)(2,1)S(1)} %pad_maximum_fusion.6), channel_id=1, source_target_pairs={{0,128},{128,0},{256,384},{384,256},{1,129},{129,1},{257,385},{385... | collective-permute-start | bytes 196616 | tf_op jit(solution)/shard_map/ppermute | solution.py:113
  145.1 6.1 %collective-permute-start.11 = (bf16[4,64,128]{2,1,0:T(8,128)(2,1)S(1)}, bf16[4,64,128]{2,1,0:T(8,128)(2,1)S(1)}, u32[]{:S(2)}, u32[]{:S(2)}) collective-permute-start(bf16[4,64,128]{2,1,0:T(8,128)(2,1)S(1)} %pad_maximum_fusion.7), channel_id=1, source_target_pairs={{0,256},{128,384},{256,0},{384,128},{1,257},{129,385},{257,1},{385... | collective-permute-start | bytes 196616 | tf_op jit(solution)/shard_map/ppermute | solution.py:113
  151.4 5.0 %collective-permute-start.9 = (bf16[4,64,256]{2,0,1:T(4,128)(2,1)S(1)}, bf16[4,64,256]{2,0,1:T(4,128)(2,1)S(1)}, u32[]{:S(2)}, u32[]{:S(2)}) collective-permute-start(bf16[4,64,256]{2,0,1:T(4,128)(2,1)S(1)} %bitcast.65), channel_id=1, source_target_pairs={{0,1},{1,0},{2,3},{3,2},{4,5},{5,4},{6,7},{7,6},{8,9},{9,8},{10,11... | collective-permute-start | bytes 393224 | tf_op jit(solution)/shard_map/ppermute | solution.py:160
  156.4 5.0 %collective-permute-start.12 = (bf16[4,64,128]{2,1,0:T(8,128)(2,1)S(1)}, bf16[4,64,128]{2,1,0:T(8,128)(2,1)S(1)}, u32[]{:S(2)}, u32[]{:S(2)}) collective-permute-start(bf16[4,64,128]{2,1,0:T(8,128)(2,1)S(1)} %pad_maximum_fusion.8), channel_id=1, source_target_pairs={{0,384},{128,256},{256,128},{384,0},{1,385},{129,257},{257,129},{3... | collective-permute-start | bytes 196616 | tf_op jit(solution)/shard_map/ppermute | solution.py:113
  161.5 2.4 %collective-permute-done.12.refs_3_ = bf16[4,64,128]{2,1,0:T(8,128)(2,1)S(1)} collective-permute-done((bf16[4,64,128]{2,1,0:T(8,128)(2,1)S(1)}, bf16[4,64,128]{2,1,0:T(8,128)(2,1)S(1)}, u32[]{:S(2)}, u32[]{:S(2)}) %collective-permute-start.12) | collective-permute-done | bytes 65568 | tf_op jit(solution)/shard_map/ppermute | solution.py:113
  163.9 1.4 shard_map.79
  165.7 1.2 copy.10
  (57 shorter events, 3.0 us)
Async XLA Ops:
  0.0 0.9 copy-start.3
  1.0 0.7 copy-start.5
  1.6 12.2 %copy-start.9 = (bf16[64,2,1024]{2,1,0:T(2,128)(2,1)S(1)}, bf16[64,2,1024]{2,1,0:T(2,128)(2,1)}, u32[]{:S(2)}) copy-start(bf16[64,2,1024]{2,1,0:T(2,128)(2,1)} %param.8) | copy-start | bytes 786436
  3.2 37.3 %copy-start.7 = (s32[32]{0:T(128)S(1)}, s32[32]{0:T(128)}, u32[]{:S(2)}) copy-start(s32[32]{0:T(128)} %case.1) | copy-start | bytes 388
  3.2 37.3 %all-to-all-start = ((bf16[32,2,8,1024]{3,2,1,0:T(8,128)(2,1)}), bf16[32,2,8,1024]{3,2,1,0:T(8,128)(2,1)S(1)}, u32[]{:S(2)}, u32[]{:S(2)}) async-start(bf16[32,2,8,1024]{3,2,1,0:T(8,128)(2,1)} %shard_map.73), calls=%async_computation | async-start | bytes 2097152 | tf_op jit(solution)/shard_map/all_to_all | solution.py:128
  14.0 9.6 %collective-permute-start = (bf16[4,64,128]{2,1,0:T(8,128)(2,1)S(1)}, bf16[4,64,128]{2,1,0:T(8,128)(2,1)S(1)}, u32[]{:S(2)}, u32[]{:S(2)}) collective-permute-start(bf16[4,64,128]{2,1,0:T(8,128)(2,1)S(1)} %get-tuple-element.24), channel_id=1, source_target_pairs={{0,128},{128,0},{256,384},{384,256},{1,129},{129,1},{257,385},{385... | collective-permute-start | bytes 196616 | tf_op jit(solution)/shard_map/ppermute | solution.py:113
  16.9 6.8 %collective-permute-start.1 = (bf16[4,64,128]{2,1,0:T(8,128)(2,1)S(1)}, bf16[4,64,128]{2,1,0:T(8,128)(2,1)S(1)}, u32[]{:S(2)}, u32[]{:S(2)}) collective-permute-start(bf16[4,64,128]{2,1,0:T(8,128)(2,1)S(1)} %get-tuple-element.23), channel_id=1, source_target_pairs={{0,256},{128,384},{256,0},{384,128},{1,257},{129,385},{257,1},{385... | collective-permute-start | bytes 196616 | tf_op jit(solution)/shard_map/ppermute | solution.py:113
  21.2 6.5 %collective-permute-start.2 = (bf16[4,64,128]{2,1,0:T(8,128)(2,1)S(1)}, bf16[4,64,128]{2,1,0:T(8,128)(2,1)S(1)}, u32[]{:S(2)}, u32[]{:S(2)}) collective-permute-start(bf16[4,64,128]{2,1,0:T(8,128)(2,1)S(1)} %get-tuple-element.22), channel_id=1, source_target_pairs={{0,384},{128,256},{256,128},{384,0},{1,385},{129,257},{257,129},{3... | collective-permute-start | bytes 196616 | tf_op jit(solution)/shard_map/ppermute | solution.py:113
  42.4 1.3 copy-start.1
  43.7 34.4 %copy-start = (bf16[1024,1024]{1,0:T(8,128)(2,1)S(1)}, bf16[1024,1024]{1,0:T(8,128)(2,1)}, u32[]{:S(2)}) copy-start(bf16[1024,1024]{1,0:T(8,128)(2,1)} %fock.3) | copy-start | bytes 6291460
  43.7 35.1 %all-to-all-start.1 = ((bf16[16,256,256]{2,1,0:T(8,128)(2,1)}), bf16[16,256,256]{2,1,0:T(8,128)(2,1)}, u32[]{:S(2)}, u32[]{:S(2)}) async-start(bf16[16,256,256]{2,1,0:T(8,128)(2,1)} %copy-done.1), calls=%async_computation.1 | async-start | bytes 4194304 | tf_op jit(solution)/shard_map/all_to_all | solution.py:132
  49.6 18.8 %collective-permute-start.3 = (bf16[4,64,128]{2,1,0:T(8,128)(2,1)S(1)}, bf16[4,64,128]{2,1,0:T(8,128)(2,1)S(1)}, u32[]{:S(2)}, u32[]{:S(2)}) collective-permute-start(bf16[4,64,128]{2,1,0:T(8,128)(2,1)S(1)} %pad_maximum_fusion.2), channel_id=1, source_target_pairs={{0,32},{32,0},{64,96},{96,64},{1,33},{33,1},{65,97},{97,65},{2,34}... | collective-permute-start | bytes 196616 | tf_op jit(solution)/shard_map/ppermute | solution.py:113
  58.5 13.7 %collective-permute-start.4 = (bf16[4,64,128]{2,1,0:T(8,128)(2,1)S(1)}, bf16[4,64,128]{2,1,0:T(8,128)(2,1)S(1)}, u32[]{:S(2)}, u32[]{:S(2)}) collective-permute-start(bf16[4,64,128]{2,1,0:T(8,128)(2,1)S(1)} %pad_maximum_fusion.3), channel_id=1, source_target_pairs={{0,64},{32,96},{64,0},{96,32},{1,65},{33,97},{65,1},{97,33},{2,66}... | collective-permute-start | bytes 196616 | tf_op jit(solution)/shard_map/ppermute | solution.py:113
  66.4 11.7 %collective-permute-start.5 = (bf16[4,64,128]{2,1,0:T(8,128)(2,1)S(1)}, bf16[4,64,128]{2,1,0:T(8,128)(2,1)S(1)}, u32[]{:S(2)}, u32[]{:S(2)}) collective-permute-start(bf16[4,64,128]{2,1,0:T(8,128)(2,1)S(1)} %pad_maximum_fusion.4), channel_id=1, source_target_pairs={{0,96},{32,64},{64,32},{96,0},{1,97},{33,65},{65,33},{97,1},{2,98}... | collective-permute-start | bytes 196616 | tf_op jit(solution)/shard_map/ppermute | solution.py:113
  78.9 54.0 %copy-start.4 = (s32[33]{0:T(128)S(1)}, s32[33]{0:T(128)}, u32[]{:S(2)}) copy-start(s32[33]{0:T(128)} %offsets.3) | copy-start | bytes 400
  80.7 0.8 copy-start.2
  81.5 51.4 %all-to-all-start.2 = ((bf16[4,4,64,256]{3,2,1,0:T(8,128)(2,1)}), bf16[4,4,64,256]{3,2,1,0:T(8,128)(2,1)S(1)}, u32[]{:S(2)}, u32[]{:S(2)}) async-start(bf16[4,4,64,256]{3,2,1,0:T(8,128)(2,1)} %copy-done.2), calls=%async_computation.2 | async-start | bytes 1048576 | tf_op jit(solution)/shard_map/all_to_all | solution.py:140
  93.4 39.4 %collective-permute-start.6 = (bf16[4,64,128]{2,1,0:T(8,128)(2,1)S(1)}, bf16[4,64,128]{2,1,0:T(8,128)(2,1)S(1)}, u32[]{:S(2)}, u32[]{:S(2)}) collective-permute-start(bf16[4,64,128]{2,1,0:T(8,128)(2,1)S(1)} %get-tuple-element.17), channel_id=1, source_target_pairs={{0,32},{32,0},{64,96},{96,64},{1,33},{33,1},{65,97},{97,65},{2,34}... | collective-permute-start | bytes 196616 | tf_op jit(solution)/shard_map/ppermute | solution.py:113
  100.7 32.2 %collective-permute-start.7 = (bf16[4,64,128]{2,1,0:T(8,128)(2,1)S(1)}, bf16[4,64,128]{2,1,0:T(8,128)(2,1)S(1)}, u32[]{:S(2)}, u32[]{:S(2)}) collective-permute-start(bf16[4,64,128]{2,1,0:T(8,128)(2,1)S(1)} %get-tuple-element.16), channel_id=1, source_target_pairs={{0,64},{32,96},{64,0},{96,32},{1,65},{33,97},{65,1},{97,33},{2,66}... | collective-permute-start | bytes 196616 | tf_op jit(solution)/shard_map/ppermute | solution.py:113
  107.7 56.1 %copy-start.6 = (s32[32,2]{0,1:T(2,128)S(1)}, s32[32,2]{0,1:T(2,128)}, u32[]{:S(2)}) copy-start(s32[32,2]{0,1:T(2,128)} %param.11) | copy-start | bytes 772
  107.8 56.1 %copy-start.8 = (f32[16]{0:T(128)S(1)}, f32[16]{0:T(128)}, u32[]{:S(2)}) copy-start(f32[16]{0:T(128)} %energy.1) | copy-start | bytes 196
  107.8 25.1 %collective-permute-start.8 = (bf16[4,64,128]{2,1,0:T(8,128)(2,1)S(1)}, bf16[4,64,128]{2,1,0:T(8,128)(2,1)S(1)}, u32[]{:S(2)}, u32[]{:S(2)}) collective-permute-start(bf16[4,64,128]{2,1,0:T(8,128)(2,1)S(1)} %get-tuple-element.15), channel_id=1, source_target_pairs={{0,96},{32,64},{64,32},{96,0},{1,97},{33,65},{65,33},{97,1},{2,98}... | collective-permute-start | bytes 196616 | tf_op jit(solution)/shard_map/ppermute | solution.py:113
  134.4 16.9 %all-to-all-start.3 = ((bf16[16,64,256]{2,1,0:T(8,128)(2,1)}), bf16[16,64,256]{2,1,0:T(8,128)(2,1)S(1)}, u32[]{:S(2)}, u32[]{:S(2)}) async-start(bf16[16,64,256]{2,1,0:T(8,128)(2,1)} %shard_map.78), calls=%async_computation.3 | async-start | bytes 1048576 | tf_op jit(solution)/shard_map/all_to_all | solution.py:147
  143.1 18.3 %collective-permute-start.10 = (bf16[4,64,128]{2,1,0:T(8,128)(2,1)S(1)}, bf16[4,64,128]{2,1,0:T(8,128)(2,1)S(1)}, u32[]{:S(2)}, u32[]{:S(2)}) collective-permute-start(bf16[4,64,128]{2,1,0:T(8,128)(2,1)S(1)} %pad_maximum_fusion.6), channel_id=1, source_target_pairs={{0,128},{128,0},{256,384},{384,256},{1,129},{129,1},{257,385},{385... | collective-permute-start | bytes 196616 | tf_op jit(solution)/shard_map/ppermute | solution.py:113
  145.1 16.4 %collective-permute-start.11 = (bf16[4,64,128]{2,1,0:T(8,128)(2,1)S(1)}, bf16[4,64,128]{2,1,0:T(8,128)(2,1)S(1)}, u32[]{:S(2)}, u32[]{:S(2)}) collective-permute-start(bf16[4,64,128]{2,1,0:T(8,128)(2,1)S(1)} %pad_maximum_fusion.7), channel_id=1, source_target_pairs={{0,256},{128,384},{256,0},{384,128},{1,257},{129,385},{257,1},{385... | collective-permute-start | bytes 196616 | tf_op jit(solution)/shard_map/ppermute | solution.py:113
  151.4 13.9 %collective-permute-start.9 = (bf16[4,64,256]{2,0,1:T(4,128)(2,1)S(1)}, bf16[4,64,256]{2,0,1:T(4,128)(2,1)S(1)}, u32[]{:S(2)}, u32[]{:S(2)}) collective-permute-start(bf16[4,64,256]{2,0,1:T(4,128)(2,1)S(1)} %bitcast.65), channel_id=1, source_target_pairs={{0,1},{1,0},{2,3},{3,2},{4,5},{5,4},{6,7},{7,6},{8,9},{9,8},{10,11... | collective-permute-start | bytes 393224 | tf_op jit(solution)/shard_map/ppermute | solution.py:160
  156.4 7.4 %collective-permute-start.12 = (bf16[4,64,128]{2,1,0:T(8,128)(2,1)S(1)}, bf16[4,64,128]{2,1,0:T(8,128)(2,1)S(1)}, u32[]{:S(2)}, u32[]{:S(2)}) collective-permute-start(bf16[4,64,128]{2,1,0:T(8,128)(2,1)S(1)} %pad_maximum_fusion.8), channel_id=1, source_target_pairs={{0,384},{128,256},{256,128},{384,0},{1,385},{129,257},{257,129},{3... | collective-permute-start | bytes 196616 | tf_op jit(solution)/shard_map/ppermute | solution.py:113

commit v3 on v0

v3 whole, which is shorter than its diff:
```python
import jax
import jax.numpy as jnp
from jax import lax
from jax.experimental import pallas as pl
from jax.experimental.pallas import tpu as pltpu
from jax.sharding import Mesh, PartitionSpec as P

CHOL = ("x", "zh")
PAIR = ("zl", "y", "core")
VMEM = pl.BlockSpec(memory_space=pltpu.VMEM)
ANY = pl.BlockSpec(memory_space=pl.ANY)
TURNS = ("zh", "zh")
SMEM = pl.BlockSpec(memory_space=pltpu.SMEM)
LIMIT = pltpu.CompilerParams(vmem_limit_bytes=32 * 1024 * 1024)


def pair_at(zl, y, core):
    return y * 8 + zl * 2 + core


def owner_index():
    return lax.axis_index("zl") * 8 + lax.axis_index("y") * 2 + lax.axis_index("core")


def first_at(offsets, chip, core):
    first = offsets[chip * 2]
    return first + ((first ^ core) & 1)


def prepare_kernel(offsets, orbitals, vectors, other_vectors, amps, other_amps, *refs):
    out, held = refs[-2:]
    core = lax.axis_index("core")
    for dest in range(16):
        pair = pair_at(dest // 4, dest % 4, core)
        for side in range(2):
            for which, source in enumerate((vectors, other_vectors)):
                chosen = source[orbitals[side, pair]]
                for part in range(4):
                    out[dest, side * 8 + which * 4 + part] = chosen[:, part * 256 : (part + 1) * 256]
    for slot in range(2):
        here = slice(slot * 1024, (slot + 1) * 1024)
        held[core * 2 + slot] = amps[:, here]
        held[(1 - core) * 2 + slot] = other_amps[:, here]
    chip = lax.axis_index("zl") * 4 + lax.axis_index("y")
    middle = offsets[chip * 2 + 1]
    for j in range(2):
        pair = first_at(offsets, chip, core) + 2 * j
        late = pair >= middle
        slot = jnp.clip(jnp.where(late, pair - middle, pair - offsets[chip * 2]), 0, 1)
        wide = held[late.astype(jnp.int32) * 2 + slot].astype(jnp.float32)
        for dest in range(16):
            for part in range(2):
                start = dest % 2 * 512 + part * 256
                tile = wide[dest // 2 * 8 : (dest // 2 + 1) * 8, start : start + 256]
                out[dest, 16 + j * 2 + part] = tile.astype(jnp.bfloat16)


def collect_kernel(offsets, arrived, out):
    core = lax.axis_index("core")
    for chip in range(16):
        for j in range(2):
            pair = first_at(offsets, chip, core) + 2 * j

            @pl.when(pair < offsets[chip * 2 + 2])
            def _():
                dest = ((pair & 7) >> 1) * 4 + (pair >> 3)
                for part in range(2):
                    out[dest, part] = arrived[chip, 16 + j * 2 + part]


def local_kernel(offsets, orbitals, energy, amps, fock, out):
    owner = owner_index()
    both = jnp.concatenate([amps[:, :1024], amps[:, 1024:]], axis=0)
    term = jnp.dot(both, fock[...], preferred_element_type=jnp.float32)
    for slot in range(2):
        pair = jnp.minimum(offsets[owner] + slot, 31)
        shift = energy[orbitals[0, pair]] + energy[orbitals[1, pair]]
        amp = both[slot * 64 : (slot + 1) * 64].astype(jnp.float32)
        out[:, slot * 1024 : (slot + 1) * 1024] = term[slot * 64 : (slot + 1) * 64] - shift * amp


def couple_kernel(case, arrived, amp_tiles, fock, out, rows, cols):
    pair = pair_at(lax.axis_index("zl"), lax.axis_index("y"), lax.axis_index("core"))
    x, zh = lax.axis_index("x"), lax.axis_index("zh")
    swap = jnp.where(case[pair] == 0, 0.5, -0.5).astype(jnp.float32)
    cols[512:640] = jnp.zeros((128, 1024), jnp.bfloat16)
    top = pl.multiple_of(512 + (zh & 1) * 64, 64)
    for part in range(4):
        here = slice(part * 256, (part + 1) * 256)
        for which in range(2):
            left = arrived[:, which * 4 + part].astype(jnp.float32).reshape(128, 256)
            right = arrived[:, 8 + which * 4 + part].astype(jnp.float32).reshape(128, 256)
            start = which * 128
            rows[start : start + 128, here] = left
            rows[start + 256 : start + 384, here] = right
            cols[start : start + 128, here] = (0.5 * right).astype(jnp.bfloat16)
            cols[start + 256 : start + 384, here] = (swap * left).astype(jnp.bfloat16)
        tiles = [amp_tiles[group * 2 + part // 2, part % 2].astype(jnp.float32) for group in range(8)]
        cols[pl.ds(top, 64), here] = jnp.concatenate(tiles, axis=0).astype(jnp.bfloat16)
    lanes = pl.multiple_of((x * 2 + (zh >> 1)) * 128, 128)
    for row in range(4):
        here = slice(row * 256, (row + 1) * 256)
        block = jnp.concatenate([rows[:, here].T.astype(jnp.bfloat16), fock[here, pl.ds(lanes, 128)]], axis=1)
        product = jnp.dot(block, cols[...], preferred_element_type=jnp.float32)
        out[row] = product.astype(jnp.bfloat16)


def finish_kernel(parts, out):
    for y in range(4):
        here = slice(y * 256, (y + 1) * 256)
        total = parts[0, :, here].astype(jnp.float32)
        for x in range(1, 4):
            total += parts[x, :, here].astype(jnp.float32)
        for zh in range(4):
            out[zh * 4 + y] = total[zh * 64 : (zh + 1) * 64].astype(jnp.bfloat16)


def route_kernel(offsets, parts, out, total):
    for y in range(4):
        sums = parts[y].astype(jnp.float32)
        for zh in range(1, 4):
            sums += parts[zh * 4 + y].astype(jnp.float32)
        total[y] = sums.astype(jnp.bfloat16)
    member = lax.axis_index("zl") * 2 + lax.axis_index("core")
    for chip in range(16):
        end = offsets[chip * 2 + 2]
        which = jnp.maximum(((end + 7 - member) >> 3) - 1, 0)
        out[chip] = total[which]


def pick_kernel(offsets, arrived, mine, theirs):
    core, owner = lax.axis_index("core"), owner_index()
    for who, out in ((owner, mine), (owner ^ 1, theirs)):
        first = offsets[who]
        pair = first + ((first ^ core) & 1)
        for y in range(4):
            out[:, y * 256 : (y + 1) * 256] = arrived[((pair & 7) >> 1) * 4 + y]


def write_kernel(offsets, mine, other, local, out):
    owner = owner_index()
    first = offsets[owner]
    count = offsets[owner + 1] - first
    for slot in range(2):
        own = ((first + slot) & 1) == lax.axis_index("core")
        coupled = jnp.where(own, mine[...].astype(jnp.float32), other[...].astype(jnp.float32))
        result = coupled + local[:, slot * 1024 : (slot + 1) * 1024]
        out[:, slot, :] = jnp.where(slot < count, result, 0.0)


def call(kernel, out, in_specs, *args, scratch=()):
    return pl.pallas_call(
        kernel,
        out_shape=out,
        in_specs=in_specs,
        out_specs=jax.tree.map(lambda _: VMEM, out),
        scratch_shapes=list(scratch),
        compiler_params=LIMIT,
    )(*args)


def half(*shape):
    return jax.ShapeDtypeStruct(shape, jnp.bfloat16)


def single(*shape):
    return jax.ShapeDtypeStruct(shape, jnp.float32)


def body(chol_vectors, amplitudes, fock, orbital_energy, pair_orbitals, pair_case, owner_offsets):
    flat = amplitudes.reshape(64, 2048)
    orbitals = pair_orbitals.T

    other_vectors, other_flat = lax.ppermute((chol_vectors, flat), "core", [(0, 1), (1, 0)])
    token = orbital_energy
    for axis in TURNS:
        token = lax.ppermute(token, (axis, "core"), [(i * 2 + 1, (i + 1) % 4 * 2 + 1) for i in range(4)])
    chosen = call(
        prepare_kernel, half(16, 20, 8, 256), [SMEM] * 2 + [VMEM] * 4 + [ANY],
        owner_offsets, orbitals, chol_vectors, other_vectors, flat, other_flat, token,
        scratch=[pltpu.VMEM((4, 64, 1024), jnp.bfloat16)],
    )
    arrived = lax.all_to_all(chosen, ("zl", "y"), 0, 0, tiled=True)
    tiles = call(collect_kernel, half(16, 2, 8, 256), [SMEM, VMEM], owner_offsets, arrived)
    tiles = lax.all_to_all(tiles, ("zl", "y"), 0, 0, tiled=True)
    partial = call(
        couple_kernel, half(4, 256, 1024), [SMEM, VMEM, VMEM, VMEM], pair_case, arrived, tiles, fock,
        scratch=[pltpu.VMEM((512, 1024), jnp.float32), pltpu.VMEM((640, 1024), jnp.bfloat16)],
    )
    parts = lax.all_to_all(partial, "x", 0, 0, tiled=True)
    parts = call(finish_kernel, half(16, 64, 256), [VMEM], parts)
    parts = lax.all_to_all(parts, ("zh", "y"), 0, 0, tiled=True)
    routed = call(
        route_kernel, half(16, 64, 256), [SMEM, VMEM], owner_offsets, parts,
        scratch=[pltpu.VMEM((4, 64, 256), jnp.bfloat16)],
    )
    arrived = lax.all_to_all(routed, ("zl", "y"), 0, 0, tiled=True)
    mine, theirs = call(pick_kernel, [half(64, 1024), half(64, 1024)], [SMEM, VMEM], owner_offsets, arrived)
    other = lax.ppermute(theirs, "core", [(0, 1), (1, 0)])
    local = call(
        local_kernel, single(64, 2048), [SMEM] * 3 + [VMEM] * 2, owner_offsets, orbitals, orbital_energy, flat, fock
    )
    return call(write_kernel, single(64, 2, 1024), [SMEM] + [VMEM] * 3, owner_offsets, mine, other, local)


def solution(mesh):
    fine = Mesh(mesh.devices.reshape(4, 4, 4, 4, 2), ("x", "zh", "zl", "y", "core"))
    in_specs = (P(None, CHOL + PAIR, None), P(CHOL, PAIR, None), P(), P(), P(), P(), P())
    return jax.shard_map(body, mesh=fine, in_specs=in_specs, out_specs=P(CHOL, PAIR, None), check_vma=False)
```

time: 276 us -> 147 us (0.53)
  waiting for transfers between devices: 230 us -> 8.56 us
  blocking collectives: 0 us -> 105 us
  starting transfers between devices: 0.04 us -> 20.8 us
  local copies, waits for them, and re-layouts: 20.2 us -> 3.31 us
  between operations: 13.5 us -> 0.16 us
  matrix products: 9.23 us -> 0 us
  Pallas kernels: 0 us -> 8.08 us
    reduce_scatter x1 -> x0, waiting for transfers between devices: 154 us -> none  [body(): lax.psum_scatter((jnp.concatenate(pieces, axis=1) + left_part).astype(jnp...]
    all_to_all x0 -> x5, blocking collectives: none -> 105 us  [the longest x1 30.2 us: body(): parts = lax.all_to_all(parts, ('zh', 'y'), 0, 0, tiled=True)]
    all_gather x1 -> x0, waiting for transfers between devices: 75.6 us -> none  [body(): gathered = lax.all_gather(chol_vectors, 'pair', axis=1, tiled=True)]
    ppermute x0 -> x5, starting transfers between devices: none -> 20.8 us  [the longest x2 10.7 us: body(): lax.ppermute((chol_vectors, flat), 'core', [(0, 1), (1, 0)])]
    dot_general x6 -> x0, matrix products: 9.23 us -> none  [the longest x1 3.07 us: body(): left_part = jnp.dot(fock_band, amp_flat, preferred_element_type=jnp.float32)]
    gather x5 -> x0, local copies, waits for them, and re-layouts: 8.58 us -> none  [the longest x1 5.42 us: body(): needed = gathered[orbit_mine.reshape(-1)]]
    ppermute x0 -> x5, waiting for transfers between devices: none -> 8.56 us  [the longest x2 8.28 us: body(): lax.ppermute(token, (axis, 'core'), [(i * 2 + 1, (i + 1) % 4 * 2 + 1) for...]
    pallas_call x0 -> x8, Pallas kernels: none -> 8.08 us  [call(): pl.pallas_call(kernel, out_shape=out, in_specs=in_specs, out_specs=jax.tr...]
  transfers between devices with their start and end apart: 2 -> 5, of which waited for: 2 -> 3; matrix products, arithmetic and copies ran while one was open for 3% -> 0% of each run, Pallas kernels for 0% -> 1%
where the time goes in v3:
time: 147 us; the launch traced here: 146 us
  blocking collectives  105 us (71%)
  starting transfers between devices  20.8 us (14%)
  waiting for transfers between devices  8.56 us (6%)
  Pallas kernels  8.08 us (5%)
  local copies, waits for them, and re-layouts  3.31 us (2%)
    all_to_all x1, blocking collectives, body(): parts = lax.all_to_all(parts, ('zh', 'y'), 0, 0, tiled=True)  30.2 us
    all_to_all x1, blocking collectives, body(): arrived = lax.all_to_all(chosen, ('zl', 'y'), 0, 0, tiled=True)  25.9 us
    all_to_all x1, blocking collectives, body(): parts = lax.all_to_all(partial, 'x', 0, 0, tiled=True)  19.2 us
    all_to_all x1, blocking collectives, body(): arrived = lax.all_to_all(routed, ('zl', 'y'), 0, 0, tiled=True)  18.5 us
    all_to_all x1, blocking collectives, body(): tiles = lax.all_to_all(tiles, ('zl', 'y'), 0, 0, tiled=True)  11.4 us
    ppermute x2, starting transfers between devices, body(): lax.ppermute((chol_vectors, flat), 'core', [(0, 1), (1, 0)])  10.7 us
    ppermute x2, waiting for transfers between devices, body(): lax.ppermute(token, (axis, 'core'), [(i * 2 + 1, (i + 1) % 4 * 2 + 1) for...  8.28 us
    ppermute x2, starting transfers between devices, body(): lax.ppermute(token, (axis, 'core'), [(i * 2 + 1, (i + 1) % 4 * 2 + 1) for...  8.21 us
  transfers between devices with their start and end apart: 5, of which 3 were waited for; matrix products, arithmetic and copies ran while one was open for 0% of the time, Pallas kernels for 1%

profile of v3, /device:TPU:1, one launch (start us, length us, event | category | flops | bytes accessed | tf_op | source)
XLA Modules:
  0.0 146.2 jit_solution(17027758015914753923)
XLA Ops:
  0.0 1.0 copy.8
  1.0 8.8 %collective-permute-start.1 = (bf16[64,2048]{1,0:T(8,128)(2,1)S(1)}, bf16[64,2048]{1,0:T(8,128)(2,1)S(1)}, u32[]{:S(2)}, u32[]{:S(2)}) collective-permute-start(bf16[64,2048]{1,0:T(8,128)(2,1)S(1)} %bitcast.3), channel_id=1, source_target_pairs={{0,1},{1,0},{2,3},{3,2},{4,5},{5,4},{6,7},{7,6},{8,9},{9,8},{10,11... | collective-permute-start | bytes 786440 | tf_op jit(solution)/shard_map/ppermute | solution.py:174
  9.8 1.9 %collective-permute-start = (bf16[16,8,1024]{2,1,0:T(8,128)(2,1)}, bf16[16,8,1024]{2,1,0:T(8,128)(2,1)S(1)}, u32[]{:S(2)}, u32[]{:S(2)}) collective-permute-start(bf16[16,8,1024]{2,1,0:T(8,128)(2,1)} %vectors.1), channel_id=1, source_target_pairs={{0,1},{1,0},{2,3},{3,2},{4,5},{5,4},{6,7},{7,6},{8,9},{9,8},{10,11... | collective-permute-start | bytes 786440 | tf_op jit(solution)/shard_map/ppermute | solution.py:174
  11.7 3.4 %collective-permute-start.2 = (f32[16]{0:T(128)}, f32[16]{0:T(128)S(1)}, u32[]{:S(2)}, u32[]{:S(2)}) collective-permute-start(f32[16]{0:T(128)} %energy.1), channel_id=1, source_target_pairs={{1,33},{33,65},{65,97},{97,1},{3,35},{35,67},{67,99},{99,3},{5,37}... | collective-permute-start | bytes 200 | tf_op jit(solution)/shard_map/ppermute | solution.py:177
  15.2 4.9 %collective-permute-done.2 = f32[16]{0:T(128)S(1)} collective-permute-done((f32[16]{0:T(128)}, f32[16]{0:T(128)S(1)}, u32[]{:S(2)}, u32[]{:S(2)}) %collective-permute-start.2) | collective-permute-done | bytes 96 | tf_op jit(solution)/shard_map/ppermute | solution.py:177
  20.1 4.8 %collective-permute-start.3 = (f32[16]{0:T(128)S(1)}, f32[16]{0:T(128)S(1)}, u32[]{:S(2)}, u32[]{:S(2)}) collective-permute-start(f32[16]{0:T(128)S(1)} %collective-permute-done.2), channel_id=1, source_target_pairs={{1,33},{33,65},{65,97},{97,1},{3,35},{35,67},{67,99},{99,3},{5,37}... | collective-permute-start | bytes 200 | tf_op jit(solution)/shard_map/ppermute | solution.py:177
  24.8 3.4 %collective-permute-done.3.refs_0_ = f32[16]{0:T(128)S(1)} collective-permute-done((f32[16]{0:T(128)S(1)}, f32[16]{0:T(128)S(1)}, u32[]{:S(2)}, u32[]{:S(2)}) %collective-permute-start.3) | collective-permute-done | bytes 96 | tf_op jit(solution)/shard_map/ppermute | solution.py:177
  28.2 0.0 collective-permute-done.1.other_amps
  28.2 0.0 collective-permute-done.other_vectors
  28.3 0.9 copy-done.1
  29.2 0.7 copy-done.2
  29.9 0.7 copy-done.3
  30.5 0.7 shard_map.73
  31.3 0.0 copy-start
  31.3 0.0 copy-start.5
  31.3 25.9 %all_to_all.25.arrived = bf16[16,20,8,256]{3,2,1,0:T(8,128)(2,1)S(1)} all-to-all(bf16[16,20,8,256]{3,2,1,0:T(8,128)(2,1)S(1)} %shard_map.73), channel_id=1, replica_groups=mesh['x'=4,'zh'=4,'zl'=4,'y'=4,'core'=2] {'zl','y'}, dimensions={0} | all-to-all | bytes 2621440 | tf_op jit(solution)/shard_map/all_to_all | solution.py:183
  57.2 0.9 shard_map.74
  58.1 11.4 %all_to_all.26.amp_tiles = bf16[16,2,8,256]{3,2,1,0:T(8,128)(2,1)S(1)} all-to-all(bf16[16,2,8,256]{3,2,1,0:T(8,128)(2,1)S(1)} %shard_map.74), channel_id=1, replica_groups=mesh['x'=4,'zh'=4,'zl'=4,'y'=4,'core'=2] {'zl','y'}, dimensions={0} | all-to-all | bytes 262144 | tf_op jit(solution)/shard_map/all_to_all | solution.py:185
  69.5 0.0 copy-done
  69.5 2.5 %shard_map.75 = bf16[4,256,1024]{2,1,0:T(8,128)(2,1)S(1)} custom-call(s32[32]{0:T(128)S(1)} %copy-done.5, bf16[16,20,8,256]{3,2,1,0:T(8,128)(2,1)S(1)} %all_to_all.25.arrived, bf16[16,2,8,256]{3,2,1,0:T(8,128)(2,1)S(1)} %all_to_all.26.amp_tiles, bf16[1024,1024]{1,0:T(8,128)(2,1)S(1)} %copy-done), custom_call_target="tpu_custom_call" | custom-call | tf_op jit(solution)/shard_map/pallas_call | solution.py:152
  72.0 19.2 %all_to_all.27.parts = bf16[4,256,1024]{2,1,0:T(8,128)(2,1)S(1)} all-to-all(bf16[4,256,1024]{2,1,0:T(8,128)(2,1)S(1)} %shard_map.75), channel_id=1, replica_groups=mesh['x'=4,'zh'=4,'zl'=4,'y'=4,'core'=2] {'x'}, dimensions={0} | all-to-all | bytes 4194304 | tf_op jit(solution)/shard_map/all_to_all | solution.py:190
  91.2 0.3 shard_map.76
  91.5 0.0 copy-start.4
  91.5 0.0 copy-start.6
  91.5 30.2 %all_to_all.28.parts = bf16[16,64,256]{2,1,0:T(8,128)(2,1)S(1)} all-to-all(bf16[16,64,256]{2,1,0:T(8,128)(2,1)S(1)} %shard_map.76), channel_id=1, replica_groups=mesh['x'=4,'zh'=4,'zl'=4,'y'=4,'core'=2] {'zh','y'}, dimensions={0} | all-to-all | bytes 1048576 | tf_op jit(solution)/shard_map/all_to_all | solution.py:192
  121.7 0.6 shard_map.77
  122.4 18.5 %all_to_all.29.arrived = bf16[16,64,256]{2,1,0:T(8,128)(2,1)S(1)} all-to-all(bf16[16,64,256]{2,1,0:T(8,128)(2,1)S(1)} %shard_map.77), channel_id=1, replica_groups=mesh['x'=4,'zh'=4,'zl'=4,'y'=4,'core'=2] {'zl','y'}, dimensions={0} | all-to-all | bytes 1048576 | tf_op jit(solution)/shard_map/all_to_all | solution.py:197
  140.8 0.6 shard_map.78
  141.4 1.9 %collective-permute-start.4 = (bf16[64,1024]{1,0:T(8,128)(2,1)S(1)}, bf16[64,1024]{1,0:T(8,128)(2,1)S(1)}, u32[]{:S(2)}, u32[]{:S(2)}) collective-permute-start(bf16[64,1024]{1,0:T(8,128)(2,1)S(1)} %get-tuple-element.8), channel_id=1, source_target_pairs={{0,1},{1,0},{2,3},{3,2},{4,5},{5,4},{6,7},{7,6},{8,9},{9,8},{10,11... | collective-permute-start | bytes 393224 | tf_op jit(solution)/shard_map/ppermute | solution.py:199
  143.3 1.0 shard_map.79.local
  144.4 0.3 collective-permute-done.4.other
  144.6 1.5 %shard_map.80 = f32[64,2,1024]{2,1,0:T(2,128)} custom-call(s32[33]{0:T(128)S(1)} %copy-done.2, bf16[64,1024]{1,0:T(8,128)(2,1)S(1)} %get-tuple-element.7.mine, bf16[64,1024]{1,0:T(8,128)(2,1)S(1)} %collective-permute-done.4.other, f32[64,2048]{1,0:T(8,128)S(1)} %shard_map.79.local), custom_call_target="tpu_custom_call" | custom-call | tf_op jit(solution)/shard_map/pallas_call | solution.py:152
  (6 shorter events, 0.0 us)
Async XLA Ops:
  1.0 27.2 %collective-permute-start.1 = (bf16[64,2048]{1,0:T(8,128)(2,1)S(1)}, bf16[64,2048]{1,0:T(8,128)(2,1)S(1)}, u32[]{:S(2)}, u32[]{:S(2)}) collective-permute-start(bf16[64,2048]{1,0:T(8,128)(2,1)S(1)} %bitcast.3), channel_id=1, source_target_pairs={{0,1},{1,0},{2,3},{3,2},{4,5},{5,4},{6,7},{7,6},{8,9},{9,8},{10,11... | collective-permute-start | bytes 786440 | tf_op jit(solution)/shard_map/ppermute | solution.py:174
  9.8 18.4 %collective-permute-start = (bf16[16,8,1024]{2,1,0:T(8,128)(2,1)}, bf16[16,8,1024]{2,1,0:T(8,128)(2,1)S(1)}, u32[]{:S(2)}, u32[]{:S(2)}) collective-permute-start(bf16[16,8,1024]{2,1,0:T(8,128)(2,1)} %vectors.1), channel_id=1, source_target_pairs={{0,1},{1,0},{2,3},{3,2},{4,5},{5,4},{6,7},{7,6},{8,9},{9,8},{10,11... | collective-permute-start | bytes 786440 | tf_op jit(solution)/shard_map/ppermute | solution.py:174
  11.7 8.3 %collective-permute-start.2 = (f32[16]{0:T(128)}, f32[16]{0:T(128)S(1)}, u32[]{:S(2)}, u32[]{:S(2)}) collective-permute-start(f32[16]{0:T(128)} %energy.1), channel_id=1, source_target_pairs={{1,33},{33,65},{65,97},{97,1},{3,35},{35,67},{67,99},{99,3},{5,37}... | collective-permute-start | bytes 200 | tf_op jit(solution)/shard_map/ppermute | solution.py:177
  20.1 8.2 %collective-permute-start.3 = (f32[16]{0:T(128)S(1)}, f32[16]{0:T(128)S(1)}, u32[]{:S(2)}, u32[]{:S(2)}) collective-permute-start(f32[16]{0:T(128)S(1)} %collective-permute-done.2), channel_id=1, source_target_pairs={{1,33},{33,65},{65,97},{97,1},{3,35},{35,67},{67,99},{99,3},{5,37}... | collective-permute-start | bytes 200 | tf_op jit(solution)/shard_map/ppermute | solution.py:177
  28.2 1.0 copy-start.1
  29.2 0.7 copy-start.2
  29.9 0.7 copy-start.3
  31.3 38.2 %copy-start = (bf16[1024,1024]{1,0:T(8,128)(2,1)S(1)}, bf16[1024,1024]{1,0:T(8,128)(2,1)}, u32[]{:S(2)}) copy-start(bf16[1024,1024]{1,0:T(8,128)(2,1)} %fock.3) | copy-start | bytes 6291460
  31.3 38.2 %copy-start.5 = (s32[32]{0:T(128)S(1)}, s32[32]{0:T(128)}, u32[]{:S(2)}) copy-start(s32[32]{0:T(128)} %case.1) | copy-start | bytes 388
  91.5 51.9 %copy-start.4 = (s32[32,2]{0,1:T(2,128)S(1)}, s32[32,2]{0,1:T(2,128)}, u32[]{:S(2)}) copy-start(s32[32,2]{0,1:T(2,128)} %param.11) | copy-start | bytes 772
  91.5 51.9 %copy-start.6 = (f32[16]{0:T(128)S(1)}, f32[16]{0:T(128)}, u32[]{:S(2)}) copy-start(f32[16]{0:T(128)} %energy.1) | copy-start | bytes 196
  141.4 3.2 %collective-permute-start.4 = (bf16[64,1024]{1,0:T(8,128)(2,1)S(1)}, bf16[64,1024]{1,0:T(8,128)(2,1)S(1)}, u32[]{:S(2)}, u32[]{:S(2)}) collective-permute-start(bf16[64,1024]{1,0:T(8,128)(2,1)S(1)} %get-tuple-element.8), channel_id=1, source_target_pairs={{0,1},{1,0},{2,3},{3,2},{4,5},{5,4},{6,7},{7,6},{8,9},{9,8},{10,11... | collective-permute-start | bytes 393224 | tf_op jit(solution)/shard_map/ppermute | solution.py:199

commit v4 on v3

v4 whole, which is shorter than its diff:
```python
import jax
import jax.numpy as jnp
from jax import lax
from jax.experimental import pallas as pl
from jax.experimental.pallas import tpu as pltpu
from jax.sharding import Mesh, PartitionSpec as P

CHOL = ("x", "zh")
PAIR = ("zl", "y", "core")
VMEM = pl.BlockSpec(memory_space=pltpu.VMEM)
ANY = pl.BlockSpec(memory_space=pl.ANY)
TURNS = ("zh",)
AFTER = False
SMEM = pl.BlockSpec(memory_space=pltpu.SMEM)
LIMIT = pltpu.CompilerParams(vmem_limit_bytes=32 * 1024 * 1024)


def pair_at(zl, y, core):
    return y * 8 + zl * 2 + core


def owner_index():
    return lax.axis_index("zl") * 8 + lax.axis_index("y") * 2 + lax.axis_index("core")


def first_at(offsets, chip, core):
    first = offsets[chip * 2]
    return first + ((first ^ core) & 1)


def pack_kernel(vectors, amps, out):
    out[0] = vectors[...]
    wide = amps[...].astype(jnp.float32)
    for group in range(8):
        for slot in range(2):
            tile = wide[group * 8 : (group + 1) * 8, slot * 1024 : (slot + 1) * 1024]
            out[1, group * 2 + slot] = tile.astype(jnp.bfloat16)


def choose_vectors(orbitals, own, other, out):
    core = lax.axis_index("core")
    for dest in range(16):
        pair = pair_at(dest // 4, dest % 4, core)
        for side in range(2):
            for which, source in enumerate((own, other)):
                chosen = source[0, orbitals[side, pair]]
                for part in range(4):
                    out[dest, side * 8 + which * 4 + part] = chosen[:, part * 256 : (part + 1) * 256]


def hold_amps(own, other, held):
    core = lax.axis_index("core")
    held[core] = own[1]
    held[1 - core] = other[1]


def place_of(offsets, chip, pair):
    start, middle = offsets[chip * 2], offsets[chip * 2 + 1]
    late = pair >= middle
    return late.astype(jnp.int32), jnp.clip(jnp.where(late, pair - middle, pair - start), 0, 1)


def prepare_kernel(offsets, orbitals, own, other, out, held):
    choose_vectors(orbitals, own, other, out)
    hold_amps(own, other, held)
    chip = lax.axis_index("zl") * 4 + lax.axis_index("y")
    first = first_at(offsets, chip, lax.axis_index("core"))
    for kind in range(4):
        pair = first + 2 * jnp.minimum((kind - (first >> 1)) & 3, 1)
        late, slot = place_of(offsets, chip, pair)
        for y in range(4):
            for group in range(2):
                tile = held[late, (y * 2 + group) * 2 + slot]
                for part in range(4):
                    out[kind * 4 + y, 16 + group * 4 + part] = tile[:, part * 256 : (part + 1) * 256]


def tile_kernel(offsets, orbitals, own, other, out, tiles, held):
    choose_vectors(orbitals, own, other, out)
    hold_amps(own, other, held)
    chip = lax.axis_index("zl") * 4 + lax.axis_index("y")
    first = first_at(offsets, chip, lax.axis_index("core"))
    for j in range(2):
        late, slot = place_of(offsets, chip, first + 2 * j)
        for dest in range(16):
            tile = held[late, dest // 2 * 2 + slot]
            for part in range(2):
                start = dest % 2 * 512 + part * 256
                tiles[dest, j * 2 + part] = tile[:, start : start + 256]


def fill_kernel(offsets, chosen, tiles, token, local, out):
    out[:, :16] = chosen[...]
    core = lax.axis_index("core")
    for chip in range(16):
        for j in range(2):
            pair = first_at(offsets, chip, core) + 2 * j

            @pl.when(pair < offsets[chip * 2 + 2])
            def _():
                dest = ((pair & 7) >> 1) * 4 + (pair >> 3)
                for part in range(2):
                    out[dest, 16 + part] = tiles[chip, j * 2 + part]


def local_kernel(offsets, orbitals, energy, own, fock, after, out):
    owner = owner_index()
    tiles = [own[1, group * 2 + slot].astype(jnp.float32) for slot in range(2) for group in range(8)]
    both = jnp.concatenate(tiles, axis=0)
    term = jnp.dot(both.astype(jnp.bfloat16), fock[...], preferred_element_type=jnp.float32)
    for slot in range(2):
        pair = jnp.minimum(offsets[owner] + slot, 31)
        shift = energy[orbitals[0, pair]] + energy[orbitals[1, pair]]
        here = slice(slot * 64, (slot + 1) * 64)
        out[:, slot * 1024 : (slot + 1) * 1024] = term[here] - shift * both[here]


def chip_of(offsets, pair):
    chip = jnp.int32(0)
    for end in range(2, 32, 2):
        chip += (offsets[end] <= pair).astype(jnp.int32)
    return chip


def couple_kernel(offsets, case, arrived, out, rows, cols):
    zl, y, core = (lax.axis_index(name) for name in PAIR)
    swap = jnp.where(case[pair_at(zl, y, core)] == 0, 0.5, -0.5).astype(jnp.float32)
    for part in range(4):
        here = slice(part * 256, (part + 1) * 256)
        for which in range(2):
            left = arrived[:, which * 4 + part].astype(jnp.float32).reshape(128, 256)
            right = arrived[:, 8 + which * 4 + part].astype(jnp.float32).reshape(128, 256)
            start = which * 128
            rows[start : start + 128, here] = left
            rows[start + 256 : start + 384, here] = right
            cols[start : start + 128, here] = (0.5 * right).astype(jnp.bfloat16)
            cols[start + 256 : start + 384, here] = (swap * left).astype(jnp.bfloat16)
    for row in range(4):
        block = rows[:, row * 256 : (row + 1) * 256].T.astype(jnp.bfloat16)
        for part in range(4):
            there = cols[:, part * 256 : (part + 1) * 256]
            product = jnp.dot(block, there, preferred_element_type=jnp.float32)
            out[row * 4 + part, 0:256] = product.astype(jnp.bfloat16)
    for source in range(4):
        pair = pair_at(zl, source, core)
        chip = chip_of(offsets, pair)
        for part in range(4):
            tiles = [arrived[chip, 16 + group * 4 + part].astype(jnp.float32) for group in range(2)]
            tile = jnp.concatenate(tiles, axis=0).astype(jnp.bfloat16)
            for row in range(4):
                out[row * 4 + part, 256 + source * 16 : 272 + source * 16] = tile


def finish_kernel(parts, fock, out, cols):
    x, zh = lax.axis_index("x"), lax.axis_index("zh")
    cols[...] = jnp.zeros((512, 1024), jnp.bfloat16)
    for band in range(4):
        for quarter in range(4):
            start = pl.multiple_of(band * 128 + (zh & 1) * 64 + quarter * 16, 16)
            for y in range(4):
                tile = parts[band * 4 + quarter, 256 + y * 16 : 272 + y * 16]
                cols[pl.ds(start, 16), y * 256 : (y + 1) * 256] = tile
    top = pl.multiple_of(x * 256, 256)
    lanes = [pl.multiple_of((band * 2 + (zh >> 1)) * 128, 128) for band in range(4)]
    rows = jnp.concatenate([fock[pl.ds(top, 256), pl.ds(lane, 128)] for lane in lanes], axis=1)
    for y in range(4):
        total = jnp.dot(rows, cols[:, y * 256 : (y + 1) * 256], preferred_element_type=jnp.float32)
        for band in range(4):
            total += parts[band * 4 + y, 0:256].astype(jnp.float32)
        for dest in range(4):
            out[dest, y] = total[dest * 64 : (dest + 1) * 64].astype(jnp.bfloat16)


def late_couple_kernel(offsets, case, arrived, fock, out, rows, cols):
    zl = lax.axis_index("zl")
    pair = pair_at(zl, lax.axis_index("y"), lax.axis_index("core"))
    run = lax.axis_index("zh") + (zl >= 2).astype(jnp.int32)
    x, zh = lax.axis_index("x"), (run + 3 + (chip_of(offsets, pair) < 8).astype(jnp.int32)) & 3
    swap = jnp.where(case[pair] == 0, 0.5, -0.5).astype(jnp.float32)
    cols[512:640] = jnp.zeros((128, 1024), jnp.bfloat16)
    top = pl.multiple_of(512 + (zh & 1) * 64, 64)
    for part in range(4):
        here = slice(part * 256, (part + 1) * 256)
        for which in range(2):
            left = arrived[:, which * 4 + part].astype(jnp.float32).reshape(128, 256)
            right = arrived[:, 8 + which * 4 + part].astype(jnp.float32).reshape(128, 256)
            start = which * 128
            rows[start : start + 128, here] = left
            rows[start + 256 : start + 384, here] = right
            cols[start : start + 128, here] = (0.5 * right).astype(jnp.bfloat16)
            cols[start + 256 : start + 384, here] = (swap * left).astype(jnp.bfloat16)
        tiles = [arrived[group * 2 + part // 2, 16 + part % 2].astype(jnp.float32) for group in range(8)]
        cols[pl.ds(top, 64), here] = jnp.concatenate(tiles, axis=0).astype(jnp.bfloat16)
    lanes = pl.multiple_of((x * 2 + (zh >> 1)) * 128, 128)
    for row in range(4):
        here = slice(row * 256, (row + 1) * 256)
        block = jnp.concatenate([rows[:, here].T.astype(jnp.bfloat16), fock[here, pl.ds(lanes, 128)]], axis=1)
        product = jnp.dot(block, cols[...], preferred_element_type=jnp.float32)
        out[row] = product.astype(jnp.bfloat16)


def late_finish_kernel(parts, out):
    for y in range(4):
        here = slice(y * 256, (y + 1) * 256)
        total = parts[0, :, here].astype(jnp.float32)
        for x in range(1, 4):
            total += parts[x, :, here].astype(jnp.float32)
        for zh in range(4):
            out[zh * 4 + y] = total[zh * 64 : (zh + 1) * 64].astype(jnp.bfloat16)


def route_kernel(offsets, parts, out, total):
    for y in range(4):
        sums = parts[0, y].astype(jnp.float32)
        for zh in range(1, 4):
            sums += parts[zh, y].astype(jnp.float32)
        total[y] = sums.astype(jnp.bfloat16)
    member = lax.axis_index("zl") * 2 + lax.axis_index("core")
    for chip in range(16):
        end = offsets[chip * 2 + 2]
        which = jnp.maximum(((end + 7 - member) >> 3) - 1, 0)
        out[chip] = total[which]


def pick_kernel(offsets, arrived, mine, theirs):
    core, owner = lax.axis_index("core"), owner_index()
    for who, out in ((owner, mine), (owner ^ 1, theirs)):
        first = offsets[who]
        pair = first + ((first ^ core) & 1)
        for y in range(4):
            out[:, y * 256 : (y + 1) * 256] = arrived[((pair & 7) >> 1) * 4 + y]


def write_kernel(offsets, mine, other, local, out):
    owner = owner_index()
    first = offsets[owner]
    count = offsets[owner + 1] - first
    for slot in range(2):
        own = ((first + slot) & 1) == lax.axis_index("core")
        coupled = jnp.where(own, mine[...].astype(jnp.float32), other[...].astype(jnp.float32))
        result = coupled + local[:, slot * 1024 : (slot + 1) * 1024]
        out[:, slot, :] = jnp.where(slot < count, result, 0.0)


def call(kernel, out, in_specs, *args, scratch=()):
    return pl.pallas_call(
        kernel,
        out_shape=out,
        in_specs=in_specs,
        out_specs=jax.tree.map(lambda _: VMEM, out),
        scratch_shapes=list(scratch),
        compiler_params=LIMIT,
    )(*args)


def half(*shape):
    return jax.ShapeDtypeStruct(shape, jnp.bfloat16)


def single(*shape):
    return jax.ShapeDtypeStruct(shape, jnp.float32)


def shifted(block):
    runs = [[((run + (zl < 2)) % 4 * 4 + zl) * 4 + y for zl in range(4) for y in range(4)] for run in range(4)]
    return lax.all_to_all(block, ("zh", "zl", "y"), 0, 0, axis_index_groups=runs, tiled=True)


def local_part(own, fock, orbital_energy, orbitals, owner_offsets, after):
    return call(
        local_kernel, single(64, 2048), [SMEM] * 3 + [VMEM] * 2 + [ANY],
        owner_offsets, orbitals, orbital_energy, own, fock, after,
    )


def deliver(parts, owner_offsets):
    routed = call(
        route_kernel, half(16, 64, 256), [SMEM, VMEM], owner_offsets, parts,
        scratch=[pltpu.VMEM((4, 64, 256), jnp.bfloat16)],
    )
    arrived = lax.all_to_all(routed, ("zl", "y"), 0, 0, tiled=True)
    return call(pick_kernel, [half(64, 1024), half(64, 1024)], [SMEM, VMEM], owner_offsets, arrived)


def early_chain(own, other, fock, orbital_energy, orbitals, pair_case, owner_offsets):
    chosen = call(
        prepare_kernel, half(16, 24, 8, 256), [SMEM] * 2 + [VMEM] * 2, owner_offsets, orbitals, own, other,
        scratch=[pltpu.VMEM((2, 16, 8, 1024), jnp.bfloat16)],
    )
    arrived = lax.all_to_all(chosen, ("zl", "y"), 0, 0, tiled=True)
    partial = call(
        couple_kernel, half(16, 320, 256), [SMEM, SMEM, VMEM], owner_offsets, pair_case, arrived,
        scratch=[pltpu.VMEM((512, 1024), jnp.float32), pltpu.VMEM((512, 1024), jnp.bfloat16)],
    )
    parts = lax.all_to_all(partial, ("x", "y"), 0, 0, tiled=True)
    parts = call(
        finish_kernel, half(4, 4, 64, 256), [VMEM, VMEM], parts, fock, scratch=[pltpu.VMEM((512, 1024), jnp.bfloat16)]
    )
    parts = lax.all_to_all(parts, "zh", 0, 0, tiled=True)
    mine, theirs = deliver(parts, owner_offsets)
    local = local_part(own, fock, orbital_energy, orbitals, owner_offsets, mine)
    return mine, theirs, local


def late_chain(own, other, fock, orbital_energy, orbitals, pair_case, owner_offsets):
    chosen, tiles = call(
        tile_kernel, [half(16, 16, 8, 256), half(16, 4, 8, 256)], [SMEM] * 2 + [VMEM] * 2,
        owner_offsets, orbitals, own, other, scratch=[pltpu.VMEM((2, 16, 8, 1024), jnp.bfloat16)],
    )
    tiles = shifted(tiles)
    token = tiles[0, 0] if AFTER else other[0, 0, :, :128]
    for axis in TURNS:
        token = lax.ppermute(token, (axis, "core"), [(i * 2 + 1, (i + 1) % 4 * 2 + 1) for i in range(4)])
    local = local_part(own, fock, orbital_energy, orbitals, owner_offsets, tiles)
    chosen = call(
        fill_kernel, half(16, 18, 8, 256), [SMEM] + [VMEM] * 2 + [ANY] * 2, owner_offsets, chosen, tiles, token, local
    )
    arrived = shifted(chosen)
    partial = call(
        late_couple_kernel, half(4, 256, 1024), [SMEM, SMEM, VMEM, VMEM], owner_offsets, pair_case, arrived, fock,
        scratch=[pltpu.VMEM((512, 1024), jnp.float32), pltpu.VMEM((640, 1024), jnp.bfloat16)],
    )
    parts = lax.all_to_all(partial, "x", 0, 0, tiled=True)
    parts = call(late_finish_kernel, half(16, 64, 256), [VMEM], parts)
    parts = lax.all_to_all(parts, ("zh", "y"), 0, 0, tiled=True).reshape(4, 4, 64, 256)
    mine, theirs = deliver(parts, owner_offsets)
    return mine, theirs, local


def body(chol_vectors, amplitudes, fock, orbital_energy, pair_orbitals, pair_case, owner_offsets):
    flat = amplitudes.reshape(64, 2048)
    orbitals = pair_orbitals.T

    own = call(pack_kernel, half(2, 16, 8, 1024), [VMEM] * 2, chol_vectors, flat)
    other = lax.ppermute(own, "core", [(0, 1), (1, 0)])
    mine, theirs, local = lax.cond(
        lax.axis_index("core") == 0, early_chain, late_chain,
        own, other, fock, orbital_energy, orbitals, pair_case, owner_offsets,
    )
    other = lax.ppermute(theirs, "core", [(0, 1), (1, 0)])
    return call(write_kernel, single(64, 2, 1024), [SMEM] + [VMEM] * 3, owner_offsets, mine, other, local)


def solution(mesh):
    fine = Mesh(mesh.devices.reshape(4, 4, 4, 4, 2), ("x", "zh", "zl", "y", "core"))
    in_specs = (P(None, CHOL + PAIR, None), P(CHOL, PAIR, None), P(), P(), P(), P(), P())
    return jax.shard_map(body, mesh=fine, in_specs=in_specs, out_specs=P(CHOL, PAIR, None), check_vma=False)
```

time: 147 us -> 138 us (0.939)
  blocking collectives: 105 us -> 90.2 us
  waiting for transfers between devices: 8.56 us -> 13.4 us
  Pallas kernels: 8.08 us -> 11.1 us
    all_to_all x5 -> x4, blocking collectives: 105 us -> 90.2 us  [the longest x1 25.6 us: shifted(): lax.all_to_all(block, ('zh', 'zl', 'y'), 0, 0, axis_index_groups=runs, ti...]
    all_to_all x0 -> x1, waiting for transfers between devices: none -> 10.6 us  [shifted(): lax.all_to_all(block, ('zh', 'zl', 'y'), 0, 0, axis_index_groups=runs, ti...]
    all_to_all x0 -> x1, starting transfers between devices: none -> 8.43 us  [shifted(): lax.all_to_all(block, ('zh', 'zl', 'y'), 0, 0, axis_index_groups=runs, ti...]
    ppermute x4 -> x2, starting transfers between devices: 18.9 us -> 10.7 us  [the longest x1 8.79 us: body(): other = lax.ppermute(own, 'core', [(0, 1), (1, 0)])]
    ppermute x4 -> x2, waiting for transfers between devices: 8.29 us -> 1.51 us  [the longest x1 1.51 us: body(): other = lax.ppermute(own, 'core', [(0, 1), (1, 0)])]
    pallas_call x8 -> x9, Pallas kernels: 8.08 us -> 11.1 us  [call(): pl.pallas_call(kernel, out_shape=out, in_specs=in_specs, out_specs=jax.tr...]
    unnamed x15 -> x3, local copies, waits for them, and re-layouts: 3.31 us -> 1.94 us
  transfers between devices with their start and end apart: 5 -> 4, of which waited for: 3 -> 3; matrix products, arithmetic and copies ran while one was open for 0% -> 0% of each run, Pallas kernels for 1% -> 1%
where the time goes in v4:
time: 138 us
  blocking collectives  90.2 us (65%)
  starting transfers between devices  21 us (15%)
  waiting for transfers between devices  13.4 us (10%)
  Pallas kernels  11.1 us (8%)
  local copies, waits for them, and re-layouts  1.96 us (1%)
    all_to_all x1, blocking collectives, shifted(): lax.all_to_all(block, ('zh', 'zl', 'y'), 0, 0, axis_index_groups=runs, ti...  25.6 us
    all_to_all x1, blocking collectives, late_chain(): lax.all_to_all(parts, ('zh', 'y'), 0, 0, tiled=True).reshape(4, 4, 64, 256)  25 us
    all_to_all x1, blocking collectives, deliver(): arrived = lax.all_to_all(routed, ('zl', 'y'), 0, 0, tiled=True)  20.2 us
    all_to_all x1, blocking collectives, late_chain(): parts = lax.all_to_all(partial, 'x', 0, 0, tiled=True)  19.3 us
    pallas_call x9, Pallas kernels, call(): pl.pallas_call(kernel, out_shape=out, in_specs=in_specs, out_specs=jax.tr...  11.1 us
    all_to_all x1, waiting for transfers between devices, shifted(): lax.all_to_all(block, ('zh', 'zl', 'y'), 0, 0, axis_index_groups=runs, ti...  10.6 us
    ppermute x1, starting transfers between devices, body(): other = lax.ppermute(own, 'core', [(0, 1), (1, 0)])  8.79 us
    all_to_all x1, starting transfers between devices, shifted(): lax.all_to_all(block, ('zh', 'zl', 'y'), 0, 0, axis_index_groups=runs, ti...  8.43 us
  transfers between devices with their start and end apart: 4, of which 3 were waited for; matrix products, arithmetic and copies ran while one was open for 0% of the time, Pallas kernels for 1%

profile of v4, /device:TPU:1, one launch (start us, length us, event | category | flops | bytes accessed | tf_op | source)
XLA Modules:
  0.0 137.8 jit_solution(12491118675815110391)
XLA Ops:
  0.0 1.0 copy.8
  1.0 0.0 copy-start
  1.0 0.9 copy-done
  2.0 8.8 %collective-permute-start.1 = (bf16[2,16,8,1024]{3,2,1,0:T(8,128)(2,1)S(1)}, bf16[2,16,8,1024]{3,2,1,0:T(8,128)(2,1)S(1)}, u32[]{:S(2)}, u32[]{:S(2)}) collective-permute-start(bf16[2,16,8,1024]{3,2,1,0:T(8,128)(2,1)S(1)} %shard_map.73), channel_id=1, source_target_pairs={{0,1},{1,0},{2,3},{3,2},{4,5},{5,4},{6,7},{7,6},{8,9},{9,8},{10,11... | collective-permute-start | bytes 1572872 | tf_op jit(solution)/shard_map/ppermute | solution.py:335
  10.8 1.5 %collective-permute-done.1 = bf16[2,16,8,1024]{3,2,1,0:T(8,128)(2,1)S(1)} collective-permute-done((bf16[2,16,8,1024]{3,2,1,0:T(8,128)(2,1)S(1)}, bf16[2,16,8,1024]{3,2,1,0:T(8,128)(2,1)S(1)}, u32[]{:S(2)}, u32[]{:S(2)}) %collective-permute-start.1) | collective-permute-done | bytes 524320 | tf_op jit(solution)/shard_map/ppermute | solution.py:335
  12.3 120.3 %conditional.1 = (bf16[64,1024]{1,0:T(8,128)(2,1)}, bf16[64,1024]{1,0:T(8,128)(2,1)S(1)}, f32[64,2048]{1,0:T(8,128)S(1)}) conditional(s32[]{:T(128)} %convert_element_type.3, (s32[33]{0:T(128)}, s32[2,32]{1,0:T(2,128)}, bf16[2,16,8,1024]{3,2,1,0:T(8,128)(2,1)S(1)}, bf16[2,16,8,1024]{3,2,1,0:T(8,128)(2,1)S(1)}, f32[16]{0:T(128)}, ...), branch_computations={%region_0.0_spmd, %region_1.0_spmd} | conditional | bytes 23071212 | solution.py:336
  12.3 1.6 %branch_0_fun.7 = (bf16[16,16,8,256]{3,2,1,0:T(8,128)(2,1)S(1)}, bf16[16,4,8,256]{3,2,1,0:T(8,128)(2,1)}) custom-call(s32[33]{0:T(128)} %get-tuple-element.33.offsets, s32[2,32]{1,0:T(2,128)} %get-tuple-element.35.orbitals, bf16[2,16,8,1024]{3,2,1,0:T(8,128)(2,1)S(1)} %get-tuple-element.36.own, bf16[2,16,8,1024]{3,2,1,0:T(8,128)(2,1)S(1)} %get-tuple-element.37.other), custom_call_target="tpu_custom_call" | custom-call | tf_op jit(solution)/shard_map/cond/branch_0_fun/pallas_call | solution.py:246
  13.9 0.0 copy-start.5
  13.9 8.4 %all-to-all-start.4 = ((bf16[16,4,8,256]{3,2,1,0:T(8,128)(2,1)}), bf16[16,4,8,256]{3,2,1,0:T(8,128)(2,1)S(1)}, u32[]{:S(2)}, u32[]{:S(2)}) async-start(bf16[16,4,8,256]{3,2,1,0:T(8,128)(2,1)} %get-tuple-element.39), calls=%async_computation.4 | async-start | bytes 524288 | tf_op jit(solution)/shard_map/cond/branch_0_fun/all_to_all | solution.py:266
  22.3 1.9 %collective-permute-start = (bf16[8,128]{1,0:T(8,128)(2,1)S(1)}, bf16[8,128]{1,0:T(8,128)(2,1)S(1)}, u32[]{:S(2)}, u32[]{:S(2)}) collective-permute-start(bf16[8,128]{1,0:T(8,128)(2,1)S(1)} %slice_bitcast_fusion), channel_id=1, source_target_pairs={{1,33},{33,65},{65,97},{97,1},{3,35},{35,67},{67,99},{99,3},{5,37}... | collective-permute-start | bytes 6152 | tf_op jit(solution)/shard_map/cond/branch_0_fun/ppermute | solution.py:313
  24.3 10.6 %all-to-all-done.4.after.tiles = bf16[16,4,8,256]{3,2,1,0:T(8,128)(2,1)S(1)} async-done(((bf16[16,4,8,256]{3,2,1,0:T(8,128)(2,1)}), bf16[16,4,8,256]{3,2,1,0:T(8,128)(2,1)S(1)}, u32[]{:S(2)}, u32[]{:S(2)}) %all-to-all-start.4) | async-done | bytes 262176 | tf_op jit(solution)/shard_map/cond/branch_0_fun/all_to_all | solution.py:266
  34.8 2.1 %branch_0_fun.8.local = f32[64,2048]{1,0:T(8,128)S(1)} custom-call(s32[33]{0:T(128)} %get-tuple-element.33.offsets, s32[2,32]{1,0:T(2,128)} %get-tuple-element.35.orbitals, f32[16]{0:T(128)} %get-tuple-element.40.energy, bf16[2,16,8,1024]{3,2,1,0:T(8,128)(2,1)S(1)} %get-tuple-element.36.own, bf16[1024,1024]{1,0:T(8,128)(2,1)} %get-tuple-element.41.fock, ...), custom_call_target="tpu_custom_call" | custom-call | tf_op jit(solution)/shard_map/cond/branch_0_fun/pallas_call | solution.py:246
  36.9 0.0 collective-permute-done.token
  36.9 0.0 copy-done.5
  36.9 0.0 copy-start.1
  36.9 0.0 copy-start.8
  36.9 0.9 branch_0_fun.9
  37.9 25.6 %all_to_all.36.arrived = bf16[16,18,8,256]{3,2,1,0:T(8,128)(2,1)S(1)} all-to-all(bf16[16,18,8,256]{3,2,1,0:T(8,128)(2,1)S(1)} %branch_0_fun.9), channel_id=1, replica_groups={{32,34,36,38,40,42,44,46,16,18,20,22,24,26,28,30},{64,66,68,70,72,74,76..., dimensions={0} | all-to-all | bytes 2359296 | tf_op jit(solution)/shard_map/cond/branch_0_fun/all_to_all | solution.py:266
  63.5 0.0 copy-done.1
  63.5 0.0 copy-done.8
  63.5 2.5 %branch_0_fun.10 = bf16[4,256,1024]{2,1,0:T(8,128)(2,1)S(1)} custom-call(s32[33]{0:T(128)S(1)} %copy-done.5, s32[32]{0:T(128)S(1)} %copy-done.8, bf16[16,18,8,256]{3,2,1,0:T(8,128)(2,1)S(1)} %all_to_all.36.arrived, bf16[1024,1024]{1,0:T(8,128)(2,1)S(1)} %copy-done.1), custom_call_target="tpu_custom_call" | custom-call | tf_op jit(solution)/shard_map/cond/branch_0_fun/pallas_call | solution.py:246
  66.0 19.3 %all_to_all.37.parts = bf16[4,256,1024]{2,1,0:T(8,128)(2,1)S(1)} all-to-all(bf16[4,256,1024]{2,1,0:T(8,128)(2,1)S(1)} %branch_0_fun.10), channel_id=1, replica_groups=mesh['x'=4,'zh'=4,'zl'=4,'y'=4,'core'=2] {'x'}, dimensions={0} | all-to-all | bytes 4194304 | tf_op jit(solution)/shard_map/cond/branch_0_fun/all_to_all | solution.py:323
  85.3 0.3 branch_0_fun.11
  85.5 25.0 %all_to_all.38 = bf16[16,64,256]{2,1,0:T(8,128)(2,1)S(1)} all-to-all(bf16[16,64,256]{2,1,0:T(8,128)(2,1)S(1)} %branch_0_fun.11), channel_id=1, replica_groups=mesh['x'=4,'zh'=4,'zl'=4,'y'=4,'core'=2] {'zh','y'}, dimensions={0} | all-to-all | bytes 1048576 | tf_op jit(solution)/shard_map/cond/branch_0_fun/all_to_all | solution.py:325
  110.6 0.6 branch_0_fun.12
  111.2 20.2 %all_to_all.39.arrived = bf16[16,64,256]{2,1,0:T(8,128)(2,1)S(1)} all-to-all(bf16[16,64,256]{2,1,0:T(8,128)(2,1)S(1)} %branch_0_fun.12), channel_id=1, replica_groups=mesh['x'=4,'zh'=4,'zl'=4,'y'=4,'core'=2] {'zl','y'}, dimensions={0} | all-to-all | bytes 1048576 | tf_op jit(solution)/shard_map/cond/branch_0_fun/all_to_all | solution.py:281
  131.4 1.2 branch_0_fun.13
  132.6 1.9 %collective-permute-start.2 = (bf16[64,1024]{1,0:T(8,128)(2,1)S(1)}, bf16[64,1024]{1,0:T(8,128)(2,1)S(1)}, u32[]{:S(2)}, u32[]{:S(2)}) collective-permute-start(bf16[64,1024]{1,0:T(8,128)(2,1)S(1)} %get-tuple-element.57), channel_id=1, source_target_pairs={{0,1},{1,0},{2,3},{3,2},{4,5},{5,4},{6,7},{7,6},{8,9},{9,8},{10,11... | collective-permute-start | bytes 393224 | tf_op jit(solution)/shard_map/ppermute | solution.py:340
  134.6 1.3 collective-permute-done.2.other
  135.9 1.9 %shard_map.74 = f32[64,2,1024]{2,1,0:T(2,128)} custom-call(s32[33]{0:T(128)} %offsets.1, bf16[64,1024]{1,0:T(8,128)(2,1)} %get-tuple-element.56.mine, bf16[64,1024]{1,0:T(8,128)(2,1)S(1)} %collective-permute-done.2.other, f32[64,2048]{1,0:T(8,128)S(1)} %get-tuple-element.58.local), custom_call_target="tpu_custom_call" | custom-call | tf_op jit(solution)/shard_map/pallas_call | solution.py:246
  (2 shorter events, 0.0 us)
Async XLA Ops:
  1.0 1.0 copy-start
  2.0 10.3 %collective-permute-start.1 = (bf16[2,16,8,1024]{3,2,1,0:T(8,128)(2,1)S(1)}, bf16[2,16,8,1024]{3,2,1,0:T(8,128)(2,1)S(1)}, u32[]{:S(2)}, u32[]{:S(2)}) collective-permute-start(bf16[2,16,8,1024]{3,2,1,0:T(8,128)(2,1)S(1)} %shard_map.73), channel_id=1, source_target_pairs={{0,1},{1,0},{2,3},{3,2},{4,5},{5,4},{6,7},{7,6},{8,9},{9,8},{10,11... | collective-permute-start | bytes 1572872 | tf_op jit(solution)/shard_map/ppermute | solution.py:335
  13.9 23.0 %copy-start.5 = (s32[33]{0:T(128)S(1)}, s32[33]{0:T(128)}, u32[]{:S(2)}) copy-start(s32[33]{0:T(128)} %get-tuple-element.33.offsets) | copy-start | bytes 400 | tf_op jit(solution)/shard_map/cond
  13.9 20.9 %all-to-all-start.4 = ((bf16[16,4,8,256]{3,2,1,0:T(8,128)(2,1)}), bf16[16,4,8,256]{3,2,1,0:T(8,128)(2,1)S(1)}, u32[]{:S(2)}, u32[]{:S(2)}) async-start(bf16[16,4,8,256]{3,2,1,0:T(8,128)(2,1)} %get-tuple-element.39), calls=%async_computation.4 | async-start | bytes 524288 | tf_op jit(solution)/shard_map/cond/branch_0_fun/all_to_all | solution.py:266
  22.3 14.6 %collective-permute-start = (bf16[8,128]{1,0:T(8,128)(2,1)S(1)}, bf16[8,128]{1,0:T(8,128)(2,1)S(1)}, u32[]{:S(2)}, u32[]{:S(2)}) collective-permute-start(bf16[8,128]{1,0:T(8,128)(2,1)S(1)} %slice_bitcast_fusion), channel_id=1, source_target_pairs={{1,33},{33,65},{65,97},{97,1},{3,35},{35,67},{67,99},{99,3},{5,37}... | collective-permute-start | bytes 6152 | tf_op jit(solution)/shard_map/cond/branch_0_fun/ppermute | solution.py:313
  36.9 26.6 %copy-start.1 = (bf16[1024,1024]{1,0:T(8,128)(2,1)S(1)}, bf16[1024,1024]{1,0:T(8,128)(2,1)}, u32[]{:S(2)}) copy-start(bf16[1024,1024]{1,0:T(8,128)(2,1)} %get-tuple-element.41.fock) | copy-start | bytes 6291460 | tf_op jit(solution)/shard_map/cond
  36.9 26.6 %copy-start.8 = (s32[32]{0:T(128)S(1)}, s32[32]{0:T(128)}, u32[]{:S(2)}) copy-start(s32[32]{0:T(128)} %get-tuple-element.34.case) | copy-start | bytes 388 | tf_op jit(solution)/shard_map/cond
  132.6 3.2 %collective-permute-start.2 = (bf16[64,1024]{1,0:T(8,128)(2,1)S(1)}, bf16[64,1024]{1,0:T(8,128)(2,1)S(1)}, u32[]{:S(2)}, u32[]{:S(2)}) collective-permute-start(bf16[64,1024]{1,0:T(8,128)(2,1)S(1)} %get-tuple-element.57), channel_id=1, source_target_pairs={{0,1},{1,0},{2,3},{3,2},{4,5},{5,4},{6,7},{7,6},{8,9},{9,8},{10,11... | collective-permute-start | bytes 393224 | tf_op jit(solution)/shard_map/ppermute | solution.py:340

commit v5 on v4

--- a/solution.py
+++ b/solution.py
@@ -10,7 +10,6 @@
 VMEM = pl.BlockSpec(memory_space=pltpu.VMEM)
 ANY = pl.BlockSpec(memory_space=pl.ANY)
 TURNS = ("zh",)
-AFTER = False
 SMEM = pl.BlockSpec(memory_space=pltpu.SMEM)
 LIMIT = pltpu.CompilerParams(vmem_limit_bytes=32 * 1024 * 1024)
 
@@ -297,9 +296,7 @@
         finish_kernel, half(4, 4, 64, 256), [VMEM, VMEM], parts, fock, scratch=[pltpu.VMEM((512, 1024), jnp.bfloat16)]
     )
     parts = lax.all_to_all(parts, "zh", 0, 0, tiled=True)
-    mine, theirs = deliver(parts, owner_offsets)
-    local = local_part(own, fock, orbital_energy, orbitals, owner_offsets, mine)
-    return mine, theirs, local
+    return parts, local_part(own, fock, orbital_energy, orbitals, owner_offsets, parts)
 
 
 def late_chain(own, other, fock, orbital_energy, orbitals, pair_case, owner_offsets):
@@ -308,7 +305,7 @@
         owner_offsets, orbitals, own, other, scratch=[pltpu.VMEM((2, 16, 8, 1024), jnp.bfloat16)],
     )
     tiles = shifted(tiles)
-    token = tiles[0, 0] if AFTER else other[0, 0, :, :128]
+    token = other[0, 0, :, :128]
     for axis in TURNS:
         token = lax.ppermute(token, (axis, "core"), [(i * 2 + 1, (i + 1) % 4 * 2 + 1) for i in range(4)])
     local = local_part(own, fock, orbital_energy, orbitals, owner_offsets, tiles)
@@ -323,8 +320,7 @@
     parts = lax.all_to_all(partial, "x", 0, 0, tiled=True)
     parts = call(late_finish_kernel, half(16, 64, 256), [VMEM], parts)
     parts = lax.all_to_all(parts, ("zh", "y"), 0, 0, tiled=True).reshape(4, 4, 64, 256)
-    mine, theirs = deliver(parts, owner_offsets)
-    return mine, theirs, local
+    return parts, local
 
 
 def body(chol_vectors, amplitudes, fock, orbital_energy, pair_orbitals, pair_case, owner_offsets):
@@ -333,10 +329,11 @@
 
     own = call(pack_kernel, half(2, 16, 8, 1024), [VMEM] * 2, chol_vectors, flat)
     other = lax.ppermute(own, "core", [(0, 1), (1, 0)])
-    mine, theirs, local = lax.cond(
+    parts, local = lax.cond(
         lax.axis_index("core") == 0, early_chain, late_chain,
         own, other, fock, orbital_energy, orbitals, pair_case, owner_offsets,
     )
+    mine, theirs = deliver(parts, owner_offsets)
     other = lax.ppermute(theirs, "core", [(0, 1), (1, 0)])
     return call(write_kernel, single(64, 2, 1024), [SMEM] + [VMEM] * 3, owner_offsets, mine, other, local)
 

time: 138 us -> 138 us (level)
  no operation moved by 1% of the time
where the time goes in v5:
time: 138 us; the launch traced here: 137 us
  blocking collectives  90.1 us (65%)
  starting transfers between devices  21.1 us (15%)
  waiting for transfers between devices  13.4 us (10%)
  Pallas kernels  10.6 us (8%)
  local copies, waits for them, and re-layouts  1.97 us (1%)
    all_to_all x1, blocking collectives, shifted(): lax.all_to_all(block, ('zh', 'zl', 'y'), 0, 0, axis_index_groups=runs, ti...  25.6 us
    all_to_all x1, blocking collectives, late_chain(): lax.all_to_all(parts, ('zh', 'y'), 0, 0, tiled=True).reshape(4, 4, 64, 256)  25.4 us
    all_to_all x1, blocking collectives, deliver(): arrived = lax.all_to_all(routed, ('zl', 'y'), 0, 0, tiled=True)  19.8 us
    all_to_all x1, blocking collectives, late_chain(): parts = lax.all_to_all(partial, 'x', 0, 0, tiled=True)  19.3 us
    pallas_call x9, Pallas kernels, call(): pl.pallas_call(kernel, out_shape=out, in_specs=in_specs, out_specs=jax.tr...  10.6 us
    all_to_all x1, waiting for transfers between devices, shifted(): lax.all_to_all(block, ('zh', 'zl', 'y'), 0, 0, axis_index_groups=runs, ti...  10.6 us
    ppermute x1, starting transfers between devices, body(): other = lax.ppermute(own, 'core', [(0, 1), (1, 0)])  8.79 us
    all_to_all x1, starting transfers between devices, shifted(): lax.all_to_all(block, ('zh', 'zl', 'y'), 0, 0, axis_index_groups=runs, ti...  8.43 us
  transfers between devices with their start and end apart: 4, of which 3 were waited for; matrix products, arithmetic and copies ran while one was open for 0% of the time, Pallas kernels for 1%

profile of v5, /device:TPU:1, one launch (start us, length us, event | category | flops | bytes accessed | tf_op | source)
XLA Modules:
  0.0 137.2 jit_solution(5605707004363231963)
XLA Ops:
  0.0 1.0 copy.8
  1.0 0.0 copy-start
  1.0 0.9 copy-done
  2.0 8.8 %collective-permute-start.1 = (bf16[2,16,8,1024]{3,2,1,0:T(8,128)(2,1)S(1)}, bf16[2,16,8,1024]{3,2,1,0:T(8,128)(2,1)S(1)}, u32[]{:S(2)}, u32[]{:S(2)}) collective-permute-start(bf16[2,16,8,1024]{3,2,1,0:T(8,128)(2,1)S(1)} %shard_map.73), channel_id=1, source_target_pairs={{0,1},{1,0},{2,3},{3,2},{4,5},{5,4},{6,7},{7,6},{8,9},{9,8},{10,11... | collective-permute-start | bytes 1572872 | tf_op jit(solution)/shard_map/ppermute | solution.py:331
  10.8 1.5 %collective-permute-done.1 = bf16[2,16,8,1024]{3,2,1,0:T(8,128)(2,1)S(1)} collective-permute-done((bf16[2,16,8,1024]{3,2,1,0:T(8,128)(2,1)S(1)}, bf16[2,16,8,1024]{3,2,1,0:T(8,128)(2,1)S(1)}, u32[]{:S(2)}, u32[]{:S(2)}) %collective-permute-start.1) | collective-permute-done | bytes 524320 | tf_op jit(solution)/shard_map/ppermute | solution.py:331
  12.3 98.6 %conditional.1 = (bf16[4,4,64,256]{3,2,1,0:T(8,128)(2,1)}, f32[64,2048]{1,0:T(8,128)S(1)}) conditional(s32[]{:T(128)} %convert_element_type.3, (s32[33]{0:T(128)}, s32[2,32]{1,0:T(2,128)}, bf16[2,16,8,1024]{3,2,1,0:T(8,128)(2,1)S(1)}, bf16[2,16,8,1024]{3,2,1,0:T(8,128)(2,1)S(1)}, f32[16]{0:T(128)}, /*index=5*/bf16[1024,1024]{1,0:T(8,128)(2,1)}, ...), branch_computations={%region_0.0_spmd, %region_1.0_spmd} | conditional | bytes 22022628 | solution.py:332
  12.3 1.6 %branch_0_fun.5 = (bf16[16,16,8,256]{3,2,1,0:T(8,128)(2,1)S(1)}, bf16[16,4,8,256]{3,2,1,0:T(8,128)(2,1)}) custom-call(s32[33]{0:T(128)} %get-tuple-element.33.offsets, s32[2,32]{1,0:T(2,128)} %get-tuple-element.35.orbitals, bf16[2,16,8,1024]{3,2,1,0:T(8,128)(2,1)S(1)} %get-tuple-element.36.own, bf16[2,16,8,1024]{3,2,1,0:T(8,128)(2,1)S(1)} %get-tuple-element.37.other), custom_call_target="tpu_custom_call" | custom-call | tf_op jit(solution)/shard_map/cond/branch_0_fun/pallas_call | solution.py:245
  13.9 0.0 copy-start.6
  13.9 8.4 %all-to-all-start.3 = ((bf16[16,4,8,256]{3,2,1,0:T(8,128)(2,1)}), bf16[16,4,8,256]{3,2,1,0:T(8,128)(2,1)S(1)}, u32[]{:S(2)}, u32[]{:S(2)}) async-start(bf16[16,4,8,256]{3,2,1,0:T(8,128)(2,1)} %get-tuple-element.39), calls=%async_computation.3 | async-start | bytes 524288 | tf_op jit(solution)/shard_map/cond/branch_0_fun/all_to_all | solution.py:265
  22.3 1.9 %collective-permute-start = (bf16[8,128]{1,0:T(8,128)(2,1)S(1)}, bf16[8,128]{1,0:T(8,128)(2,1)S(1)}, u32[]{:S(2)}, u32[]{:S(2)}) collective-permute-start(bf16[8,128]{1,0:T(8,128)(2,1)S(1)} %slice_bitcast_fusion), channel_id=1, source_target_pairs={{1,33},{33,65},{65,97},{97,1},{3,35},{35,67},{67,99},{99,3},{5,37}... | collective-permute-start | bytes 6152 | tf_op jit(solution)/shard_map/cond/branch_0_fun/ppermute | solution.py:310
  24.3 10.6 %all-to-all-done.3.after.tiles = bf16[16,4,8,256]{3,2,1,0:T(8,128)(2,1)S(1)} async-done(((bf16[16,4,8,256]{3,2,1,0:T(8,128)(2,1)}), bf16[16,4,8,256]{3,2,1,0:T(8,128)(2,1)S(1)}, u32[]{:S(2)}, u32[]{:S(2)}) %all-to-all-start.3) | async-done | bytes 262176 | tf_op jit(solution)/shard_map/cond/branch_0_fun/all_to_all | solution.py:265
  34.8 2.1 %branch_0_fun.6.local = f32[64,2048]{1,0:T(8,128)S(1)} custom-call(s32[33]{0:T(128)} %get-tuple-element.33.offsets, s32[2,32]{1,0:T(2,128)} %get-tuple-element.35.orbitals, f32[16]{0:T(128)} %get-tuple-element.40.energy, bf16[2,16,8,1024]{3,2,1,0:T(8,128)(2,1)S(1)} %get-tuple-element.36.own, bf16[1024,1024]{1,0:T(8,128)(2,1)} %get-tuple-element.41.fock, ...), custom_call_target="tpu_custom_call" | custom-call | tf_op jit(solution)/shard_map/cond/branch_0_fun/pallas_call | solution.py:245
  36.9 0.0 collective-permute-done.token
  36.9 0.0 copy-done.6
  36.9 0.0 copy-start.1
  36.9 0.0 copy-start.10
  36.9 0.9 branch_0_fun.7
  37.9 25.6 %all_to_all.33.arrived = bf16[16,18,8,256]{3,2,1,0:T(8,128)(2,1)S(1)} all-to-all(bf16[16,18,8,256]{3,2,1,0:T(8,128)(2,1)S(1)} %branch_0_fun.7), channel_id=1, replica_groups={{32,34,36,38,40,42,44,46,16,18,20,22,24,26,28,30},{64,66,68,70,72,74,76..., dimensions={0} | all-to-all | bytes 2359296 | tf_op jit(solution)/shard_map/cond/branch_0_fun/all_to_all | solution.py:265
  63.5 0.0 copy-done.1
  63.5 0.0 copy-done.10
  63.5 2.5 %branch_0_fun.8 = bf16[4,256,1024]{2,1,0:T(8,128)(2,1)S(1)} custom-call(s32[33]{0:T(128)S(1)} %copy-done.6, s32[32]{0:T(128)S(1)} %copy-done.10, bf16[16,18,8,256]{3,2,1,0:T(8,128)(2,1)S(1)} %all_to_all.33.arrived, bf16[1024,1024]{1,0:T(8,128)(2,1)S(1)} %copy-done.1), custom_call_target="tpu_custom_call" | custom-call | tf_op jit(solution)/shard_map/cond/branch_0_fun/pallas_call | solution.py:245
  66.0 19.3 %all_to_all.34.parts = bf16[4,256,1024]{2,1,0:T(8,128)(2,1)S(1)} all-to-all(bf16[4,256,1024]{2,1,0:T(8,128)(2,1)S(1)} %branch_0_fun.8), channel_id=1, replica_groups=mesh['x'=4,'zh'=4,'zl'=4,'y'=4,'core'=2] {'x'}, dimensions={0} | all-to-all | bytes 4194304 | tf_op jit(solution)/shard_map/cond/branch_0_fun/all_to_all | solution.py:320
  85.3 0.3 branch_0_fun.9
  85.5 25.4 %all_to_all.35 = bf16[16,64,256]{2,1,0:T(8,128)(2,1)} all-to-all(bf16[16,64,256]{2,1,0:T(8,128)(2,1)S(1)} %branch_0_fun.9), channel_id=1, replica_groups=mesh['x'=4,'zh'=4,'zl'=4,'y'=4,'core'=2] {'zh','y'}, dimensions={0} | all-to-all | bytes 1048576 | tf_op jit(solution)/shard_map/cond/branch_0_fun/all_to_all | solution.py:322
  110.9 0.0 copy-start.5
  110.9 1.2 shard_map.74
  112.1 19.8 %all_to_all.39.arrived = bf16[16,64,256]{2,1,0:T(8,128)(2,1)S(1)} all-to-all(bf16[16,64,256]{2,1,0:T(8,128)(2,1)S(1)} %shard_map.74), channel_id=1, replica_groups=mesh['x'=4,'zh'=4,'zl'=4,'y'=4,'core'=2] {'zl','y'}, dimensions={0} | all-to-all | bytes 1048576 | tf_op jit(solution)/shard_map/all_to_all | solution.py:280
  131.8 0.0 copy-done.5
  131.9 0.6 shard_map.75
  132.4 1.9 %collective-permute-start.2 = (bf16[64,1024]{1,0:T(8,128)(2,1)S(1)}, bf16[64,1024]{1,0:T(8,128)(2,1)S(1)}, u32[]{:S(2)}, u32[]{:S(2)}) collective-permute-start(bf16[64,1024]{1,0:T(8,128)(2,1)S(1)} %get-tuple-element.55), channel_id=1, source_target_pairs={{0,1},{1,0},{2,3},{3,2},{4,5},{5,4},{6,7},{7,6},{8,9},{9,8},{10,11... | collective-permute-start | bytes 393224 | tf_op jit(solution)/shard_map/ppermute | solution.py:337
  134.4 1.3 collective-permute-done.2.other
  135.7 1.5 %shard_map.76 = f32[64,2,1024]{2,1,0:T(2,128)} custom-call(s32[33]{0:T(128)S(1)} %copy-done.5, bf16[64,1024]{1,0:T(8,128)(2,1)S(1)} %get-tuple-element.54.mine, bf16[64,1024]{1,0:T(8,128)(2,1)S(1)} %collective-permute-done.2.other, f32[64,2048]{1,0:T(8,128)S(1)} %get-tuple-element.56.local), custom_call_target="tpu_custom_call" | custom-call | tf_op jit(solution)/shard_map/pallas_call | solution.py:245
  (2 shorter events, 0.0 us)
Async XLA Ops:
  1.0 1.0 copy-start
  2.0 10.3 %collective-permute-start.1 = (bf16[2,16,8,1024]{3,2,1,0:T(8,128)(2,1)S(1)}, bf16[2,16,8,1024]{3,2,1,0:T(8,128)(2,1)S(1)}, u32[]{:S(2)}, u32[]{:S(2)}) collective-permute-start(bf16[2,16,8,1024]{3,2,1,0:T(8,128)(2,1)S(1)} %shard_map.73), channel_id=1, source_target_pairs={{0,1},{1,0},{2,3},{3,2},{4,5},{5,4},{6,7},{7,6},{8,9},{9,8},{10,11... | collective-permute-start | bytes 1572872 | tf_op jit(solution)/shard_map/ppermute | solution.py:331
  13.9 23.0 %copy-start.6 = (s32[33]{0:T(128)S(1)}, s32[33]{0:T(128)}, u32[]{:S(2)}) copy-start(s32[33]{0:T(128)} %get-tuple-element.33.offsets) | copy-start | bytes 400 | tf_op jit(solution)/shard_map/cond
  13.9 20.9 %all-to-all-start.3 = ((bf16[16,4,8,256]{3,2,1,0:T(8,128)(2,1)}), bf16[16,4,8,256]{3,2,1,0:T(8,128)(2,1)S(1)}, u32[]{:S(2)}, u32[]{:S(2)}) async-start(bf16[16,4,8,256]{3,2,1,0:T(8,128)(2,1)} %get-tuple-element.39), calls=%async_computation.3 | async-start | bytes 524288 | tf_op jit(solution)/shard_map/cond/branch_0_fun/all_to_all | solution.py:265
  22.3 14.6 %collective-permute-start = (bf16[8,128]{1,0:T(8,128)(2,1)S(1)}, bf16[8,128]{1,0:T(8,128)(2,1)S(1)}, u32[]{:S(2)}, u32[]{:S(2)}) collective-permute-start(bf16[8,128]{1,0:T(8,128)(2,1)S(1)} %slice_bitcast_fusion), channel_id=1, source_target_pairs={{1,33},{33,65},{65,97},{97,1},{3,35},{35,67},{67,99},{99,3},{5,37}... | collective-permute-start | bytes 6152 | tf_op jit(solution)/shard_map/cond/branch_0_fun/ppermute | solution.py:310
  36.9 26.6 %copy-start.1 = (bf16[1024,1024]{1,0:T(8,128)(2,1)S(1)}, bf16[1024,1024]{1,0:T(8,128)(2,1)}, u32[]{:S(2)}) copy-start(bf16[1024,1024]{1,0:T(8,128)(2,1)} %get-tuple-element.41.fock) | copy-start | bytes 6291460 | tf_op jit(solution)/shard_map/cond
  36.9 26.6 %copy-start.10 = (s32[32]{0:T(128)S(1)}, s32[32]{0:T(128)}, u32[]{:S(2)}) copy-start(s32[32]{0:T(128)} %get-tuple-element.34.case) | copy-start | bytes 388 | tf_op jit(solution)/shard_map/cond
  110.9 20.9 %copy-start.5 = (s32[33]{0:T(128)S(1)}, s32[33]{0:T(128)}, u32[]{:S(2)}) copy-start(s32[33]{0:T(128)} %offsets.5) | copy-start | bytes 400
  132.4 3.2 %collective-permute-start.2 = (bf16[64,1024]{1,0:T(8,128)(2,1)S(1)}, bf16[64,1024]{1,0:T(8,128)(2,1)S(1)}, u32[]{:S(2)}, u32[]{:S(2)}) collective-permute-start(bf16[64,1024]{1,0:T(8,128)(2,1)S(1)} %get-tuple-element.55), channel_id=1, source_target_pairs={{0,1},{1,0},{2,3},{3,2},{4,5},{5,4},{6,7},{7,6},{8,9},{9,8},{10,11... | collective-permute-start | bytes 393224 | tf_op jit(solution)/shard_map/ppermute | solution.py:337

commit v6 on v5

--- a/solution.py
+++ b/solution.py
@@ -272,13 +272,11 @@
     )
 
 
-def deliver(parts, owner_offsets):
-    routed = call(
+def route(parts, owner_offsets):
+    return call(
         route_kernel, half(16, 64, 256), [SMEM, VMEM], owner_offsets, parts,
         scratch=[pltpu.VMEM((4, 64, 256), jnp.bfloat16)],
     )
-    arrived = lax.all_to_all(routed, ("zl", "y"), 0, 0, tiled=True)
-    return call(pick_kernel, [half(64, 1024), half(64, 1024)], [SMEM, VMEM], owner_offsets, arrived)
 
 
 def early_chain(own, other, fock, orbital_energy, orbitals, pair_case, owner_offsets):
@@ -296,7 +294,7 @@
         finish_kernel, half(4, 4, 64, 256), [VMEM, VMEM], parts, fock, scratch=[pltpu.VMEM((512, 1024), jnp.bfloat16)]
     )
     parts = lax.all_to_all(parts, "zh", 0, 0, tiled=True)
-    return parts, local_part(own, fock, orbital_energy, orbitals, owner_offsets, parts)
+    return route(parts, owner_offsets), local_part(own, fock, orbital_energy, orbitals, owner_offsets, parts)
 
 
 def late_chain(own, other, fock, orbital_energy, orbitals, pair_case, owner_offsets):
@@ -320,7 +318,7 @@
     parts = lax.all_to_all(partial, "x", 0, 0, tiled=True)
     parts = call(late_finish_kernel, half(16, 64, 256), [VMEM], parts)
     parts = lax.all_to_all(parts, ("zh", "y"), 0, 0, tiled=True).reshape(4, 4, 64, 256)
-    return parts, local
+    return route(parts, owner_offsets), local
 
 
 def body(chol_vectors, amplitudes, fock, orbital_energy, pair_orbitals, pair_case, owner_offsets):
@@ -329,11 +327,12 @@
 
     own = call(pack_kernel, half(2, 16, 8, 1024), [VMEM] * 2, chol_vectors, flat)
     other = lax.ppermute(own, "core", [(0, 1), (1, 0)])
-    parts, local = lax.cond(
+    routed, local = lax.cond(
         lax.axis_index("core") == 0, early_chain, late_chain,
         own, other, fock, orbital_energy, orbitals, pair_case, owner_offsets,
     )
-    mine, theirs = deliver(parts, owner_offsets)
+    arrived = lax.all_to_all(routed, ("zl", "y"), 0, 0, tiled=True)
+    mine, theirs = call(pick_kernel, [half(64, 1024), half(64, 1024)], [SMEM, VMEM], owner_offsets, arrived)
     other = lax.ppermute(theirs, "core", [(0, 1), (1, 0)])
     return call(write_kernel, single(64, 2, 1024), [SMEM] + [VMEM] * 3, owner_offsets, mine, other, local)
 

time: 138 us -> 137 us (level)
  transfers between devices with their start and end apart: 4 -> 4, of which waited for: 3 -> 3; matrix products, arithmetic and copies ran while one was open for 0% -> 0% of each run, Pallas kernels for 1% -> 2%
where the time goes in v6:
time: 137 us
  blocking collectives  90 us (66%)
  starting transfers between devices  21.1 us (15%)
  waiting for transfers between devices  13.4 us (10%)
  Pallas kernels  10.3 us (8%)
  local copies, waits for them, and re-layouts  1.97 us (1%)
    all_to_all x1, blocking collectives, shifted(): lax.all_to_all(block, ('zh', 'zl', 'y'), 0, 0, axis_index_groups=runs, ti...  25.6 us
    all_to_all x1, blocking collectives, late_chain(): lax.all_to_all(parts, ('zh', 'y'), 0, 0, tiled=True).reshape(4, 4, 64, 256)  25 us
    all_to_all x1, blocking collectives, body(): arrived = lax.all_to_all(routed, ('zl', 'y'), 0, 0, tiled=True)  20 us
    all_to_all x1, blocking collectives, late_chain(): parts = lax.all_to_all(partial, 'x', 0, 0, tiled=True)  19.3 us
    all_to_all x1, waiting for transfers between devices, shifted(): lax.all_to_all(block, ('zh', 'zl', 'y'), 0, 0, axis_index_groups=runs, ti...  10.6 us
    pallas_call x9, Pallas kernels, call(): pl.pallas_call(kernel, out_shape=out, in_specs=in_specs, out_specs=jax.tr...  10.3 us
    ppermute x1, starting transfers between devices, body(): other = lax.ppermute(own, 'core', [(0, 1), (1, 0)])  8.79 us
    all_to_all x1, starting transfers between devices, shifted(): lax.all_to_all(block, ('zh', 'zl', 'y'), 0, 0, axis_index_groups=runs, ti...  8.43 us
  transfers between devices with their start and end apart: 4, of which 3 were waited for; matrix products, arithmetic and copies ran while one was open for 0% of the time, Pallas kernels for 2%

profile of v6, /device:TPU:1, one launch (start us, length us, event | category | flops | bytes accessed | tf_op | source)
XLA Modules:
  0.0 136.9 jit_solution(15853039441150527961)
XLA Ops:
  0.0 1.0 copy.8
  1.0 0.0 copy-start
  1.0 0.9 copy-done
  2.0 8.8 %collective-permute-start.1 = (bf16[2,16,8,1024]{3,2,1,0:T(8,128)(2,1)S(1)}, bf16[2,16,8,1024]{3,2,1,0:T(8,128)(2,1)S(1)}, u32[]{:S(2)}, u32[]{:S(2)}) collective-permute-start(bf16[2,16,8,1024]{3,2,1,0:T(8,128)(2,1)S(1)} %shard_map.73), channel_id=1, source_target_pairs={{0,1},{1,0},{2,3},{3,2},{4,5},{5,4},{6,7},{7,6},{8,9},{9,8},{10,11... | collective-permute-start | bytes 1572872 | tf_op jit(solution)/shard_map/ppermute | solution.py:329
  10.8 1.5 %collective-permute-done.1 = bf16[2,16,8,1024]{3,2,1,0:T(8,128)(2,1)S(1)} collective-permute-done((bf16[2,16,8,1024]{3,2,1,0:T(8,128)(2,1)S(1)}, bf16[2,16,8,1024]{3,2,1,0:T(8,128)(2,1)S(1)}, u32[]{:S(2)}, u32[]{:S(2)}) %collective-permute-start.1) | collective-permute-done | bytes 524320 | tf_op jit(solution)/shard_map/ppermute | solution.py:329
  12.3 0.0 copy-start.5
  12.3 99.0 %conditional.1 = (bf16[16,64,256]{2,1,0:T(8,128)(2,1)S(1)}, f32[64,2048]{1,0:T(8,128)S(1)}) conditional(s32[]{:T(128)} %convert_element_type.3, (s32[33]{0:T(128)}, s32[2,32]{1,0:T(2,128)}, bf16[2,16,8,1024]{3,2,1,0:T(8,128)(2,1)S(1)}, bf16[2,16,8,1024]{3,2,1,0:T(8,128)(2,1)S(1)}, f32[16]{0:T(128)}, /*index=5*/bf16[1024,1024]{1,0:T(8,128)(2,1)}, ...), branch_computations={%region_0.0_spmd, %region_1.0_spmd} | conditional | bytes 22022628 | solution.py:330
  12.3 1.7 %branch_0_fun.6 = (bf16[16,16,8,256]{3,2,1,0:T(8,128)(2,1)S(1)}, bf16[16,4,8,256]{3,2,1,0:T(8,128)(2,1)}) custom-call(s32[33]{0:T(128)} %get-tuple-element.33.offsets, s32[2,32]{1,0:T(2,128)} %get-tuple-element.35.orbitals, bf16[2,16,8,1024]{3,2,1,0:T(8,128)(2,1)S(1)} %get-tuple-element.36.own, bf16[2,16,8,1024]{3,2,1,0:T(8,128)(2,1)S(1)} %get-tuple-element.37.other), custom_call_target="tpu_custom_call" | custom-call | tf_op jit(solution)/shard_map/cond/branch_0_fun/pallas_call | solution.py:245
  14.0 0.0 copy-start.6
  14.0 8.4 %all-to-all-start.3 = ((bf16[16,4,8,256]{3,2,1,0:T(8,128)(2,1)}), bf16[16,4,8,256]{3,2,1,0:T(8,128)(2,1)S(1)}, u32[]{:S(2)}, u32[]{:S(2)}) async-start(bf16[16,4,8,256]{3,2,1,0:T(8,128)(2,1)} %get-tuple-element.39), calls=%async_computation.3 | async-start | bytes 524288 | tf_op jit(solution)/shard_map/cond/branch_0_fun/all_to_all | solution.py:265
  22.5 1.9 %collective-permute-start = (bf16[8,128]{1,0:T(8,128)(2,1)S(1)}, bf16[8,128]{1,0:T(8,128)(2,1)S(1)}, u32[]{:S(2)}, u32[]{:S(2)}) collective-permute-start(bf16[8,128]{1,0:T(8,128)(2,1)S(1)} %slice_bitcast_fusion), channel_id=1, source_target_pairs={{1,33},{33,65},{65,97},{97,1},{3,35},{35,67},{67,99},{99,3},{5,37}... | collective-permute-start | bytes 6152 | tf_op jit(solution)/shard_map/cond/branch_0_fun/ppermute | solution.py:308
  24.4 10.6 %all-to-all-done.3.after.tiles = bf16[16,4,8,256]{3,2,1,0:T(8,128)(2,1)S(1)} async-done(((bf16[16,4,8,256]{3,2,1,0:T(8,128)(2,1)}), bf16[16,4,8,256]{3,2,1,0:T(8,128)(2,1)S(1)}, u32[]{:S(2)}, u32[]{:S(2)}) %all-to-all-start.3) | async-done | bytes 262176 | tf_op jit(solution)/shard_map/cond/branch_0_fun/all_to_all | solution.py:265
  35.0 2.1 %branch_0_fun.7.local = f32[64,2048]{1,0:T(8,128)S(1)} custom-call(s32[33]{0:T(128)} %get-tuple-element.33.offsets, s32[2,32]{1,0:T(2,128)} %get-tuple-element.35.orbitals, f32[16]{0:T(128)} %get-tuple-element.40.energy, bf16[2,16,8,1024]{3,2,1,0:T(8,128)(2,1)S(1)} %get-tuple-element.36.own, bf16[1024,1024]{1,0:T(8,128)(2,1)} %get-tuple-element.41.fock, ...), custom_call_target="tpu_custom_call" | custom-call | tf_op jit(solution)/shard_map/cond/branch_0_fun/pallas_call | solution.py:245
  37.0 0.0 collective-permute-done.token
  37.0 0.0 copy-done.6
  37.0 0.0 copy-start.1
  37.1 0.0 copy-start.10
  37.1 0.9 branch_0_fun.8
  38.0 25.6 %all_to_all.33.arrived = bf16[16,18,8,256]{3,2,1,0:T(8,128)(2,1)S(1)} all-to-all(bf16[16,18,8,256]{3,2,1,0:T(8,128)(2,1)S(1)} %branch_0_fun.8), channel_id=1, replica_groups={{32,34,36,38,40,42,44,46,16,18,20,22,24,26,28,30},{64,66,68,70,72,74,76..., dimensions={0} | all-to-all | bytes 2359296 | tf_op jit(solution)/shard_map/cond/branch_0_fun/all_to_all | solution.py:265
  63.6 0.0 copy-done.1
  63.6 0.0 copy-done.10
  63.6 2.5 %branch_0_fun.9 = bf16[4,256,1024]{2,1,0:T(8,128)(2,1)S(1)} custom-call(s32[33]{0:T(128)S(1)} %copy-done.6, s32[32]{0:T(128)S(1)} %copy-done.10, bf16[16,18,8,256]{3,2,1,0:T(8,128)(2,1)S(1)} %all_to_all.33.arrived, bf16[1024,1024]{1,0:T(8,128)(2,1)S(1)} %copy-done.1), custom_call_target="tpu_custom_call" | custom-call | tf_op jit(solution)/shard_map/cond/branch_0_fun/pallas_call | solution.py:245
  66.1 19.3 %all_to_all.34.parts = bf16[4,256,1024]{2,1,0:T(8,128)(2,1)S(1)} all-to-all(bf16[4,256,1024]{2,1,0:T(8,128)(2,1)S(1)} %branch_0_fun.9), channel_id=1, replica_groups=mesh['x'=4,'zh'=4,'zl'=4,'y'=4,'core'=2] {'x'}, dimensions={0} | all-to-all | bytes 4194304 | tf_op jit(solution)/shard_map/cond/branch_0_fun/all_to_all | solution.py:318
  85.4 0.3 branch_0_fun.10
  85.7 25.0 %all_to_all.35 = bf16[16,64,256]{2,1,0:T(8,128)(2,1)S(1)} all-to-all(bf16[16,64,256]{2,1,0:T(8,128)(2,1)S(1)} %branch_0_fun.10), channel_id=1, replica_groups=mesh['x'=4,'zh'=4,'zl'=4,'y'=4,'core'=2] {'zh','y'}, dimensions={0} | all-to-all | bytes 1048576 | tf_op jit(solution)/shard_map/cond/branch_0_fun/all_to_all | solution.py:320
  110.7 0.6 branch_0_fun.11
  111.4 20.0 %all_to_all.39.arrived = bf16[16,64,256]{2,1,0:T(8,128)(2,1)S(1)} all-to-all(bf16[16,64,256]{2,1,0:T(8,128)(2,1)S(1)} %get-tuple-element.53), channel_id=1, replica_groups=mesh['x'=4,'zh'=4,'zl'=4,'y'=4,'core'=2] {'zl','y'}, dimensions={0} | all-to-all | bytes 1048576 | tf_op jit(solution)/shard_map/all_to_all | solution.py:334
  131.4 0.7 shard_map.74
  132.1 1.9 %collective-permute-start.2 = (bf16[64,1024]{1,0:T(8,128)(2,1)S(1)}, bf16[64,1024]{1,0:T(8,128)(2,1)S(1)}, u32[]{:S(2)}, u32[]{:S(2)}) collective-permute-start(bf16[64,1024]{1,0:T(8,128)(2,1)S(1)} %get-tuple-element.55), channel_id=1, source_target_pairs={{0,1},{1,0},{2,3},{3,2},{4,5},{5,4},{6,7},{7,6},{8,9},{9,8},{10,11... | collective-permute-start | bytes 393224 | tf_op jit(solution)/shard_map/ppermute | solution.py:336
  134.0 1.3 collective-permute-done.2.other
  135.3 0.0 copy-done.5
  135.4 1.5 %shard_map.75 = f32[64,2,1024]{2,1,0:T(2,128)} custom-call(s32[33]{0:T(128)S(1)} %copy-done.5, bf16[64,1024]{1,0:T(8,128)(2,1)S(1)} %get-tuple-element.54.mine, bf16[64,1024]{1,0:T(8,128)(2,1)S(1)} %collective-permute-done.2.other, f32[64,2048]{1,0:T(8,128)S(1)} %get-tuple-element.56.local), custom_call_target="tpu_custom_call" | custom-call | tf_op jit(solution)/shard_map/pallas_call | solution.py:245
  (2 shorter events, 0.0 us)
Async XLA Ops:
  1.0 1.0 copy-start
  2.0 10.3 %collective-permute-start.1 = (bf16[2,16,8,1024]{3,2,1,0:T(8,128)(2,1)S(1)}, bf16[2,16,8,1024]{3,2,1,0:T(8,128)(2,1)S(1)}, u32[]{:S(2)}, u32[]{:S(2)}) collective-permute-start(bf16[2,16,8,1024]{3,2,1,0:T(8,128)(2,1)S(1)} %shard_map.73), channel_id=1, source_target_pairs={{0,1},{1,0},{2,3},{3,2},{4,5},{5,4},{6,7},{7,6},{8,9},{9,8},{10,11... | collective-permute-start | bytes 1572872 | tf_op jit(solution)/shard_map/ppermute | solution.py:329
  12.3 123.0 %copy-start.5 = (s32[33]{0:T(128)S(1)}, s32[33]{0:T(128)}, u32[]{:S(2)}) copy-start(s32[33]{0:T(128)} %offsets.3) | copy-start | bytes 400
  14.0 23.0 %copy-start.6 = (s32[33]{0:T(128)S(1)}, s32[33]{0:T(128)}, u32[]{:S(2)}) copy-start(s32[33]{0:T(128)} %get-tuple-element.33.offsets) | copy-start | bytes 400 | tf_op jit(solution)/shard_map/cond
  14.0 20.9 %all-to-all-start.3 = ((bf16[16,4,8,256]{3,2,1,0:T(8,128)(2,1)}), bf16[16,4,8,256]{3,2,1,0:T(8,128)(2,1)S(1)}, u32[]{:S(2)}, u32[]{:S(2)}) async-start(bf16[16,4,8,256]{3,2,1,0:T(8,128)(2,1)} %get-tuple-element.39), calls=%async_computation.3 | async-start | bytes 524288 | tf_op jit(solution)/shard_map/cond/branch_0_fun/all_to_all | solution.py:265
  22.5 14.6 %collective-permute-start = (bf16[8,128]{1,0:T(8,128)(2,1)S(1)}, bf16[8,128]{1,0:T(8,128)(2,1)S(1)}, u32[]{:S(2)}, u32[]{:S(2)}) collective-permute-start(bf16[8,128]{1,0:T(8,128)(2,1)S(1)} %slice_bitcast_fusion), channel_id=1, source_target_pairs={{1,33},{33,65},{65,97},{97,1},{3,35},{35,67},{67,99},{99,3},{5,37}... | collective-permute-start | bytes 6152 | tf_op jit(solution)/shard_map/cond/branch_0_fun/ppermute | solution.py:308
  37.0 26.6 %copy-start.1 = (bf16[1024,1024]{1,0:T(8,128)(2,1)S(1)}, bf16[1024,1024]{1,0:T(8,128)(2,1)}, u32[]{:S(2)}) copy-start(bf16[1024,1024]{1,0:T(8,128)(2,1)} %get-tuple-element.41.fock) | copy-start | bytes 6291460 | tf_op jit(solution)/shard_map/cond
  37.1 26.6 %copy-start.10 = (s32[32]{0:T(128)S(1)}, s32[32]{0:T(128)}, u32[]{:S(2)}) copy-start(s32[32]{0:T(128)} %get-tuple-element.34.case) | copy-start | bytes 388 | tf_op jit(solution)/shard_map/cond
  132.1 3.2 %collective-permute-start.2 = (bf16[64,1024]{1,0:T(8,128)(2,1)S(1)}, bf16[64,1024]{1,0:T(8,128)(2,1)S(1)}, u32[]{:S(2)}, u32[]{:S(2)}) collective-permute-start(bf16[64,1024]{1,0:T(8,128)(2,1)S(1)} %get-tuple-element.55), channel_id=1, source_target_pairs={{0,1},{1,0},{2,3},{3,2},{4,5},{5,4},{6,7},{7,6},{8,9},{9,8},{10,11... | collective-permute-start | bytes 393224 | tf_op jit(solution)/shard_map/ppermute | solution.py:336

commit v7 on v6

--- a/solution.py
+++ b/solution.py
@@ -230,15 +230,27 @@
             out[:, y * 256 : (y + 1) * 256] = arrived[((pair & 7) >> 1) * 4 + y]
 
 
-def write_kernel(offsets, mine, other, local, out):
+def own_kernel(offsets, mine, local, out):
     owner = owner_index()
     first = offsets[owner]
     count = offsets[owner + 1] - first
     for slot in range(2):
         own = ((first + slot) & 1) == lax.axis_index("core")
-        coupled = jnp.where(own, mine[...].astype(jnp.float32), other[...].astype(jnp.float32))
-        result = coupled + local[:, slot * 1024 : (slot + 1) * 1024]
+        result = local[:, slot * 1024 : (slot + 1) * 1024] + jnp.where(own, mine[...].astype(jnp.float32), 0.0)
         out[:, slot, :] = jnp.where(slot < count, result, 0.0)
+
+
+def write_kernel(offsets, base, other, out):
+    owner = owner_index()
+    first = offsets[owner]
+    count = offsets[owner + 1] - first
+    place = (first & 1) ^ lax.axis_index("core") ^ 1
+    out[...] = base[...]
+    for slot in range(2):
+
+        @pl.when((place == slot) & (slot < count))
+        def _():
+            out[:, slot, :] = base[:, slot, :] + other[...].astype(jnp.float32)
 
 
 def call(kernel, out, in_specs, *args, scratch=()):
@@ -334,7 +346,8 @@
     arrived = lax.all_to_all(routed, ("zl", "y"), 0, 0, tiled=True)
     mine, theirs = call(pick_kernel, [half(64, 1024), half(64, 1024)], [SMEM, VMEM], owner_offsets, arrived)
     other = lax.ppermute(theirs, "core", [(0, 1), (1, 0)])
-    return call(write_kernel, single(64, 2, 1024), [SMEM] + [VMEM] * 3, owner_offsets, mine, other, local)
+    base = call(own_kernel, single(64, 2, 1024), [SMEM] + [VMEM] * 2, owner_offsets, mine, local)
+    return call(write_kernel, single(64, 2, 1024), [SMEM] + [VMEM] * 2, owner_offsets, base, other)
 
 
 def solution(mesh):

time: 137 us -> 137 us (level)
    pallas_call x9 -> x10, Pallas kernels: 10.3 us -> 11 us  [call(): pl.pallas_call(kernel, out_shape=out, in_specs=in_specs, out_specs=jax.tr...]
where the time goes in v7:
time: 137 us
  blocking collectives  90 us (66%)
  starting transfers between devices  21.1 us (15%)
  waiting for transfers between devices  12.7 us (9%)
  Pallas kernels  11 us (8%)
  local copies, waits for them, and re-layouts  1.97 us (1%)
    all_to_all x1, blocking collectives, shifted(): lax.all_to_all(block, ('zh', 'zl', 'y'), 0, 0, axis_index_groups=runs, ti...  25.6 us
    all_to_all x1, blocking collectives, late_chain(): lax.all_to_all(parts, ('zh', 'y'), 0, 0, tiled=True).reshape(4, 4, 64, 256)  25 us
    all_to_all x1, blocking collectives, body(): arrived = lax.all_to_all(routed, ('zl', 'y'), 0, 0, tiled=True)  20.1 us
    all_to_all x1, blocking collectives, late_chain(): parts = lax.all_to_all(partial, 'x', 0, 0, tiled=True)  19.3 us
    pallas_call x10, Pallas kernels, call(): pl.pallas_call(kernel, out_shape=out, in_specs=in_specs, out_specs=jax.tr...  11 us
    all_to_all x1, waiting for transfers between devices, shifted(): lax.all_to_all(block, ('zh', 'zl', 'y'), 0, 0, axis_index_groups=runs, ti...  10.6 us
    ppermute x1, starting transfers between devices, body(): other = lax.ppermute(own, 'core', [(0, 1), (1, 0)])  8.79 us
    all_to_all x1, starting transfers between devices, shifted(): lax.all_to_all(block, ('zh', 'zl', 'y'), 0, 0, axis_index_groups=runs, ti...  8.43 us
  transfers between devices with their start and end apart: 4, of which 3 were waited for; matrix products, arithmetic and copies ran while one was open for 0% of the time, Pallas kernels for 2%

profile of v7, /device:TPU:1, one launch (start us, length us, event | category | flops | bytes accessed | tf_op | source)
XLA Modules:
  0.0 136.9 jit_solution(3944039829169086899)
XLA Ops:
  0.0 1.0 copy.8
  1.0 0.0 copy-start
  1.0 0.9 copy-done
  2.0 8.8 %collective-permute-start.1 = (bf16[2,16,8,1024]{3,2,1,0:T(8,128)(2,1)S(1)}, bf16[2,16,8,1024]{3,2,1,0:T(8,128)(2,1)S(1)}, u32[]{:S(2)}, u32[]{:S(2)}) collective-permute-start(bf16[2,16,8,1024]{3,2,1,0:T(8,128)(2,1)S(1)} %shard_map.73), channel_id=1, source_target_pairs={{0,1},{1,0},{2,3},{3,2},{4,5},{5,4},{6,7},{7,6},{8,9},{9,8},{10,11... | collective-permute-start | bytes 1572872 | tf_op jit(solution)/shard_map/ppermute | solution.py:341
  10.8 1.5 %collective-permute-done.1 = bf16[2,16,8,1024]{3,2,1,0:T(8,128)(2,1)S(1)} collective-permute-done((bf16[2,16,8,1024]{3,2,1,0:T(8,128)(2,1)S(1)}, bf16[2,16,8,1024]{3,2,1,0:T(8,128)(2,1)S(1)}, u32[]{:S(2)}, u32[]{:S(2)}) %collective-permute-start.1) | collective-permute-done | bytes 524320 | tf_op jit(solution)/shard_map/ppermute | solution.py:341
  12.3 0.0 copy-start.5
  12.3 99.0 %conditional.1 = (bf16[16,64,256]{2,1,0:T(8,128)(2,1)S(1)}, f32[64,2048]{1,0:T(8,128)S(1)}) conditional(s32[]{:T(128)} %convert_element_type.3, (s32[33]{0:T(128)}, s32[2,32]{1,0:T(2,128)}, bf16[2,16,8,1024]{3,2,1,0:T(8,128)(2,1)S(1)}, bf16[2,16,8,1024]{3,2,1,0:T(8,128)(2,1)S(1)}, f32[16]{0:T(128)}, /*index=5*/bf16[1024,1024]{1,0:T(8,128)(2,1)}, ...), branch_computations={%region_0.0_spmd, %region_1.0_spmd} | conditional | bytes 22022628 | solution.py:342
  12.3 1.7 %branch_0_fun.6 = (bf16[16,16,8,256]{3,2,1,0:T(8,128)(2,1)S(1)}, bf16[16,4,8,256]{3,2,1,0:T(8,128)(2,1)}) custom-call(s32[33]{0:T(128)} %get-tuple-element.33.offsets, s32[2,32]{1,0:T(2,128)} %get-tuple-element.35.orbitals, bf16[2,16,8,1024]{3,2,1,0:T(8,128)(2,1)S(1)} %get-tuple-element.36.own, bf16[2,16,8,1024]{3,2,1,0:T(8,128)(2,1)S(1)} %get-tuple-element.37.other), custom_call_target="tpu_custom_call" | custom-call | tf_op jit(solution)/shard_map/cond/branch_0_fun/pallas_call | solution.py:257
  14.0 8.4 %all-to-all-start.3 = ((bf16[16,4,8,256]{3,2,1,0:T(8,128)(2,1)}), bf16[16,4,8,256]{3,2,1,0:T(8,128)(2,1)S(1)}, u32[]{:S(2)}, u32[]{:S(2)}) async-start(bf16[16,4,8,256]{3,2,1,0:T(8,128)(2,1)} %get-tuple-element.39), calls=%async_computation.3 | async-start | bytes 524288 | tf_op jit(solution)/shard_map/cond/branch_0_fun/all_to_all | solution.py:277
  22.5 1.9 %collective-permute-start = (bf16[8,128]{1,0:T(8,128)(2,1)S(1)}, bf16[8,128]{1,0:T(8,128)(2,1)S(1)}, u32[]{:S(2)}, u32[]{:S(2)}) collective-permute-start(bf16[8,128]{1,0:T(8,128)(2,1)S(1)} %slice_bitcast_fusion), channel_id=1, source_target_pairs={{1,33},{33,65},{65,97},{97,1},{3,35},{35,67},{67,99},{99,3},{5,37}... | collective-permute-start | bytes 6152 | tf_op jit(solution)/shard_map/cond/branch_0_fun/ppermute | solution.py:320
  24.4 10.6 %all-to-all-done.3.after.tiles = bf16[16,4,8,256]{3,2,1,0:T(8,128)(2,1)S(1)} async-done(((bf16[16,4,8,256]{3,2,1,0:T(8,128)(2,1)}), bf16[16,4,8,256]{3,2,1,0:T(8,128)(2,1)S(1)}, u32[]{:S(2)}, u32[]{:S(2)}) %all-to-all-start.3) | async-done | bytes 262176 | tf_op jit(solution)/shard_map/cond/branch_0_fun/all_to_all | solution.py:277
  35.0 2.1 %branch_0_fun.7.local = f32[64,2048]{1,0:T(8,128)S(1)} custom-call(s32[33]{0:T(128)} %get-tuple-element.33.offsets, s32[2,32]{1,0:T(2,128)} %get-tuple-element.35.orbitals, f32[16]{0:T(128)} %get-tuple-element.40.energy, bf16[2,16,8,1024]{3,2,1,0:T(8,128)(2,1)S(1)} %get-tuple-element.36.own, bf16[1024,1024]{1,0:T(8,128)(2,1)} %get-tuple-element.41.fock, ...), custom_call_target="tpu_custom_call" | custom-call | tf_op jit(solution)/shard_map/cond/branch_0_fun/pallas_call | solution.py:257
  37.0 0.0 collective-permute-done.token
  37.0 0.0 copy-done.6
  37.0 0.0 copy-start.1
  37.1 0.0 copy-start.10
  37.1 0.9 branch_0_fun.8
  38.0 25.6 %all_to_all.33.arrived = bf16[16,18,8,256]{3,2,1,0:T(8,128)(2,1)S(1)} all-to-all(bf16[16,18,8,256]{3,2,1,0:T(8,128)(2,1)S(1)} %branch_0_fun.8), channel_id=1, replica_groups={{32,34,36,38,40,42,44,46,16,18,20,22,24,26,28,30},{64,66,68,70,72,74,76..., dimensions={0} | all-to-all | bytes 2359296 | tf_op jit(solution)/shard_map/cond/branch_0_fun/all_to_all | solution.py:277
  63.6 0.0 copy-done.1
  63.6 0.0 copy-done.10
  63.6 2.5 %branch_0_fun.9 = bf16[4,256,1024]{2,1,0:T(8,128)(2,1)S(1)} custom-call(s32[33]{0:T(128)S(1)} %copy-done.6, s32[32]{0:T(128)S(1)} %copy-done.10, bf16[16,18,8,256]{3,2,1,0:T(8,128)(2,1)S(1)} %all_to_all.33.arrived, bf16[1024,1024]{1,0:T(8,128)(2,1)S(1)} %copy-done.1), custom_call_target="tpu_custom_call" | custom-call | tf_op jit(solution)/shard_map/cond/branch_0_fun/pallas_call | solution.py:257
  66.1 19.3 %all_to_all.34.parts = bf16[4,256,1024]{2,1,0:T(8,128)(2,1)S(1)} all-to-all(bf16[4,256,1024]{2,1,0:T(8,128)(2,1)S(1)} %branch_0_fun.9), channel_id=1, replica_groups=mesh['x'=4,'zh'=4,'zl'=4,'y'=4,'core'=2] {'x'}, dimensions={0} | all-to-all | bytes 4194304 | tf_op jit(solution)/shard_map/cond/branch_0_fun/all_to_all | solution.py:330
  85.4 0.3 branch_0_fun.10
  85.7 25.0 %all_to_all.35 = bf16[16,64,256]{2,1,0:T(8,128)(2,1)S(1)} all-to-all(bf16[16,64,256]{2,1,0:T(8,128)(2,1)S(1)} %branch_0_fun.10), channel_id=1, replica_groups=mesh['x'=4,'zh'=4,'zl'=4,'y'=4,'core'=2] {'zh','y'}, dimensions={0} | all-to-all | bytes 1048576 | tf_op jit(solution)/shard_map/cond/branch_0_fun/all_to_all | solution.py:332
  110.7 0.6 branch_0_fun.11
  111.3 20.1 %all_to_all.39.arrived = bf16[16,64,256]{2,1,0:T(8,128)(2,1)S(1)} all-to-all(bf16[16,64,256]{2,1,0:T(8,128)(2,1)S(1)} %get-tuple-element.53), channel_id=1, replica_groups=mesh['x'=4,'zh'=4,'zl'=4,'y'=4,'core'=2] {'zl','y'}, dimensions={0} | all-to-all | bytes 1048576 | tf_op jit(solution)/shard_map/all_to_all | solution.py:346
  131.4 0.7 shard_map.74
  132.1 1.9 %collective-permute-start.2 = (bf16[64,1024]{1,0:T(8,128)(2,1)S(1)}, bf16[64,1024]{1,0:T(8,128)(2,1)S(1)}, u32[]{:S(2)}, u32[]{:S(2)}) collective-permute-start(bf16[64,1024]{1,0:T(8,128)(2,1)S(1)} %get-tuple-element.56), channel_id=1, source_target_pairs={{0,1},{1,0},{2,3},{3,2},{4,5},{5,4},{6,7},{7,6},{8,9},{9,8},{10,11... | collective-permute-start | bytes 393224 | tf_op jit(solution)/shard_map/ppermute | solution.py:348
  134.1 0.0 copy-done.5
  134.1 0.7 shard_map.75.base
  134.8 0.6 collective-permute-done.2.other
  135.4 1.5 %shard_map.76 = f32[64,2,1024]{2,1,0:T(2,128)} custom-call(s32[33]{0:T(128)S(1)} %copy-done.5, f32[64,2,1024]{2,1,0:T(2,128)S(1)} %shard_map.75.base, bf16[64,1024]{1,0:T(8,128)(2,1)S(1)} %collective-permute-done.2.other), custom_call_target="tpu_custom_call" | custom-call | tf_op jit(solution)/shard_map/pallas_call | solution.py:257
  (3 shorter events, 0.0 us)
Async XLA Ops:
  1.0 1.0 copy-start
  2.0 10.3 %collective-permute-start.1 = (bf16[2,16,8,1024]{3,2,1,0:T(8,128)(2,1)S(1)}, bf16[2,16,8,1024]{3,2,1,0:T(8,128)(2,1)S(1)}, u32[]{:S(2)}, u32[]{:S(2)}) collective-permute-start(bf16[2,16,8,1024]{3,2,1,0:T(8,128)(2,1)S(1)} %shard_map.73), channel_id=1, source_target_pairs={{0,1},{1,0},{2,3},{3,2},{4,5},{5,4},{6,7},{7,6},{8,9},{9,8},{10,11... | collective-permute-start | bytes 1572872 | tf_op jit(solution)/shard_map/ppermute | solution.py:341
  12.3 121.8 %copy-start.5 = (s32[33]{0:T(128)S(1)}, s32[33]{0:T(128)}, u32[]{:S(2)}) copy-start(s32[33]{0:T(128)} %offsets.5) | copy-start | bytes 400
  14.0 23.0 %copy-start.6 = (s32[33]{0:T(128)S(1)}, s32[33]{0:T(128)}, u32[]{:S(2)}) copy-start(s32[33]{0:T(128)} %get-tuple-element.33.offsets) | copy-start | bytes 400 | tf_op jit(solution)/shard_map/cond
  14.0 20.9 %all-to-all-start.3 = ((bf16[16,4,8,256]{3,2,1,0:T(8,128)(2,1)}), bf16[16,4,8,256]{3,2,1,0:T(8,128)(2,1)S(1)}, u32[]{:S(2)}, u32[]{:S(2)}) async-start(bf16[16,4,8,256]{3,2,1,0:T(8,128)(2,1)} %get-tuple-element.39), calls=%async_computation.3 | async-start | bytes 524288 | tf_op jit(solution)/shard_map/cond/branch_0_fun/all_to_all | solution.py:277
  22.5 14.6 %collective-permute-start = (bf16[8,128]{1,0:T(8,128)(2,1)S(1)}, bf16[8,128]{1,0:T(8,128)(2,1)S(1)}, u32[]{:S(2)}, u32[]{:S(2)}) collective-permute-start(bf16[8,128]{1,0:T(8,128)(2,1)S(1)} %slice_bitcast_fusion), channel_id=1, source_target_pairs={{1,33},{33,65},{65,97},{97,1},{3,35},{35,67},{67,99},{99,3},{5,37}... | collective-permute-start | bytes 6152 | tf_op jit(solution)/shard_map/cond/branch_0_fun/ppermute | solution.py:320
  37.0 26.6 %copy-start.1 = (bf16[1024,1024]{1,0:T(8,128)(2,1)S(1)}, bf16[1024,1024]{1,0:T(8,128)(2,1)}, u32[]{:S(2)}) copy-start(bf16[1024,1024]{1,0:T(8,128)(2,1)} %get-tuple-element.41.fock) | copy-start | bytes 6291460 | tf_op jit(solution)/shard_map/cond
  37.1 26.6 %copy-start.10 = (s32[32]{0:T(128)S(1)}, s32[32]{0:T(128)}, u32[]{:S(2)}) copy-start(s32[32]{0:T(128)} %get-tuple-element.34.case) | copy-start | bytes 388 | tf_op jit(solution)/shard_map/cond
  132.1 3.2 %collective-permute-start.2 = (bf16[64,1024]{1,0:T(8,128)(2,1)S(1)}, bf16[64,1024]{1,0:T(8,128)(2,1)S(1)}, u32[]{:S(2)}, u32[]{:S(2)}) collective-permute-start(bf16[64,1024]{1,0:T(8,128)(2,1)S(1)} %get-tuple-element.56), channel_id=1, source_target_pairs={{0,1},{1,0},{2,3},{3,2},{4,5},{5,4},{6,7},{7,6},{8,9},{9,8},{10,11... | collective-permute-start | bytes 393224 | tf_op jit(solution)/shard_map/ppermute | solution.py:348

commit v8 on v7

--- a/solution.py
+++ b/solution.py
@@ -136,10 +136,9 @@
             cols[start + 256 : start + 384, here] = (swap * left).astype(jnp.bfloat16)
     for row in range(4):
         block = rows[:, row * 256 : (row + 1) * 256].T.astype(jnp.bfloat16)
+        product = jnp.dot(block, cols[...], preferred_element_type=jnp.float32).astype(jnp.bfloat16)
         for part in range(4):
-            there = cols[:, part * 256 : (part + 1) * 256]
-            product = jnp.dot(block, there, preferred_element_type=jnp.float32)
-            out[row * 4 + part, 0:256] = product.astype(jnp.bfloat16)
+            out[row * 4 + part, 0:256] = product[:, part * 256 : (part + 1) * 256]
     for source in range(4):
         pair = pair_at(zl, source, core)
         chip = chip_of(offsets, pair)

time: 137 us -> 137 us (level)
  no operation moved by 1% of the time
where the time goes in v8:
time: 137 us
  blocking collectives  90 us (66%)
  starting transfers between devices  21.1 us (15%)
  waiting for transfers between devices  12.7 us (9%)
  Pallas kernels  10.9 us (8%)
  local copies, waits for them, and re-layouts  1.97 us (1%)
    all_to_all x1, blocking collectives, shifted(): lax.all_to_all(block, ('zh', 'zl', 'y'), 0, 0, axis_index_groups=runs, ti...  25.6 us
    all_to_all x1, blocking collectives, late_chain(): lax.all_to_all(parts, ('zh', 'y'), 0, 0, tiled=True).reshape(4, 4, 64, 256)  25 us
    all_to_all x1, blocking collectives, body(): arrived = lax.all_to_all(routed, ('zl', 'y'), 0, 0, tiled=True)  20.1 us
    all_to_all x1, blocking collectives, late_chain(): parts = lax.all_to_all(partial, 'x', 0, 0, tiled=True)  19.3 us
    pallas_call x10, Pallas kernels, call(): pl.pallas_call(kernel, out_shape=out, in_specs=in_specs, out_specs=jax.tr...  10.9 us
    all_to_all x1, waiting for transfers between devices, shifted(): lax.all_to_all(block, ('zh', 'zl', 'y'), 0, 0, axis_index_groups=runs, ti...  10.6 us
    ppermute x1, starting transfers between devices, body(): other = lax.ppermute(own, 'core', [(0, 1), (1, 0)])  8.79 us
    all_to_all x1, starting transfers between devices, shifted(): lax.all_to_all(block, ('zh', 'zl', 'y'), 0, 0, axis_index_groups=runs, ti...  8.43 us
  transfers between devices with their start and end apart: 4, of which 3 were waited for; matrix products, arithmetic and copies ran while one was open for 0% of the time, Pallas kernels for 2%

profile of v8, /device:TPU:1, one launch (start us, length us, event | category | flops | bytes accessed | tf_op | source)
XLA Modules:
  0.0 136.8 jit_solution(3944039829169086899)
XLA Ops:
  0.0 1.0 copy.8
  1.0 0.0 copy-start
  1.0 0.9 copy-done
  2.0 8.8 %collective-permute-start.1 = (bf16[2,16,8,1024]{3,2,1,0:T(8,128)(2,1)S(1)}, bf16[2,16,8,1024]{3,2,1,0:T(8,128)(2,1)S(1)}, u32[]{:S(2)}, u32[]{:S(2)}) collective-permute-start(bf16[2,16,8,1024]{3,2,1,0:T(8,128)(2,1)S(1)} %shard_map.73), channel_id=1, source_target_pairs={{0,1},{1,0},{2,3},{3,2},{4,5},{5,4},{6,7},{7,6},{8,9},{9,8},{10,11... | collective-permute-start | bytes 1572872 | tf_op jit(solution)/shard_map/ppermute | solution.py:340
  10.8 1.5 %collective-permute-done.1 = bf16[2,16,8,1024]{3,2,1,0:T(8,128)(2,1)S(1)} collective-permute-done((bf16[2,16,8,1024]{3,2,1,0:T(8,128)(2,1)S(1)}, bf16[2,16,8,1024]{3,2,1,0:T(8,128)(2,1)S(1)}, u32[]{:S(2)}, u32[]{:S(2)}) %collective-permute-start.1) | collective-permute-done | bytes 524320 | tf_op jit(solution)/shard_map/ppermute | solution.py:340
  12.3 0.0 copy-start.5
  12.3 99.0 %conditional.1 = (bf16[16,64,256]{2,1,0:T(8,128)(2,1)S(1)}, f32[64,2048]{1,0:T(8,128)S(1)}) conditional(s32[]{:T(128)} %convert_element_type.3, (s32[33]{0:T(128)}, s32[2,32]{1,0:T(2,128)}, bf16[2,16,8,1024]{3,2,1,0:T(8,128)(2,1)S(1)}, bf16[2,16,8,1024]{3,2,1,0:T(8,128)(2,1)S(1)}, f32[16]{0:T(128)}, /*index=5*/bf16[1024,1024]{1,0:T(8,128)(2,1)}, ...), branch_computations={%region_0.0_spmd, %region_1.0_spmd} | conditional | bytes 22022628 | solution.py:341
  12.3 1.7 %branch_0_fun.6 = (bf16[16,16,8,256]{3,2,1,0:T(8,128)(2,1)S(1)}, bf16[16,4,8,256]{3,2,1,0:T(8,128)(2,1)}) custom-call(s32[33]{0:T(128)} %get-tuple-element.33.offsets, s32[2,32]{1,0:T(2,128)} %get-tuple-element.35.orbitals, bf16[2,16,8,1024]{3,2,1,0:T(8,128)(2,1)S(1)} %get-tuple-element.36.own, bf16[2,16,8,1024]{3,2,1,0:T(8,128)(2,1)S(1)} %get-tuple-element.37.other), custom_call_target="tpu_custom_call" | custom-call | tf_op jit(solution)/shard_map/cond/branch_0_fun/pallas_call | solution.py:256
  14.0 8.4 %all-to-all-start.3 = ((bf16[16,4,8,256]{3,2,1,0:T(8,128)(2,1)}), bf16[16,4,8,256]{3,2,1,0:T(8,128)(2,1)S(1)}, u32[]{:S(2)}, u32[]{:S(2)}) async-start(bf16[16,4,8,256]{3,2,1,0:T(8,128)(2,1)} %get-tuple-element.39), calls=%async_computation.3 | async-start | bytes 524288 | tf_op jit(solution)/shard_map/cond/branch_0_fun/all_to_all | solution.py:276
  22.5 1.9 %collective-permute-start = (bf16[8,128]{1,0:T(8,128)(2,1)S(1)}, bf16[8,128]{1,0:T(8,128)(2,1)S(1)}, u32[]{:S(2)}, u32[]{:S(2)}) collective-permute-start(bf16[8,128]{1,0:T(8,128)(2,1)S(1)} %slice_bitcast_fusion), channel_id=1, source_target_pairs={{1,33},{33,65},{65,97},{97,1},{3,35},{35,67},{67,99},{99,3},{5,37}... | collective-permute-start | bytes 6152 | tf_op jit(solution)/shard_map/cond/branch_0_fun/ppermute | solution.py:319
  24.4 10.6 %all-to-all-done.3.after.tiles = bf16[16,4,8,256]{3,2,1,0:T(8,128)(2,1)S(1)} async-done(((bf16[16,4,8,256]{3,2,1,0:T(8,128)(2,1)}), bf16[16,4,8,256]{3,2,1,0:T(8,128)(2,1)S(1)}, u32[]{:S(2)}, u32[]{:S(2)}) %all-to-all-start.3) | async-done | bytes 262176 | tf_op jit(solution)/shard_map/cond/branch_0_fun/all_to_all | solution.py:276
  35.0 2.1 %branch_0_fun.7.local = f32[64,2048]{1,0:T(8,128)S(1)} custom-call(s32[33]{0:T(128)} %get-tuple-element.33.offsets, s32[2,32]{1,0:T(2,128)} %get-tuple-element.35.orbitals, f32[16]{0:T(128)} %get-tuple-element.40.energy, bf16[2,16,8,1024]{3,2,1,0:T(8,128)(2,1)S(1)} %get-tuple-element.36.own, bf16[1024,1024]{1,0:T(8,128)(2,1)} %get-tuple-element.41.fock, ...), custom_call_target="tpu_custom_call" | custom-call | tf_op jit(solution)/shard_map/cond/branch_0_fun/pallas_call | solution.py:256
  37.0 0.0 collective-permute-done.token
  37.0 0.0 copy-done.6
  37.0 0.0 copy-start.1
  37.1 0.0 copy-start.10
  37.1 0.9 branch_0_fun.8
  38.0 25.6 %all_to_all.33.arrived = bf16[16,18,8,256]{3,2,1,0:T(8,128)(2,1)S(1)} all-to-all(bf16[16,18,8,256]{3,2,1,0:T(8,128)(2,1)S(1)} %branch_0_fun.8), channel_id=1, replica_groups={{32,34,36,38,40,42,44,46,16,18,20,22,24,26,28,30},{64,66,68,70,72,74,76..., dimensions={0} | all-to-all | bytes 2359296 | tf_op jit(solution)/shard_map/cond/branch_0_fun/all_to_all | solution.py:276
  63.6 0.0 copy-done.1
  63.6 0.0 copy-done.10
  63.6 2.5 %branch_0_fun.9 = bf16[4,256,1024]{2,1,0:T(8,128)(2,1)S(1)} custom-call(s32[33]{0:T(128)S(1)} %copy-done.6, s32[32]{0:T(128)S(1)} %copy-done.10, bf16[16,18,8,256]{3,2,1,0:T(8,128)(2,1)S(1)} %all_to_all.33.arrived, bf16[1024,1024]{1,0:T(8,128)(2,1)S(1)} %copy-done.1), custom_call_target="tpu_custom_call" | custom-call | tf_op jit(solution)/shard_map/cond/branch_0_fun/pallas_call | solution.py:256
  66.1 19.3 %all_to_all.34.parts = bf16[4,256,1024]{2,1,0:T(8,128)(2,1)S(1)} all-to-all(bf16[4,256,1024]{2,1,0:T(8,128)(2,1)S(1)} %branch_0_fun.9), channel_id=1, replica_groups=mesh['x'=4,'zh'=4,'zl'=4,'y'=4,'core'=2] {'x'}, dimensions={0} | all-to-all | bytes 4194304 | tf_op jit(solution)/shard_map/cond/branch_0_fun/all_to_all | solution.py:329
  85.4 0.3 branch_0_fun.10
  85.7 25.0 %all_to_all.35 = bf16[16,64,256]{2,1,0:T(8,128)(2,1)S(1)} all-to-all(bf16[16,64,256]{2,1,0:T(8,128)(2,1)S(1)} %branch_0_fun.10), channel_id=1, replica_groups=mesh['x'=4,'zh'=4,'zl'=4,'y'=4,'core'=2] {'zh','y'}, dimensions={0} | all-to-all | bytes 1048576 | tf_op jit(solution)/shard_map/cond/branch_0_fun/all_to_all | solution.py:331
  110.7 0.6 branch_0_fun.11
  111.3 20.1 %all_to_all.39.arrived = bf16[16,64,256]{2,1,0:T(8,128)(2,1)S(1)} all-to-all(bf16[16,64,256]{2,1,0:T(8,128)(2,1)S(1)} %get-tuple-element.53), channel_id=1, replica_groups=mesh['x'=4,'zh'=4,'zl'=4,'y'=4,'core'=2] {'zl','y'}, dimensions={0} | all-to-all | bytes 1048576 | tf_op jit(solution)/shard_map/all_to_all | solution.py:345
  131.4 0.7 shard_map.74
  132.1 1.9 %collective-permute-start.2 = (bf16[64,1024]{1,0:T(8,128)(2,1)S(1)}, bf16[64,1024]{1,0:T(8,128)(2,1)S(1)}, u32[]{:S(2)}, u32[]{:S(2)}) collective-permute-start(bf16[64,1024]{1,0:T(8,128)(2,1)S(1)} %get-tuple-element.56), channel_id=1, source_target_pairs={{0,1},{1,0},{2,3},{3,2},{4,5},{5,4},{6,7},{7,6},{8,9},{9,8},{10,11... | collective-permute-start | bytes 393224 | tf_op jit(solution)/shard_map/ppermute | solution.py:347
  134.1 0.0 copy-done.5
  134.1 0.7 shard_map.75.base
  134.8 0.6 collective-permute-done.2.other
  135.4 1.4 %shard_map.76 = f32[64,2,1024]{2,1,0:T(2,128)} custom-call(s32[33]{0:T(128)S(1)} %copy-done.5, f32[64,2,1024]{2,1,0:T(2,128)S(1)} %shard_map.75.base, bf16[64,1024]{1,0:T(8,128)(2,1)S(1)} %collective-permute-done.2.other), custom_call_target="tpu_custom_call" | custom-call | tf_op jit(solution)/shard_map/pallas_call | solution.py:256
  (3 shorter events, 0.0 us)
Async XLA Ops:
  1.0 1.0 copy-start
  2.0 10.3 %collective-permute-start.1 = (bf16[2,16,8,1024]{3,2,1,0:T(8,128)(2,1)S(1)}, bf16[2,16,8,1024]{3,2,1,0:T(8,128)(2,1)S(1)}, u32[]{:S(2)}, u32[]{:S(2)}) collective-permute-start(bf16[2,16,8,1024]{3,2,1,0:T(8,128)(2,1)S(1)} %shard_map.73), channel_id=1, source_target_pairs={{0,1},{1,0},{2,3},{3,2},{4,5},{5,4},{6,7},{7,6},{8,9},{9,8},{10,11... | collective-permute-start | bytes 1572872 | tf_op jit(solution)/shard_map/ppermute | solution.py:340
  12.3 121.8 %copy-start.5 = (s32[33]{0:T(128)S(1)}, s32[33]{0:T(128)}, u32[]{:S(2)}) copy-start(s32[33]{0:T(128)} %offsets.5) | copy-start | bytes 400
  14.0 23.0 %copy-start.6 = (s32[33]{0:T(128)S(1)}, s32[33]{0:T(128)}, u32[]{:S(2)}) copy-start(s32[33]{0:T(128)} %get-tuple-element.33.offsets) | copy-start | bytes 400 | tf_op jit(solution)/shard_map/cond
  14.0 20.9 %all-to-all-start.3 = ((bf16[16,4,8,256]{3,2,1,0:T(8,128)(2,1)}), bf16[16,4,8,256]{3,2,1,0:T(8,128)(2,1)S(1)}, u32[]{:S(2)}, u32[]{:S(2)}) async-start(bf16[16,4,8,256]{3,2,1,0:T(8,128)(2,1)} %get-tuple-element.39), calls=%async_computation.3 | async-start | bytes 524288 | tf_op jit(solution)/shard_map/cond/branch_0_fun/all_to_all | solution.py:276
  22.5 14.6 %collective-permute-start = (bf16[8,128]{1,0:T(8,128)(2,1)S(1)}, bf16[8,128]{1,0:T(8,128)(2,1)S(1)}, u32[]{:S(2)}, u32[]{:S(2)}) collective-permute-start(bf16[8,128]{1,0:T(8,128)(2,1)S(1)} %slice_bitcast_fusion), channel_id=1, source_target_pairs={{1,33},{33,65},{65,97},{97,1},{3,35},{35,67},{67,99},{99,3},{5,37}... | collective-permute-start | bytes 6152 | tf_op jit(solution)/shard_map/cond/branch_0_fun/ppermute | solution.py:319
  37.0 26.6 %copy-start.1 = (bf16[1024,1024]{1,0:T(8,128)(2,1)S(1)}, bf16[1024,1024]{1,0:T(8,128)(2,1)}, u32[]{:S(2)}) copy-start(bf16[1024,1024]{1,0:T(8,128)(2,1)} %get-tuple-element.41.fock) | copy-start | bytes 6291460 | tf_op jit(solution)/shard_map/cond
  37.1 26.6 %copy-start.10 = (s32[32]{0:T(128)S(1)}, s32[32]{0:T(128)}, u32[]{:S(2)}) copy-start(s32[32]{0:T(128)} %get-tuple-element.34.case) | copy-start | bytes 388 | tf_op jit(solution)/shard_map/cond
  132.1 3.2 %collective-permute-start.2 = (bf16[64,1024]{1,0:T(8,128)(2,1)S(1)}, bf16[64,1024]{1,0:T(8,128)(2,1)S(1)}, u32[]{:S(2)}, u32[]{:S(2)}) collective-permute-start(bf16[64,1024]{1,0:T(8,128)(2,1)S(1)} %get-tuple-element.56), channel_id=1, source_target_pairs={{0,1},{1,0},{2,3},{3,2},{4,5},{5,4},{6,7},{7,6},{8,9},{9,8},{10,11... | collective-permute-start | bytes 393224 | tf_op jit(solution)/shard_map/ppermute | solution.py:347
